TPU v7x, 32 devices: a whole 2x2x4 slice. The times are simulated.
32 devices in a mesh: row: 8 (over y, x, core), seg: 4 (over z).
Axes of the slice: x: 2, y: 2, z: 4, core: 2. Of those that a mesh axis runs over, the one named last changes fastest.
Arguments:
- tokens: bfloat16 [64, 1024, 768], P('row', 'seg'), may hold values from -6 to 6
- doc_ids: int32 [64, 8], P('row'), may hold values from 0 to 7, as said below
- w_qkv: bfloat16 [2, 768, 2304], replicated, may hold values from -0.21875 to 0.21875
- w_out: bfloat16 [2, 768, 768], replicated, may hold values from -0.875 to 0.875
- w_up: bfloat16 [2, 768, 3072], replicated, may hold values from -0.21875 to 0.21875
- w_down: bfloat16 [2, 3072, 768], replicated, may hold values from -0.109375 to 0.109375
- biases: bfloat16 [2, 6, 768], replicated, may hold values from -1 to 1
- gains: bfloat16 [2, 2, 768], replicated, may hold values from 0.5 to 1.5
- b_up: bfloat16 [2, 3072], replicated, may hold values from -1 to 1
- pos_table: bfloat16 [8, 768], replicated, may hold values from -3 to 3
- cotangent: bfloat16 [64, 1024, 768], P('row', 'seg'), may hold values from -6 to 6
Outputs:
- output: bfloat16 [64, 1024, 768], P('row', 'seg')
- grad_tokens: float32 [64, 1024, 768], P('row', 'seg')
- grad_w_qkv: float32 [1536, 2304], P(('row', 'seg'))
- grad_w_out: float32 [1536, 768], P(('row', 'seg'))
- grad_w_up: float32 [1536, 3072], P(('row', 'seg'))
- grad_w_down: float32 [6144, 768], P(('row', 'seg'))
- grad_biases: float32 [9216], P(('row', 'seg'))
- grad_gains: float32 [3072], P(('row', 'seg'))
- grad_b_up: float32 [6144], P(('row', 'seg'))
- grad_pos_table: float32 [6144], P(('row', 'seg'))
Inputs may be any that keep to these rules, and one draw needn't show every extreme that they name: `doc_ids`: in each row the ids start at 0 and rise by 0 or 1 from one segment to the next; among rows 8 * g to 8 * g + 7 at least one row is a single document; where 8 is 2 or more, some row among the first 8 rows has every segment in a document of its own.
All inputs are finite; a program needn't handle non-finite values.
Results may differ from a plain program's by a relative error of at most 0.02.
Values may be sent and summed in bfloat16 or wider, within the bound.
A program may use at most 256 MiB of HBM per device.

v0:
```python
import jax
import jax.numpy as jnp
from jax import lax
from jax.sharding import PartitionSpec as P

HDIM = 64
SEGLEN = 128


NEGATIVE = -1000000000.0
EPSILON = 1e-05


def normalize(values):
    centered = values - jnp.mean(values, axis=-1, keepdims=True)
    variance = jnp.mean(centered * centered, axis=-1, keepdims=True)
    return centered * lax.rsqrt(variance + EPSILON)


def project(values, matrix):
    return jnp.einsum("...i,ij->...j", values, matrix, preferred_element_type=jnp.float32)


def project_back(values, matrix):
    return jnp.einsum("...j,ij->...i", values, matrix, preferred_element_type=jnp.float32)


def outer_total(values, grad_out):
    return jnp.einsum(
        "ni,nj->ij",
        values.reshape(-1, values.shape[-1]),
        grad_out.reshape(-1, grad_out.shape[-1]),
        preferred_element_type=jnp.float32,
    )


def row_total(values):
    return jnp.sum(values.astype(jnp.float32).reshape(-1, values.shape[-1]), axis=0)


def split_heads(values):
    return values.reshape(values.shape[:-1] + (values.shape[-1] // HDIM, HDIM))


def merge_heads(values):
    return values.reshape(values.shape[:-2] + (values.shape[-2] * values.shape[-1],))


def keep_all(values):
    return values


def scores_of(query, keys, allowed):
    scores = jnp.einsum(
        "bqhd,bkhd->bhqk", query, keys, preferred_element_type=jnp.float32
    ) * query.shape[-1] ** (-0.5)
    if allowed is None:
        return scores
    return jnp.where(allowed[:, None], scores, NEGATIVE)


def attend(query, keys, values, allowed):
    scores = scores_of(query, keys, allowed)
    peak = jnp.max(scores, axis=-1, keepdims=True)
    logsum = peak + jnp.log(jnp.sum(jnp.exp(scores - peak), axis=-1, keepdims=True))
    probs_low = jnp.exp(scores - logsum).astype(jnp.bfloat16)
    mixed = jnp.einsum("bhqk,bkhd->bqhd", probs_low, values, preferred_element_type=jnp.float32)
    return (mixed.astype(jnp.bfloat16), logsum)


def attend_back(query, keys, values, allowed, logsum, grad_mixed):
    scores = scores_of(query, keys, allowed)
    attn_probs = jnp.exp(scores - logsum)
    probs_low = attn_probs.astype(jnp.bfloat16)
    grad_values = jnp.einsum(
        "bhqk,bqhd->bkhd", probs_low, grad_mixed, preferred_element_type=jnp.float32
    )
    grad_probs = jnp.einsum(
        "bqhd,bkhd->bhqk", grad_mixed, values, preferred_element_type=jnp.float32
    )
    inner_sum = jnp.sum(grad_probs * attn_probs, axis=-1, keepdims=True)
    grad_scores = (attn_probs * (grad_probs - inner_sum)).astype(jnp.bfloat16)
    scale = query.shape[-1] ** (-0.5)
    grad_query = (
        jnp.einsum("bhqk,bkhd->bqhd", grad_scores, keys, preferred_element_type=jnp.float32) * scale
    )
    grad_keys = (
        jnp.einsum("bhqk,bqhd->bkhd", grad_scores, query, preferred_element_type=jnp.float32)
        * scale
    )
    return (grad_query, grad_keys, grad_values)


def unpack(proj_qkv):
    model_width = proj_qkv.shape[-1] // 3
    return (
        split_heads(proj_qkv[..., :model_width]),
        split_heads(proj_qkv[..., model_width : 2 * model_width]),
        split_heads(proj_qkv[..., 2 * model_width :]),
    )


def local_attend(proj_qkv, allowed):
    query, keys, values = unpack(proj_qkv)
    mixed, logsum = attend(query, keys, values, allowed)
    return (merge_heads(mixed), logsum)


def local_attend_back(proj_qkv, allowed, logsum, grad_mixed):
    query, keys, values = unpack(proj_qkv)
    grad_query, grad_keys, grad_values = attend_back(
        query, keys, values, allowed, logsum, split_heads(grad_mixed)
    )
    return jnp.concatenate(
        [merge_heads(grad_query), merge_heads(grad_keys), merge_heads(grad_values)], axis=-1
    )


def cross_attend(proj_qkv, allowed):
    model_width = proj_qkv.shape[-1] // 3
    key_values = lax.all_gather(proj_qkv[..., model_width:], "seg", axis=1, tiled=True)
    query = split_heads(proj_qkv[..., :model_width])
    mixed, logsum = attend(
        query,
        split_heads(key_values[..., :model_width]),
        split_heads(key_values[..., model_width:]),
        allowed,
    )
    return (merge_heads(mixed), (logsum, key_values))


def cross_attend_back(proj_qkv, allowed, kept, grad_mixed):
    logsum, key_values = kept
    model_width = proj_qkv.shape[-1] // 3
    query = split_heads(proj_qkv[..., :model_width])
    grad_query, grad_keys, grad_values = attend_back(
        query,
        split_heads(key_values[..., :model_width]),
        split_heads(key_values[..., model_width:]),
        allowed,
        logsum,
        split_heads(grad_mixed),
    )
    key_terms = jnp.concatenate([merge_heads(grad_keys), merge_heads(grad_values)], axis=-1)
    key_grads = lax.psum_scatter(
        key_terms.astype(jnp.bfloat16), "seg", scatter_dimension=1, tiled=True
    ).astype(jnp.float32)
    return jnp.concatenate([merge_heads(grad_query), key_grads], axis=-1)


def block_forward(rows, index, weights, attend_fn, allowed):
    w_qkv, w_out, w_up, w_down, biases, gains, b_up = weights
    bias = biases[index].astype(jnp.float32)
    gain = gains[index].astype(jnp.float32)
    qkv_bias = jnp.concatenate([bias[0], jnp.zeros_like(bias[0]), bias[1]])
    proj_qkv = (project(rows, w_qkv[index]) + qkv_bias).astype(jnp.bfloat16)
    mixed, kept = attend_fn(proj_qkv, allowed)
    resid_one = rows.astype(jnp.float32) + (project(mixed, w_out[index]) + bias[2])
    first = (normalize(resid_one) * gain[0] + bias[3]).astype(jnp.bfloat16)
    inner = project(first, w_up[index]) + b_up[index].astype(jnp.float32)
    hidden = jax.nn.gelu(inner).astype(jnp.bfloat16)
    resid_two = first.astype(jnp.float32) + (project(hidden, w_down[index]) + bias[4])
    result = (normalize(resid_two) * gain[1] + bias[5]).astype(jnp.bfloat16)
    return (result, (rows, proj_qkv, kept, mixed, resid_one, first, inner, hidden, resid_two))


def norm_back(resid, gain, grad_out, own_rows):
    normal, pullback = jax.vjp(normalize, resid)
    (grad_resid,) = pullback(grad_out * gain)
    return (grad_resid, row_total(own_rows(grad_out * normal)), row_total(own_rows(grad_out)))


def block_backward(grad_result, cache, index, weights, back_fn, allowed, own_rows):
    w_qkv, w_out, w_up, w_down, biases, gains, b_up = weights
    rows, proj_qkv, kept, mixed, resid_one, first, inner, hidden, resid_two = cache
    gain = gains[index].astype(jnp.float32)
    grad_two, gain_two, shift_two = norm_back(resid_two, gain[1], grad_result, own_rows)
    grad_second = grad_two.astype(jnp.bfloat16)
    grad_w_down = outer_total(own_rows(hidden), own_rows(grad_second))
    bias_down = row_total(own_rows(grad_second))
    _, gelu_pull = jax.vjp(jax.nn.gelu, inner)
    (grad_inner,) = gelu_pull(project_back(grad_second, w_down[index]))
    grad_inner = grad_inner.astype(jnp.bfloat16)
    grad_w_up = outer_total(own_rows(first), own_rows(grad_inner))
    grad_b_up = row_total(own_rows(grad_inner))
    grad_first = grad_two + project_back(grad_inner, w_up[index])
    grad_one, gain_one, shift_one = norm_back(resid_one, gain[0], grad_first, own_rows)
    grad_branch = grad_one.astype(jnp.bfloat16)
    grad_w_out = outer_total(own_rows(mixed), own_rows(grad_branch))
    bias_out = row_total(own_rows(grad_branch))
    grad_mixed = project_back(grad_branch, w_out[index]).astype(jnp.bfloat16)
    grad_qkv = back_fn(proj_qkv, allowed, kept, grad_mixed).astype(jnp.bfloat16)
    grad_w_qkv = outer_total(own_rows(rows), own_rows(grad_qkv))
    qkv_total = row_total(own_rows(grad_qkv))
    model_width = rows.shape[-1]
    grad_rows = grad_one + project_back(grad_qkv, w_qkv[index])
    grad_biases = jnp.stack(
        [
            qkv_total[:model_width],
            qkv_total[2 * model_width :],
            bias_out,
            shift_one,
            bias_down,
            shift_two,
        ]
    )
    grad_gains = jnp.stack([gain_one, gain_two])
    return (
        grad_rows,
        (grad_w_qkv, grad_w_out, grad_w_up, grad_w_down, grad_biases, grad_gains, grad_b_up),
    )


def per_device(
    tokens, doc_ids, w_qkv, w_out, w_up, w_down, biases, gains, b_up, pos_table, cotangent
):
    weights = (w_qkv, w_out, w_up, w_down, biases, gains, b_up)
    row_count, local_length, model_width = tokens.shape
    seg_here = local_length // SEGLEN
    segments = doc_ids.shape[1]
    first_seg = lax.axis_index("seg") * seg_here

    def own_rows(values):
        return lax.dynamic_slice_in_dim(values, first_seg, seg_here, 1)

    seg_input = tokens.reshape(row_count * seg_here, SEGLEN, model_width)
    seg_out, seg_cache = block_forward(seg_input, 0, weights, local_attend, None)
    seg_blocks = seg_out.reshape(row_count, seg_here, SEGLEN, model_width)
    seg_cls = seg_blocks[:, :, 0]
    cot_blocks = cotangent.reshape(row_count, seg_here, SEGLEN, model_width)
    seg_place = jnp.arange(segments)
    same_doc = doc_ids[:, :, None] == doc_ids[:, None, :]
    doc_start = jnp.min(jnp.where(same_doc, seg_place[None, None, :], segments), axis=2)
    position = seg_place[None, :] - doc_start
    onehot_all = (position[:, :, None] == seg_place[None, None, :]).astype(jnp.bfloat16)
    embed_all = jnp.einsum("rsp,pd->rsd", onehot_all, pos_table, preferred_element_type=jnp.float32)
    allowed = own_rows(same_doc)
    cls_in = (seg_cls.astype(jnp.float32) + own_rows(embed_all)).astype(jnp.bfloat16)
    cls_out, cls_cache = block_forward(cls_in, 1, weights, cross_attend, allowed)
    grad_cls, cross_grads = block_backward(
        cot_blocks[:, :, 0].astype(jnp.float32),
        cls_cache,
        1,
        weights,
        cross_attend_back,
        allowed,
        keep_all,
    )
    output = seg_blocks.at[:, :, 0].set(cls_out).reshape(row_count, local_length, model_width)
    grad_seg = (
        cot_blocks.astype(jnp.float32)
        .at[:, :, 0]
        .set(grad_cls)
        .reshape(row_count * seg_here, SEGLEN, model_width)
    )
    grad_rows, seg_grads = block_backward(
        grad_seg, seg_cache, 0, weights, local_attend_back, None, keep_all
    )
    onehot_own = own_rows(onehot_all).astype(jnp.float32)
    grad_pos = jnp.einsum("rsp,rsd->pd", onehot_own, grad_cls, precision=lax.Precision.HIGHEST)
    joined = [
        jnp.stack([seg_part, cross_part]) for seg_part, cross_part in zip(seg_grads, cross_grads)
    ]
    stacked = (
        joined[0].reshape(-1, joined[0].shape[-1]),
        joined[1].reshape(-1, joined[1].shape[-1]),
        joined[2].reshape(-1, joined[2].shape[-1]),
        joined[3].reshape(-1, joined[3].shape[-1]),
        joined[4].reshape(-1),
        joined[5].reshape(-1),
        joined[6].reshape(-1),
        grad_pos.reshape(-1),
    )
    shards = (
        lax.psum_scatter(stacked[0], ("row", "seg"), scatter_dimension=0, tiled=True),
        lax.psum_scatter(stacked[1], ("row", "seg"), scatter_dimension=0, tiled=True),
        lax.psum_scatter(stacked[2], ("row", "seg"), scatter_dimension=0, tiled=True),
        lax.psum_scatter(stacked[3], ("row", "seg"), scatter_dimension=0, tiled=True),
        lax.psum_scatter(stacked[4], ("row", "seg"), scatter_dimension=0, tiled=True),
        lax.psum_scatter(stacked[5], ("row", "seg"), scatter_dimension=0, tiled=True),
        lax.psum_scatter(stacked[6], ("row", "seg"), scatter_dimension=0, tiled=True),
        lax.psum_scatter(stacked[7], ("row", "seg"), scatter_dimension=0, tiled=True),
    )
    grad_tokens = grad_rows.reshape(row_count, local_length, model_width)
    return (output, grad_tokens) + tuple(shards)


def solution(mesh):
    return jax.shard_map(
        per_device,
        mesh=mesh,
        in_specs=(
            P("row", "seg", None),
            P("row", None),
            P(),
            P(),
            P(),
            P(),
            P(),
            P(),
            P(),
            P(),
            P("row", "seg", None),
        ),
        out_specs=(
            P("row", "seg", None),
            P("row", "seg", None),
            P(("row", "seg"), None),
            P(("row", "seg"), None),
            P(("row", "seg"), None),
            P(("row", "seg"), None),
            P(("row", "seg")),
            P(("row", "seg")),
            P(("row", "seg")),
            P(("row", "seg")),
        ),
        check_vma=False,
    )
```

profile of v0, /device:TPU:0, one launch (start us, length us, event | category | flops | bytes accessed | tf_op | source)
XLA Modules:
  0.0 1169.1 jit_solution(10155862220870118058)
XLA Ops:
  12.8 10.2 add_convert_fusion
  23.0 3.8 fusion.158
  26.8 3.5 copy.216
  30.3 5.4 copy.215
  35.8 4.9 copy.214
  40.7 4.2 multiply_reduce_fusion.1
  44.9 3.9 exponential_reduce_fusion
  49.4 4.1 convolution_convert_fusion.2
  53.5 5.1 fusion.162
  62.2 21.3 %multiply_convert_fusion = (bf16[16,128,3072]{2,1,0:T(8,128)(2,1)}, f32[16,128,3072]{2,1,0:T(8,128)}) fusion(f32[3072]{0:T(1024)S(1)} %bitcast.339, bf16[16,128,768]{2,1,0:T(8,128)(2,1)S(1)} %add_convert_fusion.2, bf16[2,768,3072]{2,1,0:T(8,128)(2,1)} %param.19), kind=kOutput, calls=%fused_computation.10 | convolution fusion | flops 9726590976 | bytes 45625344 | tf_op jit(solution)/shard_map/...i,ij->...j/dot_general | solution.py:21
  83.5 14.8 %fusion.163 = (f32[16,128]{1,0:T(8,128)S(1)}, f32[16,128,768]{2,1,0:T(8,128)S(1)}) fusion(f32[768]{0:T(1024)S(1)} %get-tuple-element.130, bf16[16,128,3072]{2,1,0:T(8,128)(2,1)} %get-tuple-element.108, bf16[2,3072,768]{2,1,0:T(8,128)(2,1)} %param.20, bf16[16,128,768]{2,1,0:T(8,128)(2,1)S(1)} %add_convert_fusion.2), kind=kOutput, calls=%fused_computation.263 | convolution fusion | flops 9669965824 | bytes 26749952 | tf_op jit(solution)/shard_map/...i,ij->...j/dot_general | solution.py:21
  100.9 1.7 copy-done.18
  102.9 2.6 fusion.51
  107.8 15.6 %all_gather.3 = bf16[8,8,1536]{2,0,1:T(8,128)(2,1)S(1)} all-gather(bf16[8,2,1536]{2,0,1:T(8,128)(2,1)S(1)} %slice.272), channel_id=1, replica_groups=mesh['row'=8,'seg'=4] {'seg'}, dimensions={1}, use_global_device_ids=true | all-gather | bytes 245760 | tf_op jit(solution)/shard_map/all_gather | solution.py:121
  128.4 1.6 fusion.165
  131.0 3.2 fusion.48
  134.3 3.3 fusion.166
  139.8 4.3 convert_reduce_fusion.4
  144.1 2.0 multiply_reduce_fusion.8
  147.6 2.5 multiply_reduce_fusion.7
  160.8 5.2 convert_element_type.210
  167.5 4.2 copy.252
  174.3 2.1 convolution_bitcast_fusion.6
  176.3 2.4 reduce-scatter.6.cloned.1.call-done
  179.6 3.1 fusion.91
  182.7 2.4 scatter.9
  185.1 3.4 reduce_sum.357
  188.5 5.8 fusion.14
  194.3 4.0 fusion.156
  198.3 2.7 copy-done.11
  201.6 31.5 %convert_reduce_fusion = (f32[3072]{0:T(1024)S(1)}, bf16[16,128,3072]{2,1,0:T(8,128)(2,1)}) fusion(f32[16,128,3072]{2,1,0:T(8,128)} %get-tuple-element.109, f32[3072]{0:T(1024)S(1)} %bitcast.340, bf16[16,128,768]{2,1,0:T(8,128)(2,1)S(1)} %get-tuple-element.69, bf16[2,3072,768]{2,1,0:T(8,128)(2,1)} %param.20), kind=kOutput, calls=%fused_computation.9 | convolution fusion | flops 9808376832 | bytes 45637632 | tf_op jit(solution)/shard_map/...j,ij->...i/dot_general | solution.py:25
  233.2 18.7 %multiply_reduce_fusion.2 = (f32[768]{0:T(1024)S(1)}, f32[16,128]{1,0:T(8,128)S(1)}, f32[768]{0:T(1024)S(1)}, f32[16,128,768]{2,1,0:T(8,128)}) fusion(f32[16,128,768]{2,1,0:T(8,128)S(1)} %bitcast.298, f32[16,128]{1,0:T(8,128)S(1)} %copy-done.53, f32[16,128]{1,0:T(8,128)S(1)} %copy-done.41, f32[768]{0:T(1024)S(1)} %copy-done.61, ...), kind=kOutput, calls=%fused_computation.33 | convolution fusion | flops 9679400960 | bytes 36217856 | tf_op jit(solution)/shard_map/...j,ij->...i/dot_general | solution.py:25
  251.9 4.1 fusion.155
  256.7 3.2 copy-done.10
  260.0 4.0 convolution_convert_fusion.1
  264.0 3.5 copy.242
  267.5 10.8 convolution_convert_fusion
  278.3 9.1 multiply_reduce_fusion
  287.4 10.3 multiply_convert_fusion.1
  297.8 5.7 multiply_convert_fusion.2
  303.5 2.4 multiply_convert_fusion.3
  308.2 4.5 copy.251
  312.7 2.4 copy.250
  315.1 2.4 copy.249
  320.2 3.6 copy-done.12
  326.1 6.9 fusion.65
  333.0 4.8 pad_maximum_fusion.3
  337.9 3.9 convolution_bitcast_fusion.1
  341.9 13.0 %convolution_bitcast_fusion.2 = f32[1,768,2304]{2,1,0:T(8,128)} fusion(bf16[2048,2304]{0,1:T(8,128)(2,1)} %copy-done.12, bf16[2048,768]{1,0:T(8,128)(2,1)S(1)} %bitcast.333), kind=kOutput, calls=%fused_computation.52 | convolution fusion | flops 7247757312 | bytes 19660800 | tf_op jit(solution)/shard_map/ni,nj->ij/dot_general | solution.py:29
  354.9 11.1 pad_maximum_fusion.2
  368.8 13.0 %convolution_bitcast_fusion = f32[1,3072,768]{2,1,0:T(8,128)S(1)} fusion(bf16[16,128,3072]{2,1,0:T(8,128)(2,1)} %get-tuple-element.108, bf16[16,128,768]{2,1,0:T(8,128)(2,1)S(1)} %copy-done.20), kind=kOutput, calls=%fused_computation.50 | convolution fusion | flops 9663676416 | bytes 25165824 | tf_op jit(solution)/shard_map/ni,nj->ij/dot_general | solution.py:29
  381.8 6.6 pad_maximum_fusion.1
  391.2 12.6 %convolution_bitcast_fusion.5 = f32[1,768,3072]{2,1,0:T(8,128)S(1)} fusion(bf16[16,128,768]{2,1,0:T(8,128)(2,1)S(1)} %copy-done.24, bf16[16,128,3072]{2,1,0:T(8,128)(2,1)} %get-tuple-element.67), kind=kOutput, calls=%fused_computation.55 | convolution fusion | flops 9663676416 | bytes 25165824 | tf_op jit(solution)/shard_map/ni,nj->ij/dot_general | solution.py:29
  403.9 6.7 pad_maximum_fusion
  411.4 1.9 scatter.6
  413.3 4.7 copy.248
  418.0 4.6 copy.247
  422.7 2.8 copy.246
  425.5 13.8 %add_add_fusion.4 = f32[16,128,768]{2,1,0:T(8,128)} fusion(f32[16,128,768]{2,1,0:T(8,128)} %copy-done.10, f32[16,128]{1,0:T(8,128)S(1)} %copy-done.63, bf16[2,768,2304]{2,1,0:T(8,128)(2,1)} %param.17, bf16[16,128,768]{2,1,0:T(8,128)(2,1)} %copy.248, bf16[16,128,768]{2,1,0:T(8,128)(2,1)} %copy.247, bf16[16,128,768]{2,1,0:T(8,128)(2,1)} %copy.246), kind=kOutput, calls=%fused_computation.46 | convolution fusion | flops 7279214592 | bytes 25567232 | tf_op jit(solution)/shard_map/...j,ij->...i/dot_general | solution.py:25
  439.2 14.8 %all-reduce.7.cloned.1.call-done = (f32[9216]{0:T(1024)}, f32[3072]{0:T(1024)}, f32[6144]{0:T(1024)}, f32[6144]{0:T(1024)}) async-done(((f32[9216]{0:T(1024)}, f32[3072]{0:T(1024)}, f32[6144]{0:T(1024)}, f32[6144]{0:T(1024)}), (f32[9216]{0:T(1024)}, f32[3072]{0:T(1024)}, f32[6144]{0:T(1024)}, f32[6144]{0:T(1024)})) %all-reduce.7.cloned.1.call-update) | async-done | bytes 98320
  459.3 109.6 %reduce-scatter.10.cloned.1.call-done = f32[48,768]{1,0:T(8,128)} async-done(((f32[1536,768]{1,0:T(8,128)}), f32[48,768]{1,0:T(8,128)}) %reduce-scatter.10.cloned.1.call-update) | async-done | bytes 147472 | tf_op jit(solution)/shard_map/reduce_scatter | solution.py:276
  568.9 168.4 %reduce-scatter.8.cloned.1.call-done = f32[48,2304]{1,0:T(8,128)} async-done(((f32[1536,2304]{1,0:T(8,128)}), f32[48,2304]{1,0:T(8,128)}) %reduce-scatter.8.cloned.1.call-update) | async-done | bytes 442384 | tf_op jit(solution)/shard_map/reduce_scatter | solution.py:275
  737.3 212.2 %reduce-scatter.14.cloned.1.call-done = f32[192,768]{1,0:T(8,128)} async-done(((f32[6144,768]{1,0:T(8,128)}), f32[192,768]{1,0:T(8,128)}) %reduce-scatter.14.cloned.1.call-update) | async-done | bytes 589840 | tf_op jit(solution)/shard_map/reduce_scatter | solution.py:278
  949.5 212.5 %reduce-scatter.12.cloned.1.call-done = f32[48,3072]{1,0:T(8,128)} async-done(((f32[1536,3072]{1,0:T(8,128)}), f32[48,3072]{1,0:T(8,128)}) %reduce-scatter.12.cloned.1.call-update) | async-done | bytes 589840 | tf_op jit(solution)/shard_map/reduce_scatter | solution.py:277
  (306 shorter events, 60.0 us)
Async XLA Ops:
  7.2 95.5 %copy-start = (bf16[8,768]{1,0:T(8,128)(2,1)S(1)}, bf16[8,768]{1,0:T(8,128)(2,1)}, u32[]{:S(2)}) copy-start(bf16[8,768]{1,0:T(8,128)(2,1)} %param.24) | copy-start | bytes 36868
  7.2 171.6 %reduce-scatter.6.cloned.1.call-start = ((), (), s32[]{:S(2)}) async-start(), calls=%async_computation.5 | async-start | bytes 245760 | tf_op jit(solution)/shard_map/reduce_scatter | solution.py:145
  9.2 93.4 %copy-start.58 = (s32[8,8]{0,1:T(8,128)}, s32[8,8]{0,1:T(8,128)S(1)}, u32[]{:S(2)}) copy-start(s32[8,8]{0,1:T(8,128)S(1)} %copy.220) | copy-start | bytes 772
  11.3 50.8 %copy-start.67 = (f32[1,3072]{1,0:T(1,128)}, f32[1,3072]{1,0:T(1,128)S(1)}, u32[]{:S(2)}) copy-start(f32[1,3072]{1,0:T(1,128)S(1)} %get-tuple-element.97) | copy-start | bytes 36868
  30.3 10.4 copy-start.5
  44.9 4.5 copy-start.2
  48.8 4.7 copy-start.16
  49.4 4.1 copy-start.13
  59.5 24.0 %copy-start.48 = (f32[16,128]{1,0:T(8,128)}, f32[16,128]{1,0:T(8,128)S(1)}, u32[]{:S(2)}) copy-start(f32[16,128]{1,0:T(8,128)S(1)} %multiply_reduce_fusion.6) | copy-start | bytes 24580
  59.5 24.0 %copy-start.52 = (f32[16,128]{1,0:T(8,128)}, f32[16,128]{1,0:T(8,128)S(1)}, u32[]{:S(2)}) copy-start(f32[16,128]{1,0:T(8,128)S(1)} %fusion.145) | copy-start | bytes 24580
  60.6 22.9 %copy-start.60 = (f32[768]{0:T(1024)}, f32[768]{0:T(1024)S(1)}, u32[]{:S(2)}) copy-start(f32[768]{0:T(1024)S(1)} %get-tuple-element.132) | copy-start | bytes 9220
  60.6 38.6 %copy-start.54 = (f32[768]{0:T(1024)}, f32[768]{0:T(1024)S(1)}, u32[]{:S(2)}) copy-start(f32[768]{0:T(1024)S(1)} %get-tuple-element.133) | copy-start | bytes 9220
  62.1 21.4 %copy-start.23 = (bf16[16,128,768]{2,1,0:T(8,128)(2,1)}, bf16[16,128,768]{2,1,0:T(8,128)(2,1)S(1)}, u32[]{:S(2)}) copy-start(bf16[16,128,768]{2,1,0:T(8,128)(2,1)S(1)} %add_convert_fusion.2) | copy-start | bytes 9437188
  102.9 31.4 %copy-start.27 = (bf16[8,2,768]{2,0,1:T(8,128)(2,1)}, bf16[8,2,768]{2,0,1:T(8,128)(2,1)S(1)}, u32[]{:S(2)}) copy-start(bf16[8,2,768]{2,0,1:T(8,128)(2,1)S(1)} %fusion.132) | copy-start | bytes 73732
  105.5 28.8 %copy-start.77 = (f32[768]{0:T(1024)S(1)}, f32[768]{0:T(1024)}, u32[]{:S(2)}) copy-start(f32[768]{0:T(1024)} %get-tuple-element.47) | copy-start | bytes 9220
  125.7 24.4 %copy-start.31 = (f32[8,12,2,8]{3,2,1,0:T(2,128)}, f32[8,12,2,8]{3,2,1,0:T(2,128)S(1)}, u32[]{:S(2)}) copy-start(f32[8,12,2,8]{3,2,1,0:T(2,128)S(1)} %get-tuple-element.113) | copy-start | bytes 18436
  128.2 9.4 copy-start.36
  131.0 6.6 copy-start.32
  131.0 7.5 copy-start.66
  131.0 13.1 %slice-start.4 = ((s8[9437184]{0:T(1024)(128)(4,1)}), s8[4194304]{0:T(1024)(128)(4,1)S(1)}, s32[]{:S(2)}) async-start(s8[9437184]{0:T(1024)(128)(4,1)} %bitcast.322), calls=%async_computation.15 | async-start | bytes 8388608
  134.2 5.5 copy-start.25
  134.3 9.8 slice-start.5
  134.3 9.8 copy-start.57
  137.6 6.5 slice-start.6
  139.8 6.3 copy-start.44
  144.1 6.0 copy-start.42
  146.3 13.0 %copy-start.74 = (f32[8,2]{0,1:T(2,128)}, f32[8,2]{0,1:T(2,128)S(1)}, u32[]{:S(2)}) copy-start(f32[8,2]{0,1:T(2,128)S(1)} %negate_multiply_fusion.2) | copy-start | bytes 196
  146.3 3.8 copy-start.34
  154.3 11.8 %copy-start.35 = (bf16[8,2,768]{2,0,1:T(8,128)(2,1)S(1)}, bf16[8,2,768]{2,0,1:T(8,128)(2,1)}, u32[]{:S(2)}) copy-start(bf16[8,2,768]{2,0,1:T(8,128)(2,1)} %copy-done.34) | copy-start | bytes 73732
  154.3 12.6 %copy-start.64 = (f32[768]{0:T(1024)S(1)}, f32[768]{0:T(1024)}, u32[]{:S(2)}) copy-start(f32[768]{0:T(1024)} %get-tuple-element.72) | copy-start | bytes 9220
  156.3 9.7 copy-start.37
  158.0 296.0 %all-reduce.7.cloned.1.call-start = ((), (), s32[]{:S(2)}) async-start(), calls=%async_computation.10 | async-start | bytes 196608
  160.8 11.0 copy-start.65
  160.8 11.5 copy-start.76
  166.0 10.3 copy-start.59
  166.0 13.5 %copy-start.75 = (f32[8,2]{0,1:T(2,128)S(1)}, f32[8,2]{0,1:T(2,128)}, u32[]{:S(2)}) copy-start(f32[8,2]{0,1:T(2,128)} %copy-done.74) | copy-start | bytes 196
  174.2 14.2 %copy-start.55 = (f32[768]{0:T(1024)S(1)}, f32[768]{0:T(1024)}, u32[]{:S(2)}) copy-start(f32[768]{0:T(1024)} %copy-done.54) | copy-start | bytes 9220
  179.6 14.7 %copy-start.29 = (bf16[8,2,2304]{2,0,1:T(8,128)(2,1)}, bf16[8,2,2304]{2,0,1:T(8,128)(2,1)S(1)}, u32[]{:S(2)}) copy-start(bf16[8,2,2304]{2,0,1:T(8,128)(2,1)S(1)} %constant_dynamic-update-slice_fusion) | copy-start | bytes 221188
  185.1 9.2 slice-start
  188.4 5.8 copy-start.51
  188.5 5.8 slice-start.1
  201.0 32.2 %slice-start.2 = ((s8[6291456]{0:T(1024)(128)(4,1)}), s8[4194304]{0:T(1024)(128)(4,1)S(1)}, s32[]{:S(2)}) async-start(s8[6291456]{0:T(1024)(128)(4,1)} %bitcast.297), calls=%async_computation.13 | async-start | bytes 8388608
  201.6 31.6 %copy-start.19 = (bf16[16,128,768]{2,1,0:T(8,128)(2,1)}, bf16[16,128,768]{2,1,0:T(8,128)(2,1)S(1)}, u32[]{:S(2)}) copy-start(bf16[16,128,768]{2,1,0:T(8,128)(2,1)S(1)} %get-tuple-element.69) | copy-start | bytes 9437188
  201.6 31.6 %slice-start.3 = ((s8[6291456]{0:T(1024)(128)(4,1)}), s8[2097152]{0:T(1024)(128)(4,1)S(1)}, s32[]{:S(2)}) async-start(s8[6291456]{0:T(1024)(128)(4,1)} %bitcast.297), calls=%async_computation.14 | async-start | bytes 4194304
  201.6 31.6 %copy-start.41 = (f32[16,128]{1,0:T(8,128)S(1)}, f32[16,128]{1,0:T(8,128)}, u32[]{:S(2)}) copy-start(f32[16,128]{1,0:T(8,128)} %copy-done.40) | copy-start | bytes 24580
  201.6 31.6 %copy-start.53 = (f32[16,128]{1,0:T(8,128)S(1)}, f32[16,128]{1,0:T(8,128)}, u32[]{:S(2)}) copy-start(f32[16,128]{1,0:T(8,128)} %copy-done.52) | copy-start | bytes 24580
  201.6 31.6 %copy-start.61 = (f32[768]{0:T(1024)S(1)}, f32[768]{0:T(1024)}, u32[]{:S(2)}) copy-start(f32[768]{0:T(1024)} %copy-done.60) | copy-start | bytes 9220
  233.2 18.7 %copy-start.49 = (f32[16,128]{1,0:T(8,128)S(1)}, f32[16,128]{1,0:T(8,128)}, u32[]{:S(2)}) copy-start(f32[16,128]{1,0:T(8,128)} %copy-done.48) | copy-start | bytes 24580
  256.1 3.9 copy-start.10
  256.1 3.9 copy-start.15
  256.1 7.9 copy-start.62
  267.5 10.8 copy-start.9
  287.4 10.3 copy-start.7
  297.8 5.7 copy-start.6
  308.2 4.5 copy-start.8
  332.9 5.0 copy-start.28
  332.9 5.0 copy-start.30
  332.9 235.9 %reduce-scatter.10.cloned.1.call-start = ((), (), s32[]{:S(2)}) async-start(), calls=%async_computation.7 | async-start | bytes 4866048 | tf_op jit(solution)/shard_map/reduce_scatter | solution.py:276
  337.9 399.4 %reduce-scatter.8.cloned.1.call-start = ((), (), s32[]{:S(2)}) async-start(), calls=%async_computation.6 | async-start | bytes 14598144 | tf_op jit(solution)/shard_map/reduce_scatter | solution.py:275
  337.9 4.0 copy-start.22
  366.0 583.5 %reduce-scatter.14.cloned.1.call-start = ((), (), s32[]{:S(2)}) async-start(), calls=%async_computation.9 | async-start | bytes 19464192 | tf_op jit(solution)/shard_map/reduce_scatter | solution.py:278
  388.4 773.6 %reduce-scatter.12.cloned.1.call-start = ((), (), s32[]{:S(2)}) async-start(), calls=%async_computation.8 | async-start | bytes 19464192 | tf_op jit(solution)/shard_map/reduce_scatter | solution.py:277
  418.0 7.4 copy-start.63
  425.5 736.6 %copy-start.1 = (bf16[8,768]{1,0:T(8,128)(2,1)S(1)}, bf16[8,768]{1,0:T(8,128)(2,1)}, u32[]{:S(2)}) copy-start(bf16[8,768]{1,0:T(8,128)(2,1)} %param.24) | copy-start | bytes 36868
  (27 other events, 57.9 us)
Sparse Core Ops, SparseCore 0:
  158.1 20.6 reduce-scatter.5
  333.0 120.8 all-reduce.6
  460.9 107.8 reduce-scatter.9
  575.3 161.9 reduce-scatter.7
  744.1 205.3 reduce-scatter.13
  956.3 205.6 reduce-scatter.11
where the time goes:
time: 1170 us
  waiting for transfers between devices  720 us (62%)
  matrix products  240 us (21%)
  local copies, waits for them, and re-layouts  92.5 us (8%)
  other arithmetic  85.2 us (7%)
  between operations  15.7 us (1%)
  blocking collectives  15.6 us (1%)
    reduce_scatter x1, waiting for transfers between devices, per_device(): lax.psum_scatter(stacked[2], ('row', 'seg'), scatter_dimension=0, tiled=T...  213 us
    reduce_scatter x1, waiting for transfers between devices, per_device(): lax.psum_scatter(stacked[3], ('row', 'seg'), scatter_dimension=0, tiled=T...  212 us
    reduce_scatter x1, waiting for transfers between devices, per_device(): lax.psum_scatter(stacked[0], ('row', 'seg'), scatter_dimension=0, tiled=T...  168 us
    reduce_scatter x1, waiting for transfers between devices, per_device(): lax.psum_scatter(stacked[1], ('row', 'seg'), scatter_dimension=0, tiled=T...  110 us
    dot_general x8, matrix products, project_back(): jnp.einsum('...j,ij->...i', values, matrix, preferred_element_type=jnp.fl...  77.7 us
    dot_general x8, matrix products, project(): jnp.einsum('...i,ij->...j', values, matrix, preferred_element_type=jnp.fl...  62.1 us
    dot_general x8, matrix products, outer_total(): jnp.einsum('ni,nj->ij', values.reshape(-1, values.shape[-1]), grad_out.re...  54.3 us
    another operation x8, other arithmetic, per_device(): jnp.stack([seg_part, cross_part])  29.3 us
  transfers between devices with their start and end apart: 6, of which 6 were waited for; matrix products, arithmetic and copies ran while one was open for 11% of the time, Pallas kernels for 0%

commit v1 on v0

v1 whole, which is shorter than its diff:
```python
import functools

import jax
import jax.numpy as jnp
from jax import lax
from jax.experimental import pallas as pl
from jax.experimental.pallas import tpu as pltpu
from jax.sharding import PartitionSpec as P


HDIM = 64
SEGLEN = 128
LANES = 128
EPSILON = 1e-05
GELU_A = 0.7978845608028654
GELU_B = 0.044715 * GELU_A
F32, BF16 = jnp.float32, jnp.bfloat16


def mm(a, b):
    return lax.dot_general(a, b, (((1,), (0,)), ((), ())), preferred_element_type=F32)


def mm_nt(a, b):
    return lax.dot_general(a, b, (((1,), (1,)), ((), ())), preferred_element_type=F32)


def mm_tn(a, b):
    return lax.dot_general(a, b, (((0,), (0,)), ((), ())), preferred_element_type=F32)


def low_lanes(shape):
    return lax.broadcasted_iota(jnp.int32, shape, 1) < HDIM


def stack_heads(pair):
    keep = low_lanes(pair.shape)
    zero = jnp.zeros_like(pair)
    return jnp.concatenate([jnp.where(keep, pair, zero), jnp.where(keep, zero, pair)], axis=0)


def norm_stats(values):
    centered = values - jnp.mean(values, axis=-1, keepdims=True)
    variance = jnp.mean(centered * centered, axis=-1, keepdims=True)
    rstd = lax.rsqrt(variance + EPSILON)
    return centered * rstd, rstd


def gelu_both(u):
    square = u * u
    t = jnp.tanh(u * (GELU_A + GELU_B * square))
    half = 0.5 * u
    hidden = half + half * t
    slope = 0.5 + 0.5 * t + half * (1.0 - t * t) * (GELU_A + (3.0 * GELU_B) * square)
    return hidden, slope


def forward_kernel(
    x_ref, wqkv_hbm, wout_hbm, wup_hbm, wdown_hbm, bias_ref, gain_ref, bup_ref,
    qkv_ref, probs_ref, n1_ref, r1_ref, slope_ref, n2_ref, r2_ref, y_ref, cls_ref, xt_ref, mixedt_ref, firstt_ref, hiddent_ref,
    wqkv, wout, wup, wdown, mixed_ref, sems, *, ff_chunk,
):
    step = pl.program_id(0)
    copies = [
        pltpu.make_async_copy(src.at[0], dst, sems.at[i])
        for i, (src, dst) in enumerate(
            ((wqkv_hbm, wqkv), (wout_hbm, wout), (wup_hbm, wup), (wdown_hbm, wdown))
        )
    ]

    @pl.when(step == 0)
    def _():
        for copy in copies:
            copy.start()
        copies[0].wait()

    rows, width = x_ref.shape
    bias = bias_ref[...].astype(F32)
    gain = gain_ref[...].astype(F32)
    x = x_ref[...]
    xt_ref[...] = x.T
    for part in range(3):
        cols = slice(part * width, (part + 1) * width)
        out = mm(x, wqkv[:, cols])
        if part == 0:
            out = out + bias[0:1]
        if part == 2:
            out = out + bias[1:2]
        qkv_ref[:, cols] = out.astype(BF16)
    for seg in range(rows // SEGLEN):
        at = slice(seg * SEGLEN, (seg + 1) * SEGLEN)
        for pair in range(width // LANES):
            q = qkv_ref[at, pair * LANES : (pair + 1) * LANES]
            k = qkv_ref[at, width + pair * LANES : width + (pair + 1) * LANES]
            v = qkv_ref[at, 2 * width + pair * LANES : 2 * width + (pair + 1) * LANES]
            scores = mm_nt(k, stack_heads(q * HDIM**-0.5))
            e = jnp.exp(scores - jnp.max(scores, axis=0, keepdims=True))
            p = (e * (1.0 / jnp.sum(e, axis=0, keepdims=True))).astype(BF16)
            probs_ref[seg, pair] = p
            pt = jnp.concatenate([p[:, :SEGLEN].T, p[:, SEGLEN:].T], axis=1)
            mixed_ref[at, pair * LANES : (pair + 1) * LANES] = mm(pt, stack_heads(v)).astype(BF16)

    @pl.when(step == 0)
    def _():
        for copy in copies[1:]:
            copy.wait()

    mixed = mixed_ref[...]
    mixedt_ref[...] = mixed.T
    resid = x.astype(F32) + mm(mixed, wout[...]) + bias[2:3]
    n1, r1 = norm_stats(resid)
    n1_ref[...] = n1.astype(BF16)
    r1_ref[...] = jnp.broadcast_to(r1, r1_ref.shape)
    first = (n1 * gain[0:1] + bias[3:4]).astype(BF16)
    firstt_ref[...] = first.T
    total = first.astype(F32) + bias[4:5]
    inners = wup.shape[1]
    for c in range(inners // ff_chunk):
        cols = slice(c * ff_chunk, (c + 1) * ff_chunk)
        inner = mm(first, wup[:, cols]) + bup_ref[:, cols].astype(F32)
        hidden, slope = gelu_both(inner)
        hidden = hidden.astype(BF16)
        hiddent_ref[cols, :] = hidden.T
        slope_ref[:, cols] = slope.astype(BF16)
        total = total + mm(hidden, wdown[cols, :])
    n2, r2 = norm_stats(total)
    n2_ref[...] = n2.astype(BF16)
    r2_ref[...] = jnp.broadcast_to(r2, r2_ref.shape)
    y = (n2 * gain[1:2] + bias[5:6]).astype(BF16)
    y_ref[...] = y
    for seg in range(rows // SEGLEN):
        cls_ref[pl.ds(step * (rows // SEGLEN) + seg, 1), :] = y[seg * SEGLEN : seg * SEGLEN + 8].astype(F32)[0:1]


def forward_block(x, w_qkv, w_out, w_up, w_down, bias, gain, bup, tile=256, ff_chunk=768):
    total, width = x.shape
    inners = w_up.shape[-1]
    segs = tile // SEGLEN
    pairs = width // LANES
    any_spec = pl.BlockSpec(memory_space=pl.ANY)

    def rows_of(cols):
        return pl.BlockSpec((tile, cols), lambda i: (i, 0))

    def whole(a):
        return pl.BlockSpec(a.shape, lambda i: (0,) * a.ndim)

    def cols_of(rows):
        return pl.BlockSpec((rows, tile), lambda i: (0, i))

    outs = [
        ((total, 3 * width), BF16, rows_of(3 * width)),
        ((total // SEGLEN, pairs, SEGLEN, 2 * SEGLEN), BF16, pl.BlockSpec((segs, pairs, SEGLEN, 2 * SEGLEN), lambda i: (i, 0, 0, 0))),
        ((total, width), BF16, rows_of(width)),
        ((total, LANES), F32, rows_of(LANES)),
        ((total, inners), BF16, rows_of(inners)),
        ((total, width), BF16, rows_of(width)),
        ((total, LANES), F32, rows_of(LANES)),
        ((total, width), BF16, rows_of(width)),
        ((total // SEGLEN, width), F32, pl.BlockSpec((total // SEGLEN, width), lambda i: (0, 0))),
        ((width, total), BF16, cols_of(width)),
        ((width, total), BF16, cols_of(width)),
        ((width, total), BF16, cols_of(width)),
        ((inners, total), BF16, cols_of(inners)),
    ]
    return pl.pallas_call(
        functools.partial(forward_kernel, ff_chunk=ff_chunk),
        grid=(total // tile,),
        in_specs=[rows_of(width), any_spec, any_spec, any_spec, any_spec, whole(bias), whole(gain), whole(bup)],
        out_specs=[o[2] for o in outs],
        out_shape=[jax.ShapeDtypeStruct(o[0], o[1]) for o in outs],
        scratch_shapes=[
            pltpu.VMEM(w_qkv.shape[1:], BF16),
            pltpu.VMEM(w_out.shape[1:], BF16),
            pltpu.VMEM(w_up.shape[1:], BF16),
            pltpu.VMEM(w_down.shape[1:], BF16),
            pltpu.VMEM((tile, width), BF16),
            pltpu.SemaphoreType.DMA((4,)),
        ],
        compiler_params=pltpu.CompilerParams(vmem_limit_bytes=60 * 2**20),
        name="segment_forward",
    )(x, w_qkv, w_out, w_up, w_down, bias, gain, bup)

def fold_rows(values):
    rows, cols = values.shape
    return jnp.sum(values.reshape(rows // 8, 8, cols), axis=0)


def norm_back(grad, gain, normal, rstd):
    scaled = grad * gain
    a = jnp.mean(scaled, axis=-1, keepdims=True)
    b = jnp.mean(scaled * normal, axis=-1, keepdims=True)
    return (scaled - a - normal * b) * rstd


def backward_kernel(
    gcls_ref, ccls_ref, cot_ref, y_ref, n2_ref, r2_ref, slope_ref, n1_ref, r1_ref, qkv_ref, probs_ref,
    wqkv_hbm, wout_hbm, wup_hbm, wdown_hbm, gain_ref,
    out_ref, gsecond_ref, ginner_ref, gbranch_ref, gqkv_ref, gx_ref, sums_ref, bsums_ref,
    wqkv, wout, wup, wdown, sems, *, ff_chunk,
):
    step = pl.program_id(0)
    copies = [
        pltpu.make_async_copy(src.at[0], dst, sems.at[i])
        for i, (src, dst) in enumerate(
            ((wdown_hbm, wdown), (wup_hbm, wup), (wout_hbm, wout), (wqkv_hbm, wqkv))
        )
    ]

    @pl.when(step == 0)
    def _():
        for copy in copies:
            copy.start()
        sums_ref[...] = jnp.zeros_like(sums_ref)
        bsums_ref[...] = jnp.zeros_like(bsums_ref)
        for copy in copies[:2]:
            copy.wait()

    rows, width = cot_ref.shape
    segs = rows // SEGLEN
    inners = wup.shape[1]
    gain = gain_ref[...].astype(F32)
    place = lax.broadcasted_iota(jnp.int32, (rows, width), 0)
    gy = cot_ref[...].astype(F32)
    y = y_ref[...].astype(F32)
    for seg in range(segs):
        at = pl.ds(step * segs + seg, 1)
        gy = jnp.where(place == seg * SEGLEN, gcls_ref[at, :], gy)
        y = jnp.where(place == seg * SEGLEN, ccls_ref[at, :], y)
    out_ref[...] = y.astype(BF16)
    n2 = n2_ref[...].astype(F32)
    sums_ref[0] += fold_rows(gy * n2)
    sums_ref[1] += fold_rows(gy)
    g_two = norm_back(gy, gain[1:2], n2, r2_ref[:, 0:1])
    g_second = g_two.astype(BF16)
    gsecond_ref[...] = g_second
    sums_ref[2] += fold_rows(g_second.astype(F32))
    g_first = g_two
    for c in range(inners // ff_chunk):
        cols = slice(c * ff_chunk, (c + 1) * ff_chunk)
        g_inner = mm_nt(g_second, wdown[cols, :]) * slope_ref[:, cols].astype(F32)
        g_low = g_inner.astype(BF16)
        ginner_ref[:, cols] = g_low
        bsums_ref[:, cols] += fold_rows(g_low.astype(F32))
        g_first = g_first + mm_nt(g_low, wup[:, cols])
    n1 = n1_ref[...].astype(F32)
    sums_ref[3] += fold_rows(g_first * n1)
    sums_ref[4] += fold_rows(g_first)
    g_one = norm_back(g_first, gain[0:1], n1, r1_ref[:, 0:1])
    g_branch = g_one.astype(BF16)
    gbranch_ref[...] = g_branch
    sums_ref[5] += fold_rows(g_branch.astype(F32))

    @pl.when(step == 0)
    def _():
        for copy in copies[2:]:
            copy.wait()

    g_mixed = mm_nt(g_branch, wout[...]).astype(BF16)
    for seg in range(segs):
        at = slice(seg * SEGLEN, (seg + 1) * SEGLEN)
        for pair in range(width // LANES):
            lanes = [slice(part * width + pair * LANES, part * width + (pair + 1) * LANES) for part in range(3)]
            q = qkv_ref[at, lanes[0]] * HDIM**-0.5
            k = qkv_ref[at, lanes[1]]
            v = qkv_ref[at, lanes[2]]
            p_low = probs_ref[seg, pair]
            p = p_low.astype(F32)
            g_out = stack_heads(g_mixed[at, lanes[0]])
            g_p = mm_nt(v, g_out)
            inner_sum = jnp.sum(g_p * p, axis=0, keepdims=True)
            g_s = (p * (g_p - inner_sum)).astype(BF16)
            g_v = mm(p_low, g_out)
            g_k = mm(g_s, stack_heads(q))
            g_st = jnp.concatenate([g_s[:, :SEGLEN].T, g_s[:, SEGLEN:].T], axis=1)
            g_q = mm(g_st, stack_heads(k)) * HDIM**-0.5
            gqkv_ref[at, lanes[0]] = g_q.astype(BF16)
            gqkv_ref[at, lanes[1]] = g_k.astype(BF16)
            gqkv_ref[at, lanes[2]] = g_v.astype(BF16)
    g_qkv = gqkv_ref[...]
    sums_ref[6] += fold_rows(g_qkv[:, :width].astype(F32))
    sums_ref[7] += fold_rows(g_qkv[:, 2 * width :].astype(F32))
    gx_ref[...] = g_one + mm_nt(g_qkv, wqkv[...])


def backward_block(gcls, ccls, cot, y, n2, r2, slope, n1, r1, qkv, probs, w_qkv, w_out, w_up, w_down, gain, tile=256, ff_chunk=768):
    total, width = cot.shape
    inners = w_up.shape[-1]
    segs = tile // SEGLEN
    pairs = width // LANES
    any_spec = pl.BlockSpec(memory_space=pl.ANY)

    def rows_of(cols):
        return pl.BlockSpec((tile, cols), lambda i: (i, 0))

    def whole(a):
        return pl.BlockSpec(a.shape, lambda i: (0,) * len(a.shape))

    outs = [
        ((total, width), BF16, rows_of(width)),
        ((total, width), BF16, rows_of(width)),
        ((total, inners), BF16, rows_of(inners)),
        ((total, width), BF16, rows_of(width)),
        ((total, 3 * width), BF16, rows_of(3 * width)),
        ((total, width), F32, rows_of(width)),
        ((8, 8, width), F32, pl.BlockSpec((8, 8, width), lambda i: (0, 0, 0))),
        ((8, inners), F32, pl.BlockSpec((8, inners), lambda i: (0, 0))),
    ]
    return pl.pallas_call(
        functools.partial(backward_kernel, ff_chunk=ff_chunk),
        grid=(total // tile,),
        in_specs=[whole(gcls), whole(ccls), rows_of(width), rows_of(width), rows_of(width), rows_of(LANES), rows_of(inners),
                  rows_of(width), rows_of(LANES), rows_of(3 * width),
                  pl.BlockSpec((segs, pairs, SEGLEN, 2 * SEGLEN), lambda i: (i, 0, 0, 0)),
                  any_spec, any_spec, any_spec, any_spec, whole(gain)],
        out_specs=[o[2] for o in outs],
        out_shape=[jax.ShapeDtypeStruct(o[0], o[1]) for o in outs],
        scratch_shapes=[
            pltpu.VMEM(w_qkv.shape[1:], BF16),
            pltpu.VMEM(w_out.shape[1:], BF16),
            pltpu.VMEM(w_up.shape[1:], BF16),
            pltpu.VMEM(w_down.shape[1:], BF16),
            pltpu.SemaphoreType.DMA((4,)),
        ],
        compiler_params=pltpu.CompilerParams(vmem_limit_bytes=60 * 2**20),
        name="segment_backward",
    )(gcls, ccls, cot, y, n2, r2, slope, n1, r1, qkv, probs, w_qkv, w_out, w_up, w_down, gain)

NEGATIVE = -1000000000.0
MESH = pl.DeviceIdType.MESH


def turned(values):
    return values.astype(F32).T.astype(BF16)


def cross_kernel(
    cls_ref, cot_ref, place_ref, keycol_ref, keyrow_ref, table_ref, wqkv_hbm, wout_hbm, wup_hbm, wdown_hbm, bias_ref, gain_ref, bup_ref,
    ccls_ref, gcls_ref, sums_ref, bsums_ref, gpos_ref, xt_ref, mixedt_ref, firstt_ref, hiddent_ref, gqkv_ref, gbranch_ref, ginner_ref, gsecond_ref,
    wqkv, wout, wup, wdown, packed, gathered, qkv_ref, probs_ref, mixed_ref, slope_ref, whole_ref, sems, send_sems, recv_sems, *, ff_chunk, devices,
):
    copies = [
        pltpu.make_async_copy(src.at[1], dst, sems.at[i])
        for i, (src, dst) in enumerate(
            ((wqkv_hbm, wqkv), (wout_hbm, wout), (wup_hbm, wup), (wdown_hbm, wdown))
        )
    ]
    for copy in copies:
        copy.start()
    own, width = cls_ref.shape
    rows = own * devices
    inners = wup.shape[1]
    me = lax.axis_index("seg")
    line = lax.axis_index("row")
    barrier = pltpu.get_barrier_semaphore()
    for hop in range(1, devices):
        pl.semaphore_signal(barrier, inc=1, device_id=(line, lax.rem(me + hop, devices)), device_id_type=MESH)
    packed[0:own, :] = cls_ref[...].astype(BF16)
    packed[own:, :] = cot_ref[...]
    pl.semaphore_wait(barrier, devices - 1)
    sends = []
    for hop in range(1, devices):
        send = pltpu.make_async_remote_copy(
            src_ref=packed, dst_ref=gathered.at[hop], send_sem=send_sems.at[hop], recv_sem=recv_sems.at[hop],
            device_id=(line, lax.rem(me + hop, devices)), device_id_type=MESH,
        )
        send.start()
        sends.append(send)
    bias = bias_ref[...].astype(F32)
    gain = gain_ref[...].astype(F32)
    onehot = (place_ref[...] == lax.broadcasted_iota(jnp.int32, (rows, table_ref.shape[0]), 1)).astype(F32)
    embed = mm(onehot.astype(BF16), table_ref[...])
    allowed = keycol_ref[...] == keyrow_ref[...]
    gathered[0] = packed[...]
    for send in sends:
        send.wait()
    for hop in range(devices):
        at = pl.ds(pl.multiple_of(lax.rem(me - hop + devices, devices) * own, own), own)
        block = gathered[hop].astype(F32)
        whole_ref[0, at, :] = block[:own]
        whole_ref[1, at, :] = block[own:]
    x = (whole_ref[0] + embed).astype(BF16)
    gy = whole_ref[1]
    xt_ref[...] = turned(x)
    copies[0].wait()
    for part in range(3):
        cols = slice(part * width, (part + 1) * width)
        out = mm(x, wqkv[:, cols])
        if part == 0:
            out = out + bias[0:1]
        if part == 2:
            out = out + bias[1:2]
        qkv_ref[:, cols] = out.astype(BF16)
    for pair in range(width // LANES):
        q, k, v = (qkv_ref[:, part * width + pair * LANES : part * width + (pair + 1) * LANES] for part in range(3))
        scores = jnp.where(allowed, mm_nt(k, stack_heads(q * HDIM**-0.5)), NEGATIVE)
        e = jnp.exp(scores - jnp.max(scores, axis=0, keepdims=True))
        p = e * (1.0 / jnp.sum(e, axis=0, keepdims=True))
        probs_ref[pair] = p
        pt = p.T.astype(BF16)
        low = low_lanes((rows, LANES))
        mixed = jnp.where(low, mm(pt[:rows], v), mm(pt[rows:], v))
        mixed_ref[:, pair * LANES : (pair + 1) * LANES] = mixed.astype(BF16)
    copies[1].wait()
    mixed = mixed_ref[...]
    mixedt_ref[...] = turned(mixed)
    n1, r1 = norm_stats(x.astype(F32) + mm(mixed, wout[...]) + bias[2:3])
    first = (n1 * gain[0:1] + bias[3:4]).astype(BF16)
    firstt_ref[...] = turned(first)
    copies[2].wait()
    copies[3].wait()
    total = first.astype(F32) + bias[4:5]
    for c in range(inners // ff_chunk):
        cols = slice(c * ff_chunk, (c + 1) * ff_chunk)
        hidden, slope = gelu_both(mm(first, wup[:, cols]) + bup_ref[:, cols].astype(F32))
        hidden = hidden.astype(BF16)
        hiddent_ref[cols, :] = turned(hidden)
        slope_ref[:, cols] = slope
        total = total + mm(hidden, wdown[cols, :])
    n2, r2 = norm_stats(total)
    mine = pl.ds(pl.multiple_of(me * own, own), own)
    whole_ref[0] = (n2 * gain[1:2] + bias[5:6]).astype(BF16).astype(F32)
    ccls_ref[...] = whole_ref[0, mine, :]

    def row_sum(values):
        return jnp.sum(values.astype(F32), axis=0, keepdims=True)

    sums_ref[0:1, :] = row_sum(gy * n2)
    sums_ref[1:2, :] = row_sum(gy)
    g_two = norm_back(gy, gain[1:2], n2, r2)
    g_second = g_two.astype(BF16)
    gsecond_ref[...] = g_second
    sums_ref[2:3, :] = row_sum(g_second)
    g_first = g_two
    for c in range(inners // ff_chunk):
        cols = slice(c * ff_chunk, (c + 1) * ff_chunk)
        g_inner = (mm_nt(g_second, wdown[cols, :]) * slope_ref[:, cols]).astype(BF16)
        ginner_ref[:, cols] = g_inner
        bsums_ref[:, cols] = row_sum(g_inner)
        g_first = g_first + mm_nt(g_inner, wup[:, cols])
    sums_ref[3:4, :] = row_sum(g_first * n1)
    sums_ref[4:5, :] = row_sum(g_first)
    g_one = norm_back(g_first, gain[0:1], n1, r1)
    g_branch = g_one.astype(BF16)
    gbranch_ref[...] = g_branch
    sums_ref[5:6, :] = row_sum(g_branch)
    g_mixed = mm_nt(g_branch, wout[...]).astype(BF16)
    for pair in range(width // LANES):
        lanes = [slice(part * width + pair * LANES, part * width + (pair + 1) * LANES) for part in range(3)]
        q, k, v = (qkv_ref[:, at] for at in lanes)
        p = probs_ref[pair]
        g_out = stack_heads(g_mixed[:, lanes[0]])
        g_p = mm_nt(v, g_out)
        g_s = p * (g_p - jnp.sum(g_p * p, axis=0, keepdims=True))
        g_st = g_s.T.astype(BF16)
        g_s = g_s.astype(BF16)
        low = low_lanes((rows, LANES))
        g_q = jnp.where(low, mm(g_st[:rows], k), mm(g_st[rows:], k)) * HDIM**-0.5
        gqkv_ref[:, lanes[0]] = g_q.astype(BF16)
        gqkv_ref[:, lanes[1]] = mm(g_s, stack_heads(q * HDIM**-0.5)).astype(BF16)
        gqkv_ref[:, lanes[2]] = mm(p.astype(BF16), g_out).astype(BF16)
    g_qkv = gqkv_ref[...]
    sums_ref[6:7, :] = row_sum(g_qkv[:, :width])
    sums_ref[7:8, :] = row_sum(g_qkv[:, 2 * width :])
    g_x = g_one + mm_nt(g_qkv, wqkv[...])
    whole_ref[1] = g_x
    gcls_ref[...] = whole_ref[1, mine, :]
    gpos_ref[...] = lax.dot_general(onehot, g_x, (((0,), (0,)), ((), ())), preferred_element_type=F32, precision=lax.Precision.HIGHEST)


def cross_block(cls, cot, place, keys, table, w_qkv, w_out, w_up, w_down, bias, gain, bup, devices, ff_chunk=768):
    own, width = cls.shape
    rows = own * devices
    inners = w_up.shape[-1]
    vmem = pl.BlockSpec(memory_space=pltpu.VMEM)
    any_spec = pl.BlockSpec(memory_space=pl.ANY)
    outs = [
        ((own, width), F32), ((own, width), F32), ((8, width), F32), ((1, inners), F32), (table.shape, F32),
        ((width, rows), BF16), ((width, rows), BF16), ((width, rows), BF16), ((inners, rows), BF16),
        ((rows, 3 * width), BF16), ((rows, width), BF16), ((rows, inners), BF16), ((rows, width), BF16),
    ]
    return pl.pallas_call(
        functools.partial(cross_kernel, ff_chunk=ff_chunk, devices=devices),
        in_specs=[vmem] * 6 + [any_spec] * 4 + [vmem] * 3,
        out_specs=[vmem] * len(outs),
        out_shape=[jax.ShapeDtypeStruct(*o) for o in outs],
        scratch_shapes=[
            pltpu.VMEM(w_qkv.shape[1:], BF16),
            pltpu.VMEM(w_out.shape[1:], BF16),
            pltpu.VMEM(w_up.shape[1:], BF16),
            pltpu.VMEM(w_down.shape[1:], BF16),
            pltpu.VMEM((2 * own, width), BF16),
            pltpu.VMEM((devices, 2 * own, width), BF16),
            pltpu.VMEM((rows, 3 * width), BF16),
            pltpu.VMEM((width // LANES, rows, 2 * rows), F32),
            pltpu.VMEM((rows, width), BF16),
            pltpu.VMEM((rows, inners), F32),
            pltpu.VMEM((2, rows, width), F32),
            pltpu.SemaphoreType.DMA((4,)),
            pltpu.SemaphoreType.DMA((devices,)),
            pltpu.SemaphoreType.DMA((devices,)),
        ],
        compiler_params=pltpu.CompilerParams(vmem_limit_bytes=50 * 2**20, collective_id=0, has_side_effects=True),
        name="cross_block",
    )(cls, cot, place, keys, jnp.tile(keys.reshape(1, rows), (1, 2)), table, w_qkv, w_out, w_up, w_down, bias, gain, bup)

def small_grads(sums, bsums, csums, cbsums, gpos, cross_share):
    seg_rows = jnp.sum(sums, axis=1)
    cross_rows = csums * cross_share
    seg_up = jnp.sum(bsums, axis=0)
    order = jnp.array([6, 7, 5, 4, 2, 1])
    biases = jnp.stack([seg_rows[order], cross_rows[order]])
    gains = jnp.stack([seg_rows[jnp.array([3, 0])], cross_rows[jnp.array([3, 0])]])
    ups = jnp.stack([seg_up, cbsums[0] * cross_share])
    return biases.reshape(-1), gains.reshape(-1), ups.reshape(-1), (gpos * cross_share).reshape(-1)


def per_device(
    tokens, doc_ids, w_qkv, w_out, w_up, w_down, biases, gains, b_up, pos_table, cotangent, *, sizes
):
    lines, planes = sizes
    row_count, local_length, width = tokens.shape
    seg_here = local_length // SEGLEN
    segments = doc_ids.shape[1]
    total = row_count * local_length
    own = row_count * seg_here
    me = lax.axis_index("seg")
    axes = ("row", "seg")

    seg_place = jnp.arange(segments)
    same_doc = doc_ids[:, :, None] == doc_ids[:, None, :]
    doc_start = jnp.min(jnp.where(same_doc, seg_place[None, None, :], segments), axis=2)

    def by_device(values):
        return values.reshape(row_count, planes, seg_here).transpose(1, 0, 2).reshape(-1, 1)

    place = by_device(seg_place[None, :] - doc_start)
    keys = by_device(doc_ids + segments * jnp.arange(row_count)[:, None])

    cot = cotangent.reshape(total, width)
    cot_cls = cotangent.reshape(own, SEGLEN, width)[:, 0]
    qkv, probs, n1, r1, slope, n2, r2, y, cls, xt, mixedt, firstt, hiddent = forward_block(
        tokens.reshape(total, width), w_qkv, w_out, w_up, w_down, biases[0], gains[0], b_up[0:1]
    )
    (ccls, gcls, csums, cbsums, gpos, cxt, cmixedt, cfirstt, chiddent, cgqkv, cgbranch, cginner, cgsecond) = cross_block(
        cls, cot_cls, place, keys, pos_table, w_qkv, w_out, w_up, w_down, biases[1], gains[1], b_up[1:2], planes
    )
    output, gsecond, ginner, gbranch, gqkv, gx, sums, bsums = backward_block(
        gcls, ccls, cot, y, n2, r2, slope, n1, r1, qkv, probs, w_qkv, w_out, w_up, w_down, gains[0]
    )
    small = small_grads(sums, bsums, csums, cbsums, gpos, 1.0 / planes)
    small = [lax.psum_scatter(part, axes, scatter_dimension=0, tiled=True) for part in small]

    def mine(values, dim):
        return lax.dynamic_slice_in_dim(values, me * own, own, dim)

    big = []
    for seg_a, seg_b, cross_a, cross_b in (
        (xt, gqkv, cxt, cgqkv), (mixedt, gbranch, cmixedt, cgbranch), (firstt, ginner, cfirstt, cginner), (hiddent, gsecond, chiddent, cgsecond)
    ):
        both = jnp.concatenate([mm(seg_a, seg_b), mm(mine(cross_a, 1), mine(cross_b, 0))], axis=0)
        big.append(lax.psum_scatter(both, axes, scatter_dimension=0, tiled=True))
    return (output.reshape(tokens.shape), gx.reshape(tokens.shape), *big, *small)


def solution(mesh):
    sizes = (mesh.shape["row"], mesh.shape["seg"])
    tokens_at = P("row", "seg", None)
    return jax.shard_map(
        functools.partial(per_device, sizes=sizes),
        mesh=mesh,
        in_specs=(tokens_at, P("row", None)) + (P(),) * 8 + (tokens_at,),
        out_specs=(tokens_at, tokens_at) + (P(("row", "seg"), None),) * 4 + (P(("row", "seg")),) * 4,
        check_vma=False,
    )
```

time: 1170 us -> 1030 us (0.88)
  matrix products: 240 us -> 45.2 us
  Pallas kernels: 0 us -> 157 us
  local copies, waits for them, and re-layouts: 92.5 us -> 20.1 us
  other arithmetic: 85.2 us -> 29.3 us
  waiting for transfers between devices: 720 us -> 756 us
  blocking collectives: 15.6 us -> 0 us
    dot_general x38 -> x8, matrix products: 240 us -> 45.2 us  [mm(): lax.dot_general(a, b, (((1,), (0,)), ((), ())), preferred_element_type=F32)]
    pallas_call x0 -> x3, Pallas kernels: none -> 157 us  [the longest x1 72 us: backward_block(): pl.pallas_call(functools.partial(backward_kernel, ff_chunk=ff_chunk), gri...]
    unnamed x7 -> x6, waiting for transfers between devices: 14.9 us -> 50.5 us
    another operation x8 -> x2, other arithmetic: 29.3 us -> 0.01 us  [the longest x1 0.01 us: small_grads(): biases = jnp.stack([seg_rows[order], cross_rows[order]])]
    reduce_sum x19 -> x2, other arithmetic: 28.9 us -> 1.9 us  [the longest x1 0.98 us: small_grads(): seg_rows = jnp.sum(sums, axis=1)]
    concatenate x2 -> x4, other arithmetic: 1.65 us -> 25.5 us  [per_device(): jnp.concatenate([mm(seg_a, seg_b), mm(mine(cross_a, 1), mine(cross_b, 0))...]
    convert_element_type x10 -> x0, other arithmetic: 23.3 us -> none  [the longest x2 11.6 us: attend_back(): grad_scores = (attn_probs * (grad_probs - inner_sum)).astype(jnp.bfloat16)]
    reshape x17 -> x5, local copies, waits for them, and re-layouts: 19.2 us -> 1.98 us  [the longest x1 0.61 us: small_grads(): gains.reshape(-1)]
  transfers between devices with their start and end apart: 6 -> 5, of which waited for: 6 -> 5; matrix products, arithmetic and copies ran while one was open for 11% -> 7% of each run, Pallas kernels for 0% -> 0%
where the time goes in v1:
time: 1030 us; the launch traced here: 1020 us
  waiting for transfers between devices  756 us (73%)
  Pallas kernels  157 us (15%)
  matrix products  45.2 us (4%)
  other arithmetic  29.3 us (3%)
  local copies, waits for them, and re-layouts  20.1 us (2%)
  between operations  14.3 us (1%)
    reduce_scatter x4, waiting for transfers between devices, per_device(): big.append(lax.psum_scatter(both, axes, scatter_dimension=0, tiled=True))  706 us
    pallas_call x1, Pallas kernels, backward_block(): pl.pallas_call(functools.partial(backward_kernel, ff_chunk=ff_chunk), gri...  72 us
    pallas_call x1, Pallas kernels, forward_block(): pl.pallas_call(functools.partial(forward_kernel, ff_chunk=ff_chunk), grid...  64.1 us
    unnamed x6, waiting for transfers between devices  50.5 us
    dot_general x8, matrix products, mm(): lax.dot_general(a, b, (((1,), (0,)), ((), ())), preferred_element_type=F32)  45.2 us
    concatenate x4, other arithmetic, per_device(): jnp.concatenate([mm(seg_a, seg_b), mm(mine(cross_a, 1), mine(cross_b, 0))...  25.5 us
    pallas_call x1, Pallas kernels, cross_block(): pl.pallas_call(functools.partial(cross_kernel, ff_chunk=ff_chunk, devices...  21.3 us
  transfers between devices with their start and end apart: 5, of which 5 were waited for; matrix products, arithmetic and copies ran while one was open for 7% of the time, Pallas kernels for 0%

profile of v1, /device:TPU:0, one launch (start us, length us, event | category | flops | bytes accessed | tf_op | source)
XLA Modules:
  0.0 1022.6 jit_solution(14470796737674785763)
XLA Ops:
  7.2 0.0 all-reduce.7.cloned.1.call-start
  7.2 0.8 copy.54
  8.0 0.1 copy.55
  8.1 0.1 reshape.125.keycol_ref
  8.2 0.1 tile.10
  8.3 1.0 select_reduce_fusion
  9.3 0.8 fusion.16
  10.2 1.3 slice_bitcast_fusion
  11.5 1.4 fusion.17
  12.9 0.1 tile.12.keyrow_ref
  13.0 1.0 slice.37
  13.9 0.1 copy.52
  14.0 0.1 subtract_bitcast_fusion
  14.1 0.1 copy.53
  14.2 0.1 reshape.124.place_ref
  14.3 0.7 pad_clamp_fusion.1
  14.9 0.6 copy_bitcast_fusion.1
  15.5 64.1 %segment_forward.1 = (bf16[2048,2304]{1,0:T(8,128)(2,1)}, bf16[16,6,128,256]{3,2,1,0:T(8,128)(2,1)}, bf16[2048,768]{1,0:T(8,128)(2,1)}, f32[2048,128]{1,0:T(8,12...) custom-call(bf16[2048,768]{1,0:T(8,128)(2,1)} %bitcast.41, ...), custom_call_target="tpu_custom_call" | custom-call | tf_op jit(solution)/shard_map/segment_forward/pallas_call | solution.py:166
  79.7 0.8 copy-done.2
  80.5 21.3 %cross_block.1 = (f32[16,768]{1,0:T(8,128)S(1)}, f32[16,768]{1,0:T(8,128)S(1)}, f32[8,768]{1,0:T(8,128)S(1)}, f32[1,3072]{1,0:T(1,128)S(1)}, f32[8,768]{1,0:T(8,...) custom-call(f32[16,768]{1,0:T(8,128)S(1)} %copy-done.2, ...), custom_call_target="tpu_custom_call" | custom-call | tf_op jit(solution)/shard_map/cross_block/pallas_call | solution.py:482
  101.8 0.6 copy-done
  102.4 0.6 copy-done.1
  103.0 72.0 %segment_backward.1 = (bf16[2048,768]{1,0:T(8,128)(2,1)}, bf16[2048,768]{1,0:T(8,128)(2,1)}, bf16[2048,3072]{1,0:T(8,128)(2,1)}, bf16[2048,768]{1,0:T(8,128)(2,1...) custom-call(f32[16,768]{1,0:T(8,128)} %copy-done.1, ...), custom_call_target="tpu_custom_call" | custom-call | tf_op jit(solution)/shard_map/segment_backward/pallas_call | solution.py:309
  175.0 1.0 reduce_sum.18
  176.0 0.6 gather_fusion
  176.6 0.6 gather_fusion.1
  177.2 0.6 gather_fusion.2
  177.7 0.6 gather_fusion.3
  178.3 0.6 reshape.88
  178.9 0.6 reshape.89
  179.6 0.9 reduce_sum.19
  180.5 0.6 copy.63
  181.1 0.6 reshape.91
  181.7 0.0 all-reduce.7.cloned.1.call-update
  181.8 0.0 reduce-scatter.7.cloned.1.call-start
  181.8 5.4 fusion.19
  187.3 0.5 fusion.4
  187.8 2.4 pad_maximum_fusion.3
  190.2 0.0 reduce-scatter.7.cloned.1.call-update
  190.2 0.0 reduce-scatter.5.cloned.1.call-start
  190.3 1.1 fusion.6
  191.4 0.7 copy-done.6
  192.2 10.0 fusion.18
  202.2 5.4 pad_maximum_fusion.2
  207.5 0.0 reduce-scatter.5.cloned.1.call-update
  207.6 0.0 reduce-scatter.11.cloned.1.call-start
  207.6 1.4 fusion
  209.1 0.4 copy-done.7
  209.5 12.5 %fusion.21 = f32[3072,768]{1,0:T(8,128)S(1)} fusion(bf16[3072,2048]{1,0:T(8,128)(2,1)} %get-tuple-element.69, bf16[2048,768]{1,0:T(8,128)(2,1)S(1)} %copy-done.7), kind=kOutput, calls=%fused_computation.47 | convolution fusion | flops 9663676416 | bytes 25165824 | tf_op jit(solution)/shard_map/dot_general | solution.py:21
  222.0 10.6 %pad_maximum_fusion.1 = f32[6144,768]{1,0:T(8,128)} fusion(f32[3072,768]{1,0:T(8,128)S(1)} %fusion, f32[3072,768]{1,0:T(8,128)S(1)} %fusion.21), kind=kLoop, calls=%fused_computation.5 | loop fusion | flops 4718592 | bytes 37748736 | tf_op jit(solution)/shard_map/concatenate | solution.py:561
  232.7 0.0 reduce-scatter.9.cloned.1.call-start
  232.7 1.4 fusion.2
  234.2 0.4 copy-done.5
  234.6 12.8 %fusion.20 = f32[768,3072]{1,0:T(8,128)S(1)} fusion(bf16[768,2048]{1,0:T(8,128)(2,1)S(1)} %copy-done.5, bf16[2048,3072]{1,0:T(8,128)(2,1)} %get-tuple-element.66), kind=kOutput, calls=%fused_computation.46 | convolution fusion | flops 9663676416 | bytes 25165824 | tf_op jit(solution)/shard_map/dot_general | solution.py:21
  247.4 7.1 pad_maximum_fusion
  254.5 50.4 %all-reduce.7.cloned.1.call-done = (f32[9216]{0:T(1024)}, f32[3072]{0:T(1024)}, f32[6144]{0:T(1024)}, f32[6144]{0:T(1024)}) async-done(((f32[9216]{0:T(1024)}, f32[3072]{0:T(1024)}, f32[6144]{0:T(1024)}, f32[6144]{0:T(1024)}), (f32[9216]{0:T(1024)}, f32[3072]{0:T(1024)}, f32[6144]{0:T(1024)}, f32[6144]{0:T(1024)})) %all-reduce.7.cloned.1.call-update) | async-done | bytes 98320
  305.0 1.3 dynamic-slice.2
  306.3 1.3 dynamic-slice.3
  307.6 1.3 dynamic-slice
  309.0 1.3 dynamic-slice.1
  310.3 108.7 %reduce-scatter.7.cloned.1.call-done = f32[48,768]{1,0:T(8,128)} async-done(((f32[1536,768]{1,0:T(8,128)}), f32[48,768]{1,0:T(8,128)}) %reduce-scatter.7.cloned.1.call-update) | async-done | bytes 147472 | tf_op jit(solution)/shard_map/reduce_scatter | solution.py:562
  418.9 169.6 %reduce-scatter.5.cloned.1.call-done = f32[48,2304]{1,0:T(8,128)} async-done(((f32[1536,2304]{1,0:T(8,128)}), f32[48,2304]{1,0:T(8,128)}) %reduce-scatter.5.cloned.1.call-update) | async-done | bytes 442384 | tf_op jit(solution)/shard_map/reduce_scatter | solution.py:562
  588.6 213.5 %reduce-scatter.11.cloned.1.call-done = f32[192,768]{1,0:T(8,128)} async-done(((f32[6144,768]{1,0:T(8,128)}), f32[192,768]{1,0:T(8,128)}) %reduce-scatter.11.cloned.1.call-update) | async-done | bytes 589840 | tf_op jit(solution)/shard_map/reduce_scatter | solution.py:562
  802.1 213.7 %reduce-scatter.9.cloned.1.call-done = f32[48,3072]{1,0:T(8,128)} async-done(((f32[1536,3072]{1,0:T(8,128)}), f32[48,3072]{1,0:T(8,128)}) %reduce-scatter.9.cloned.1.call-update) | async-done | bytes 589840 | tf_op jit(solution)/shard_map/reduce_scatter | solution.py:562
  (24 shorter events, 0.1 us)
Async XLA Ops:
  7.2 297.8 %all-reduce.7.cloned.1.call-start = ((), (), s32[]{:S(2)}) async-start(), calls=%async_computation.8 | async-start | bytes 196608
  15.5 64.2 %copy-start.3 = (bf16[8,768]{1,0:T(8,128)(2,1)S(1)}, bf16[8,768]{1,0:T(8,128)(2,1)}, u32[]{:S(2)}) copy-start(bf16[8,768]{1,0:T(8,128)(2,1)} %table_ref.1) | copy-start | bytes 36868
  79.7 0.8 copy-start.2
  101.8 0.6 copy-start
  102.4 0.6 copy-start.1
  103.0 74.1 %copy-start.4 = (s32[2]{0:T(128)S(1)}, s32[2]{0:T(128)}, u32[]{:S(2)}) copy-start(s32[2]{0:T(128)} %constant.42) | copy-start | bytes 28
  181.8 237.2 %reduce-scatter.7.cloned.1.call-start = ((), (), s32[]{:S(2)}) async-start(), calls=%async_computation.5 | async-start | bytes 4866048 | tf_op jit(solution)/shard_map/reduce_scatter | solution.py:562
  190.2 398.3 %reduce-scatter.5.cloned.1.call-start = ((), (), s32[]{:S(2)}) async-start(), calls=%async_computation.4 | async-start | bytes 14598144 | tf_op jit(solution)/shard_map/reduce_scatter | solution.py:562
  190.3 1.9 copy-start.6
  207.6 594.5 %reduce-scatter.11.cloned.1.call-start = ((), (), s32[]{:S(2)}) async-start(), calls=%async_computation.7 | async-start | bytes 19464192 | tf_op jit(solution)/shard_map/reduce_scatter | solution.py:562
  207.6 1.9 copy-start.7
  232.7 783.1 %reduce-scatter.9.cloned.1.call-start = ((), (), s32[]{:S(2)}) async-start(), calls=%async_computation.6 | async-start | bytes 19464192 | tf_op jit(solution)/shard_map/reduce_scatter | solution.py:562
  232.7 1.9 copy-start.5
Sparse Core Ops, SparseCore 0:
  181.9 123.0 all-reduce.6
  311.0 107.8 reduce-scatter.6
  426.5 161.9 reduce-scatter.4
  596.5 205.4 reduce-scatter.10
  810.0 205.6 reduce-scatter.8

commit v2 on v1

--- a/solution.py
+++ b/solution.py
@@ -504,6 +504,411 @@
         name="cross_block",
     )(cls, cot, place, keys, jnp.tile(keys.reshape(1, rows), (1, 2)), table, w_qkv, w_out, w_up, w_down, bias, gain, bup)
 
+RING = 4
+CROSS_UNITS = 3
+SEG_UNITS = 12
+UNITS = CROSS_UNITS + SEG_UNITS
+PAIRS = (UNITS + 1) // 2
+AHEAD = 4
+PART = 48
+
+
+def add_low(a, b):
+    return (a.astype(F32) + b.astype(F32)).astype(BF16)
+
+
+def total_kernel(
+    firstt, ginner, hiddent, gsecond, mixedt, gbranch, xt, gqkv,
+    cfirstt, cginner, chiddent, cgsecond, cmixedt, cgbranch, cxt, cgqkv,
+    sums, bsums, csums, cbsums, gpos,
+    dqkv_ref, dout_ref, dup_ref, ddown_ref, small_ref,
+    aslot, bslot, csend, crecv, keep, r1, r2, r3, rf, acc, racc,
+    load_sems, csend_sems, crecv_sems, s1_sems, q1_sems, s2_sems, q2_sems, s3_sems, q3_sems, sf_sems, qf_sems, sa_sems, qa_sems,
+    *, share,
+):
+    width = bslot.shape[-1]
+    line, z = lax.axis_index("row"), lax.axis_index("seg")
+    y, x, c = line // 4, (line // 2) % 2, line % 2
+    zh, zl = z // 2, z % 2
+    flip_c = (y * 4 + x * 2 + 1 - c, z)
+    flip_x = (y * 4 + (1 - x) * 2 + c, z)
+    flip_y = ((1 - y) * 4 + x * 2 + c, z)
+    flip_zl = (line, zh * 2 + 1 - zl)
+    flip_zh = (line, (1 - zh) * 2 + zl)
+    flip_yzh = ((1 - y) * 4 + x * 2 + c, (1 - zh) * 2 + zl)
+    barrier = pltpu.get_barrier_semaphore()
+    for peer in (flip_c, flip_x, flip_y, flip_zl, flip_zh, flip_yzh):
+        pl.semaphore_signal(barrier, inc=1, device_id=peer, device_id_type=MESH)
+
+    def load(u, do):
+        slot = u % 2
+        a_sem, b_sem = load_sems.at[slot, 0], load_sems.at[slot, 1]
+
+        def pair(a, b):
+            for copy in (pltpu.make_async_copy(a, aslot.at[slot], a_sem), pltpu.make_async_copy(b, bslot.at[slot], b_sem)):
+                getattr(copy, do)()
+
+        def columns(ref, j):
+            return ref.at[:, pl.ds(pl.multiple_of(j * width, width), width)]
+
+        @pl.when(u < 4)
+        def _():
+            pair(firstt, columns(ginner, u))
+
+        @pl.when((u >= 4) & (u < 8))
+        def _():
+            pair(hiddent.at[:, :, :, u - 4], gsecond)
+
+        @pl.when(u == 8)
+        def _():
+            pair(mixedt, gbranch)
+
+        @pl.when(u >= 9)
+        def _():
+            pair(xt, columns(gqkv, u - 9))
+
+    load(0, "start")
+
+    def remote(src, dst, send_sem, recv_sem, peer):
+        return pltpu.make_async_remote_copy(
+            src_ref=src, dst_ref=dst, send_sem=send_sem, recv_sem=recv_sem, device_id=peer, device_id_type=MESH
+        )
+
+    def choose(t, a, b):
+        return t * a + (1 - t) * b
+
+    def pick(t, a, b):
+        return tuple(choose(t, p, q) for p, q in zip(a, b))
+
+    def way(t):
+        bits = (choose(t, x, y), choose(t, zl, x), choose(t, zh, zl))
+        peers = (pick(t, flip_x, flip_y), pick(t, flip_zl, flip_x), pick(t, flip_zh, flip_zl))
+        return bits, peers
+
+    def core_copy(n):
+        slot = n % RING
+        return remote(csend.at[slot], crecv.at[slot], csend_sems.at[slot], crecv_sems.at[slot], flip_c)
+
+    def copy_one(n, t):
+        (b1, _, _), (peer, _, _) = way(t)
+        return remote(keep.at[n, pl.ds(4 * (1 - b1), 4)], r1.at[n], s1_sems.at[n], q1_sems.at[n], peer)
+
+    def copy_two(n, t):
+        (b1, b2, _), (_, peer, _) = way(t)
+        return remote(keep.at[n, pl.ds(4 * b1 + 2 * (1 - b2), 2)], r2.at[n], s2_sems.at[n], q2_sems.at[n], peer)
+
+    def copy_three(n, t):
+        (b1, b2, b3), (_, _, peer) = way(t)
+        return remote(keep.at[n, 4 * b1 + 2 * b2 + 1 - b3], r3.at[n], s3_sems.at[n], q3_sems.at[n], peer)
+
+    def own_block(n, t):
+        (b1, b2, b3), _ = way(t)
+        return keep.at[n, 4 * b1 + 2 * b2 + b3]
+
+    def step_one(n, t):
+        core_copy(n).wait_recv()
+        keep[n] = add_low(keep[n], crecv[n % RING])
+
+        @pl.when(jnp.asarray(n) < AHEAD)
+        def _():
+            copy_one(n, t).start()
+
+    def step_two(n, t):
+        (b1, _, _), _ = way(t)
+        copy_one(n, t).wait()
+        at = pl.ds(4 * b1, 4)
+        keep[n, at] = add_low(keep[n, at], r1[n])
+        copy_two(n, t).start()
+
+    def step_three(n, t):
+        (b1, b2, _), _ = way(t)
+        copy_two(n, t).wait()
+        at = pl.ds(4 * b1 + 2 * b2, 2)
+        keep[n, at] = add_low(keep[n, at], r2[n])
+        copy_three(n, t).start()
+
+    def final_to(n, t, slot, peer):
+        return remote(own_block(n, t), rf.at[n, slot], sf_sems.at[n], qf_sems.at[n, slot], peer)
+
+    def sends_final(n, t, act):
+        straight = (y == 1) & ((t == 1) | (zh == 1))
+
+        @pl.when(straight)
+        def _():
+            act(final_to(n, t, 0, flip_y))
+
+        @pl.when((t == 0) & (y == 0) & (zh == 1))
+        def _():
+            act(final_to(n, t, 0, flip_zh))
+
+        @pl.when((t == 0) & (y == 1) & (zh == 0))
+        def _():
+            act(final_to(n, t, 1, flip_yzh))
+
+    def step_final(n, t):
+        copy_three(n, t).wait()
+        (b1, b2, b3), _ = way(t)
+        at = 4 * b1 + 2 * b2 + b3
+        keep[n, at] = add_low(keep[n, at], r3[n])
+        sends_final(n, t, lambda copy: copy.start())
+
+    def put(u, value):
+        def columns(j):
+            return pl.ds(pl.multiple_of(j * width, width), width)
+
+        @pl.when(u < 4)
+        def _():
+            dup_ref[:, columns(u)] = value
+
+        @pl.when((u >= 4) & (u < 8))
+        def _():
+            ddown_ref[pl.ds(pl.multiple_of((u - 4) * PART, PART), PART), :] = value
+
+        @pl.when(u == 8)
+        def _():
+            dout_ref[...] = value
+
+        @pl.when(u >= 9)
+        def _():
+            dqkv_ref[:, columns(u - 9)] = value
+
+    def step_out(n, t, u):
+        sends_final(n, t, lambda copy: copy.wait_send())
+
+        @pl.when(y == 0)
+        def _():
+            final_to(n, t, 0, flip_y).wait_recv()
+
+            @pl.when((t == 1) | (zh == 0))
+            def _():
+                put(u, own_block(n, t)[...].astype(F32) + rf[n, 0].astype(F32))
+
+            @pl.when((t == 0) & (zh == 1))
+            def _():
+                final_to(n, t, 1, flip_y).wait_recv()
+                put(u, rf[n, 0].astype(F32) + rf[n, 1].astype(F32))
+
+    def cross_final(n):
+        return remote(keep.at[n, pl.ds(2 * x, 2)], rf.at[n], sf_sems.at[n], qf_sems.at[n, 0], flip_y)
+
+    def cross_step_final(n):
+        copy_two(n, 0).wait()
+        at = pl.ds(4 * y + 2 * x, 2)
+        keep[n, at] = add_low(keep[n, at], r2[n])
+
+        @pl.when(y == 0)
+        def _():
+            cross_final(n).start()
+
+    def cross_step_out(n, index):
+        @pl.when(y == 0)
+        def _():
+            cross_final(n).wait_send()
+
+        @pl.when(y == 1)
+        def _():
+            cross_final(n).wait_recv()
+            for sub in range(4):
+                block = rf[n, sub] if sub < 2 else keep[n, 4 + 2 * x + sub - 2]
+                put(4 * index + sub, block.astype(F32))
+
+    small_peers = (flip_c, flip_x, flip_y, flip_zl, flip_zh)
+
+    def small_copy(d):
+        return remote(acc.at[d], racc.at[d], sa_sems.at[d], qa_sems.at[d], small_peers[d])
+
+    def small_step(d):
+        small_copy(d).wait()
+        acc[d + 1] = acc[d] + racc[d]
+        if d + 1 < len(small_peers):
+            small_copy(d + 1).start()
+        else:
+            small_ref[...] = acc[d + 1]
+
+    seg_rows = [jnp.sum(sums[i], axis=0, keepdims=True) for i in range(8)]
+    seg_up = jnp.sum(bsums[...], axis=0, keepdims=True)
+    order = (6, 7, 5, 4, 2, 1)
+    for i, row in enumerate(order):
+        acc[0, i : i + 1, :] = seg_rows[row]
+        acc[0, 6 + i : 7 + i, :] = csums[row : row + 1, :] * share
+    for i, row in enumerate((3, 0)):
+        acc[0, 12 + i : 13 + i, :] = seg_rows[row]
+        acc[0, 14 + i : 15 + i, :] = csums[row : row + 1, :] * share
+    for i in range(4):
+        acc[0, 16 + i : 17 + i, :] = seg_up[:, i * width : (i + 1) * width]
+        acc[0, 20 + i : 21 + i, :] = cbsums[:, i * width : (i + 1) * width] * share
+    acc[0, 24:32, :] = gpos[...] * share
+
+    def cross_unit(n, parts):
+        if n >= RING:
+            core_copy(n).wait_send()
+        for rel in (1, 0):
+            core = c if rel == 0 else 1 - c
+            for sub, (left, right) in enumerate(parts):
+                for far in range(2):
+                    value = mm(left(far, core), right).astype(BF16)
+                    at = (sub // 2) * 4 + far * 2 + sub % 2
+                    if rel == 1:
+                        csend[n % RING, at] = value
+                    else:
+                        keep[n, at] = value
+            if rel == 1:
+                if n == 0:
+                    pl.semaphore_wait(barrier, 6)
+                    small_copy(0).start()
+                core_copy(n).start()
+
+    def plain(ref):
+        return lambda far, core: ref[far, core, z]
+
+    def nested(ref, j):
+        return lambda far, core: ref[far, core, z, j]
+
+    def cut(ref, j):
+        return ref[:, j * width : (j + 1) * width]
+
+    cross_parts = (
+        lambda: [(plain(cfirstt), cut(cginner, j)) for j in range(4)],
+        lambda: [(nested(chiddent, j), cgsecond[...]) for j in range(4)],
+        lambda: [(plain(cmixedt), cgbranch[...])] + [(plain(cxt), cut(cgqkv, j)) for j in range(3)],
+    )
+
+    def compute(u):
+        n = u + CROSS_UNITS - jnp.maximum(CROSS_UNITS - 1 - u, 0)
+        t = n % 2
+        for i in range(CROSS_UNITS):
+            @pl.when(u == i)
+            def _(i=i):
+                cross_unit(2 * i, cross_parts[i]())
+                if i > 0:
+                    step_one(2 * i - 1, 1)
+
+        load(u, "wait")
+
+        @pl.when(u + 1 < SEG_UNITS)
+        def _():
+            load(u + 1, "start")
+
+        @pl.when(n >= RING)
+        def _():
+            core_copy(n).wait_send()
+
+        right = bslot[u % 2]
+        for rel in (1, 0):
+            core = c if rel == 0 else 1 - c
+            left = aslot[u % 2, :, core].reshape(8 * PART, -1)
+            value = mm(left, right).astype(BF16)
+            for far in range(2):
+                for part in range(4):
+                    block = value[(far * 4 + part) * PART : (far * 4 + part + 1) * PART]
+                    at = choose(t, far * 4 + (part % 2) * 2 + part // 2, (part // 2) * 4 + far * 2 + part % 2)
+                    if rel == 1:
+                        csend[n % RING, at] = block
+                    else:
+                        keep[n, at] = block
+            if rel == 1:
+                core_copy(n).start()
+        step_one(n - 1, (n - 1) % 2)
+
+    def step(u, carry):
+        @pl.when(u < SEG_UNITS)
+        def _():
+            compute(u)
+
+        @pl.when(u == SEG_UNITS)
+        def _():
+            step_one(UNITS - 1, (UNITS - 1) % 2)
+
+        for d in range(len(small_peers)):
+            @pl.when(u == 2 * d + 1)
+            def _(d=d):
+                small_step(d)
+
+        def on_pair(p, even, odd, cross):
+            @pl.when((p >= 0) & (p < CROSS_UNITS))
+            def _():
+                cross(2 * p)
+
+            @pl.when((p >= CROSS_UNITS) & (p < PAIRS))
+            def _():
+                even(2 * p)
+
+            @pl.when((p >= 0) & (p < PAIRS - 1))
+            def _():
+                odd(2 * p + 1)
+
+        @pl.when(u % 2 == 1)
+        def _():
+            p = u // 2 - 1
+            on_pair(
+                p - 3,
+                lambda n: step_out(n, 0, 2 * (p - 3) - CROSS_UNITS),
+                lambda n: step_out(n, 1, p - 3 + jnp.maximum(p - 3 - CROSS_UNITS + 1, 0)),
+                lambda n: None,
+            )
+            on_pair(p - 2, lambda n: step_final(n, 0), lambda n: step_final(n, 1), lambda n: cross_step_out(n, p - 2))
+            on_pair(p - 1, lambda n: step_three(n, 0), lambda n: step_three(n, 1), lambda n: cross_step_final(n))
+            on_pair(p, lambda n: step_two(n, 0), lambda n: step_two(n, 1), lambda n: step_two(n, 0))
+            q = p + AHEAD // 2
+
+            @pl.when((q >= AHEAD // 2) & (q < PAIRS))
+            def _():
+                copy_one(2 * q, 0).start()
+
+            @pl.when((q >= AHEAD // 2) & (q < PAIRS - 1))
+            def _():
+                copy_one(2 * q + 1, 1).start()
+
+        return carry
+
+    lax.fori_loop(0, 2 * PAIRS + 8, step, 0)
+    for n in range(UNITS - RING, UNITS):
+        core_copy(n).wait_send()
+
+
+def total_grads(big, cross, small, share):
+    firstt, ginner, hiddent, gsecond, mixedt, gbranch, xt, gqkv = big
+    cfirstt, cginner, chiddent, cgsecond, cmixedt, cgbranch, cxt, cgqkv = cross
+    width, depth = firstt.shape
+    inners = ginner.shape[1]
+    rows = cfirstt.shape[1]
+    assert width == 16 * PART and inners == 4 * width
+
+    def blocks(a, n):
+        return a.reshape((2, 2, 4) + ((n,) if n > 1 else ()) + (PART, a.shape[1]))
+
+    operands = [
+        blocks(firstt, 1), ginner, blocks(hiddent, 4), gsecond, blocks(mixedt, 1), gbranch, blocks(xt, 1), gqkv,
+        blocks(cfirstt, 1), cginner, blocks(chiddent, 4), cgsecond, blocks(cmixedt, 1), cgbranch, blocks(cxt, 1), cgqkv, *small,
+    ]
+    vmem = pl.BlockSpec(memory_space=pltpu.VMEM)
+    any_spec = pl.BlockSpec(memory_space=pl.ANY)
+    outs = [(PART, 3 * width), (PART, width), (PART, inners), (4 * PART, width), (32, width)]
+    dma = pltpu.SemaphoreType.DMA
+    return pl.pallas_call(
+        functools.partial(total_kernel, share=share),
+        in_specs=[any_spec] * 8 + [vmem] * (len(operands) - 8),
+        out_specs=[vmem] * len(outs),
+        out_shape=[jax.ShapeDtypeStruct(o, F32) for o in outs],
+        scratch_shapes=[
+            pltpu.VMEM((2, 2, 2, 4, PART, depth), BF16),
+            pltpu.VMEM((2, depth, width), BF16),
+            pltpu.VMEM((RING, 8, PART, width), BF16),
+            pltpu.VMEM((RING, 8, PART, width), BF16),
+            pltpu.VMEM((UNITS, 8, PART, width), BF16),
+            pltpu.VMEM((UNITS, 4, PART, width), BF16),
+            pltpu.VMEM((UNITS, 2, PART, width), BF16),
+            pltpu.VMEM((UNITS, PART, width), BF16),
+            pltpu.VMEM((UNITS, 2, PART, width), BF16),
+            pltpu.VMEM((6, 32, width), F32),
+            pltpu.VMEM((5, 32, width), F32),
+            dma((2, 2)), dma((RING,)), dma((RING,)), dma((UNITS,)), dma((UNITS,)), dma((UNITS,)), dma((UNITS,)),
+            dma((UNITS,)), dma((UNITS,)), dma((UNITS,)), dma((UNITS, 2)), dma((5,)), dma((5,)),
+        ],
+        compiler_params=pltpu.CompilerParams(vmem_limit_bytes=60 * 2**20, collective_id=1, has_side_effects=True),
+        name="total_grads",
+    )(*operands)
+
 def small_grads(sums, bsums, csums, cbsums, gpos, cross_share):
     seg_rows = jnp.sum(sums, axis=1)
     cross_rows = csums * cross_share
@@ -525,7 +930,6 @@
     total = row_count * local_length
     own = row_count * seg_here
     me = lax.axis_index("seg")
-    axes = ("row", "seg")
 
     seg_place = jnp.arange(segments)
     same_doc = doc_ids[:, :, None] == doc_ids[:, None, :]
@@ -548,19 +952,38 @@
     output, gsecond, ginner, gbranch, gqkv, gx, sums, bsums = backward_block(
         gcls, ccls, cot, y, n2, r2, slope, n1, r1, qkv, probs, w_qkv, w_out, w_up, w_down, gains[0]
     )
-    small = small_grads(sums, bsums, csums, cbsums, gpos, 1.0 / planes)
-    small = [lax.psum_scatter(part, axes, scatter_dimension=0, tiled=True) for part in small]
+    seg_pairs = (firstt, ginner, hiddent, gsecond, mixedt, gbranch, xt, gqkv)
+    cross_pairs = (cfirstt, cginner, chiddent, cgsecond, cmixedt, cgbranch, cxt, cgqkv)
+    if (lines, planes) == (8, 4) and width == 16 * PART:
+        *big, small = total_grads(seg_pairs, cross_pairs, (sums, bsums, csums, cbsums, gpos), 1.0 / planes)
+        small = small.reshape(-1)
+        index = lax.axis_index("row") * planes + me
+        shards, start = [], 0
+        for size in (12 * width, 4 * width, 8 * width, segments * width):
+            count = size // (lines * planes)
+            shards.append(lax.dynamic_slice_in_dim(small, start + index * count, count, 0))
+            start += size
+    else:
+        big, shards = generic_total(seg_pairs, cross_pairs, (sums, bsums, csums, cbsums, gpos), planes, own)
+    return (output.reshape(tokens.shape), gx.reshape(tokens.shape), *big, *shards)
+
+
+def generic_total(seg_pairs, cross_pairs, small, planes, own):
+    axes = ("row", "seg")
+    me = lax.axis_index("seg")
+    shards = [
+        lax.psum_scatter(part, axes, scatter_dimension=0, tiled=True) for part in small_grads(*small, 1.0 / planes)
+    ]
 
     def mine(values, dim):
         return lax.dynamic_slice_in_dim(values, me * own, own, dim)
 
     big = []
-    for seg_a, seg_b, cross_a, cross_b in (
-        (xt, gqkv, cxt, cgqkv), (mixedt, gbranch, cmixedt, cgbranch), (firstt, ginner, cfirstt, cginner), (hiddent, gsecond, chiddent, cgsecond)
-    ):
-        both = jnp.concatenate([mm(seg_a, seg_b), mm(mine(cross_a, 1), mine(cross_b, 0))], axis=0)
+    for at in (6, 4, 0, 2):
+        cross = mm(mine(cross_pairs[at], 1), mine(cross_pairs[at + 1], 0))
+        both = jnp.concatenate([mm(seg_pairs[at], seg_pairs[at + 1]), cross], axis=0)
         big.append(lax.psum_scatter(both, axes, scatter_dimension=0, tiled=True))
-    return (output.reshape(tokens.shape), gx.reshape(tokens.shape), *big, *small)
+    return big, shards
 
 
 def solution(mesh):

time: 1030 us -> 286 us (0.28)
  waiting for transfers between devices: 756 us -> 0 us
  Pallas kernels: 157 us -> 259 us
  matrix products: 45.2 us -> 0 us
  other arithmetic: 29.3 us -> 0.37 us
  between operations: 14.3 us -> 0.75 us
    reduce_scatter x4 -> x0, waiting for transfers between devices: 706 us -> none  [per_device(): big.append(lax.psum_scatter(both, axes, scatter_dimension=0, tiled=True))]
    pallas_call x0 -> x1, Pallas kernels: none -> 102 us  [total_grads(): pl.pallas_call(functools.partial(total_kernel, share=share), in_specs=[an...]
    unnamed x6 -> x0, waiting for transfers between devices: 50.5 us -> none
    dot_general x8 -> x0, matrix products: 45.2 us -> none  [mm(): lax.dot_general(a, b, (((1,), (0,)), ((), ())), preferred_element_type=F32)]
    concatenate x4 -> x0, other arithmetic: 25.5 us -> none  [per_device(): jnp.concatenate([mm(seg_a, seg_b), mm(mine(cross_a, 1), mine(cross_b, 0))...]
  transfers between devices with their start and end apart: 5 -> 0, of which waited for: 5 -> 0; matrix products, arithmetic and copies ran while one was open for 7% -> 0% of each run, Pallas kernels for 0% -> 0%
where the time goes in v2:
time: 286 us
  Pallas kernels  259 us (91%)
  local copies, waits for them, and re-layouts  25.3 us (9%)
    pallas_call x1, Pallas kernels, total_grads(): pl.pallas_call(functools.partial(total_kernel, share=share), in_specs=[an...  102 us
    pallas_call x1, Pallas kernels, backward_block(): pl.pallas_call(functools.partial(backward_kernel, ff_chunk=ff_chunk), gri...  72 us
    pallas_call x1, Pallas kernels, forward_block(): pl.pallas_call(functools.partial(forward_kernel, ff_chunk=ff_chunk), grid...  63.8 us
    pallas_call x1, Pallas kernels, cross_block(): pl.pallas_call(functools.partial(cross_kernel, ff_chunk=ff_chunk, devices...  21.3 us
    unnamed x38, local copies, waits for them, and re-layouts  16.8 us

profile of v2, /device:TPU:0, one launch (start us, length us, event | category | flops | bytes accessed | tf_op | source)
XLA Modules:
  0.0 285.8 jit_solution(17927612102982503067)
XLA Ops:
  0.6 0.8 fusion.1
  1.5 0.6 copy_bitcast_fusion.1
  2.1 1.3 slice_bitcast_fusion
  3.4 1.4 fusion.2
  4.8 0.0 copy-start.15
  4.8 0.0 copy-start.13
  4.8 63.8 %segment_forward.1 = (bf16[2048,2304]{1,0:T(8,128)(2,1)}, bf16[16,6,128,256]{3,2,1,0:T(8,128)(2,1)}, bf16[2048,768]{1,0:T(8,128)(2,1)}, f32[2048,128]{1,0:T(8,12...) custom-call(bf16[2048,768]{1,0:T(8,128)(2,1)} %bitcast.38, ...), custom_call_target="tpu_custom_call" | custom-call | tf_op jit(solution)/shard_map/segment_forward/pallas_call | solution.py:166
  68.5 0.0 copy-done.15
  68.6 0.1 copy.42
  68.6 0.1 copy.43
  68.7 0.1 reshape.113.keycol_ref
  68.8 0.1 tile.10
  68.9 0.1 tile.12.keyrow_ref
  69.0 1.0 slice.29
  70.0 0.3 select_reduce_fusion
  70.3 0.1 copy.40
  70.3 0.1 subtract_bitcast_fusion
  70.4 0.1 copy.41
  70.5 0.1 reshape.112.place_ref
  70.6 0.0 copy-done.13
  70.6 0.0 copy-start.8
  70.6 0.8 copy-done.8
  71.4 21.3 %cross_block.1 = (f32[16,768]{1,0:T(8,128)S(1)}, f32[16,768]{1,0:T(8,128)S(1)}, f32[8,768]{1,0:T(8,128)S(1)}, f32[1,3072]{1,0:T(1,128)S(1)}, f32[8,768]{1,0:T(8,...) custom-call(f32[16,768]{1,0:T(8,128)S(1)} %copy-done.8, ...), custom_call_target="tpu_custom_call" | custom-call | tf_op jit(solution)/shard_map/cross_block/pallas_call | solution.py:482
  92.7 0.0 copy-start
  92.7 0.9 copy-done
  93.6 0.0 copy-start.1
  93.6 0.7 copy-done.1
  94.4 0.0 copy-start.2
  94.4 0.7 copy-done.2
  95.1 0.0 copy-start.3
  95.1 0.7 copy-done.3
  95.8 0.0 copy-start.4
  95.8 0.7 copy-done.4
  96.4 0.0 copy-start.5
  96.4 0.7 copy-done.5
  97.1 0.0 copy-start.6
  97.1 0.6 copy-done.6
  97.7 0.0 copy-start.7
  97.7 0.6 copy-done.7
  98.4 0.0 copy-start.9
  98.4 0.6 copy-done.9
  99.0 0.0 copy-start.10
  99.0 0.6 copy-done.10
  99.6 0.0 copy-start.11
  99.6 0.6 copy-done.11
  100.2 0.0 copy-start.12
  100.2 0.6 copy-done.12
  100.8 0.0 copy-start.14
  100.8 0.6 copy-done.14
  101.4 72.0 %segment_backward.1 = (bf16[2048,768]{1,0:T(8,128)(2,1)}, bf16[2048,768]{1,0:T(8,128)(2,1)}, bf16[2048,3072]{1,0:T(8,128)(2,1)}, bf16[2048,768]{1,0:T(8,128)(2,1...) custom-call(f32[16,768]{1,0:T(8,128)} %copy-done.10, ...), custom_call_target="tpu_custom_call" | custom-call | tf_op jit(solution)/shard_map/segment_backward/pallas_call | solution.py:309
  173.5 102.4 %total_grads.1 = (f32[48,2304]{1,0:T(8,128)}, f32[48,768]{1,0:T(8,128)}, f32[48,3072]{1,0:T(8,128)}, f32[192,768]{1,0:T(8,128)}, f32[32,768]{1,0:T(8,128)}) custom-call(bf16[2,2,4,48,2048]{4,3,2,1,0:T(8,128)(2,1)} %bitcast.41, bf16[2048,3072]{1,0:T(8,128)(2,1)} %get-tuple-element.63.ginner, bf16[2,2,4,4,48,2048]{5,4,3,2,1,0:T(8,128)(2,1)} %bitcast.35, ...), custom_call_target="tpu_custom_call" | custom-call | tf_op jit(solution)/shard_map/total_grads/pallas_call | solution.py:888
  275.8 0.9 reshape.111
  276.7 0.6 fusion
  277.4 0.7 dynamic_slice.12
  278.0 0.6 dynamic_slice.13
  278.6 1.8 copy.59
  280.4 1.6 copy.60
  282.0 1.9 copy.61
  283.9 1.9 copy.62
  (5 shorter events, 0.0 us)
Async XLA Ops:
  4.8 63.8 %copy-start.15 = (s32[8,8]{1,0:T(8,128)S(1)}, s32[8,8]{1,0:T(8,128)}, u32[]{:S(2)}) copy-start(s32[8,8]{1,0:T(8,128)} %param.12) | copy-start | bytes 772
  4.8 65.8 %copy-start.13 = (bf16[8,768]{1,0:T(8,128)(2,1)S(1)}, bf16[8,768]{1,0:T(8,128)(2,1)}, u32[]{:S(2)}) copy-start(bf16[8,768]{1,0:T(8,128)(2,1)} %table_ref.1) | copy-start | bytes 36868
  70.6 0.8 copy-start.8
  92.7 0.9 copy-start
  93.6 0.7 copy-start.1
  94.4 0.7 copy-start.2
  95.1 0.7 copy-start.3
  95.8 0.7 copy-start.4
  96.4 0.7 copy-start.5
  97.1 0.6 copy-start.6
  97.7 0.6 copy-start.7
  98.4 0.6 copy-start.9
  99.0 0.6 copy-start.10
  99.6 0.6 copy-start.11
  100.2 0.6 copy-start.12
  100.8 0.6 copy-start.14

commit v3 on v2

--- a/solution.py
+++ b/solution.py
@@ -11,6 +11,7 @@
 HDIM = 64
 SEGLEN = 128
 LANES = 128
+GROUP = 2 * LANES
 EPSILON = 1e-05
 GELU_A = 0.7978845608028654
 GELU_B = 0.044715 * GELU_A
@@ -37,6 +38,10 @@
     keep = low_lanes(pair.shape)
     zero = jnp.zeros_like(pair)
     return jnp.concatenate([jnp.where(keep, pair, zero), jnp.where(keep, zero, pair)], axis=0)
+
+
+def pair_lanes(half):
+    return [slice(part * GROUP + half * LANES, part * GROUP + (half + 1) * LANES) for part in range(3)]
 
 
 def norm_stats(values):
@@ -75,8 +80,9 @@
         copies[0].wait()
 
     rows, width = x_ref.shape
-    bias = bias_ref[...].astype(F32)
-    gain = gain_ref[...].astype(F32)
+    bias = bias_ref[0].astype(F32)
+    gain = gain_ref[0].astype(F32)
+    up_bias = bup_ref[0:1, :].astype(F32)
     x = x_ref[...]
     xt_ref[...] = x.T
     for part in range(3):
@@ -86,13 +92,13 @@
             out = out + bias[0:1]
         if part == 2:
             out = out + bias[1:2]
-        qkv_ref[:, cols] = out.astype(BF16)
+        out = out.astype(BF16)
+        for group in range(width // GROUP):
+            qkv_ref[group, :, part * GROUP : (part + 1) * GROUP] = out[:, group * GROUP : (group + 1) * GROUP]
     for seg in range(rows // SEGLEN):
         at = slice(seg * SEGLEN, (seg + 1) * SEGLEN)
         for pair in range(width // LANES):
-            q = qkv_ref[at, pair * LANES : (pair + 1) * LANES]
-            k = qkv_ref[at, width + pair * LANES : width + (pair + 1) * LANES]
-            v = qkv_ref[at, 2 * width + pair * LANES : 2 * width + (pair + 1) * LANES]
+            q, k, v = (qkv_ref[pair // 2, at, lanes] for lanes in pair_lanes(pair % 2))
             scores = mm_nt(k, stack_heads(q * HDIM**-0.5))
             e = jnp.exp(scores - jnp.max(scores, axis=0, keepdims=True))
             p = (e * (1.0 / jnp.sum(e, axis=0, keepdims=True))).astype(BF16)
@@ -117,7 +123,7 @@
     inners = wup.shape[1]
     for c in range(inners // ff_chunk):
         cols = slice(c * ff_chunk, (c + 1) * ff_chunk)
-        inner = mm(first, wup[:, cols]) + bup_ref[:, cols].astype(F32)
+        inner = mm(first, wup[:, cols]) + up_bias[:, cols]
         hidden, slope = gelu_both(inner)
         hidden = hidden.astype(BF16)
         hiddent_ref[cols, :] = hidden.T
@@ -149,7 +155,7 @@
         return pl.BlockSpec((rows, tile), lambda i: (0, i))
 
     outs = [
-        ((total, 3 * width), BF16, rows_of(3 * width)),
+        ((width // GROUP, total, 3 * GROUP), BF16, pl.BlockSpec((width // GROUP, tile, 3 * GROUP), lambda i: (0, i, 0))),
         ((total // SEGLEN, pairs, SEGLEN, 2 * SEGLEN), BF16, pl.BlockSpec((segs, pairs, SEGLEN, 2 * SEGLEN), lambda i: (i, 0, 0, 0))),
         ((total, width), BF16, rows_of(width)),
         ((total, LANES), F32, rows_of(LANES)),
@@ -193,18 +199,13 @@
     return (scaled - a - normal * b) * rstd
 
 
-def backward_kernel(
-    gcls_ref, ccls_ref, cot_ref, y_ref, n2_ref, r2_ref, slope_ref, n1_ref, r1_ref, qkv_ref, probs_ref,
-    wqkv_hbm, wout_hbm, wup_hbm, wdown_hbm, gain_ref,
-    out_ref, gsecond_ref, ginner_ref, gbranch_ref, gqkv_ref, gx_ref, sums_ref, bsums_ref,
-    wqkv, wout, wup, wdown, sems, *, ff_chunk,
+def early_kernel(
+    gcls_ref, ccls_ref, cot_ref, y_ref, n2_ref, r2_ref, slope_ref, n1_ref, r1_ref, wup_hbm, wdown_hbm, gain_ref,
+    out_ref, gsecond_ref, ginner_ref, gbranch_ref, sums_ref, bsums_ref, wup, wdown, sems, *, ff_chunk,
 ):
     step = pl.program_id(0)
     copies = [
-        pltpu.make_async_copy(src.at[0], dst, sems.at[i])
-        for i, (src, dst) in enumerate(
-            ((wdown_hbm, wdown), (wup_hbm, wup), (wout_hbm, wout), (wqkv_hbm, wqkv))
-        )
+        pltpu.make_async_copy(src.at[0], dst, sems.at[i]) for i, (src, dst) in enumerate(((wdown_hbm, wdown), (wup_hbm, wup)))
     ]
 
     @pl.when(step == 0)
@@ -213,13 +214,13 @@
             copy.start()
         sums_ref[...] = jnp.zeros_like(sums_ref)
         bsums_ref[...] = jnp.zeros_like(bsums_ref)
-        for copy in copies[:2]:
+        for copy in copies:
             copy.wait()
 
     rows, width = cot_ref.shape
     segs = rows // SEGLEN
     inners = wup.shape[1]
-    gain = gain_ref[...].astype(F32)
+    gain = gain_ref[0].astype(F32)
     place = lax.broadcasted_iota(jnp.int32, (rows, width), 0)
     gy = cot_ref[...].astype(F32)
     y = y_ref[...].astype(F32)
@@ -246,48 +247,14 @@
     n1 = n1_ref[...].astype(F32)
     sums_ref[3] += fold_rows(g_first * n1)
     sums_ref[4] += fold_rows(g_first)
-    g_one = norm_back(g_first, gain[0:1], n1, r1_ref[:, 0:1])
-    g_branch = g_one.astype(BF16)
+    g_branch = norm_back(g_first, gain[0:1], n1, r1_ref[:, 0:1]).astype(BF16)
     gbranch_ref[...] = g_branch
     sums_ref[5] += fold_rows(g_branch.astype(F32))
 
-    @pl.when(step == 0)
-    def _():
-        for copy in copies[2:]:
-            copy.wait()
-
-    g_mixed = mm_nt(g_branch, wout[...]).astype(BF16)
-    for seg in range(segs):
-        at = slice(seg * SEGLEN, (seg + 1) * SEGLEN)
-        for pair in range(width // LANES):
-            lanes = [slice(part * width + pair * LANES, part * width + (pair + 1) * LANES) for part in range(3)]
-            q = qkv_ref[at, lanes[0]] * HDIM**-0.5
-            k = qkv_ref[at, lanes[1]]
-            v = qkv_ref[at, lanes[2]]
-            p_low = probs_ref[seg, pair]
-            p = p_low.astype(F32)
-            g_out = stack_heads(g_mixed[at, lanes[0]])
-            g_p = mm_nt(v, g_out)
-            inner_sum = jnp.sum(g_p * p, axis=0, keepdims=True)
-            g_s = (p * (g_p - inner_sum)).astype(BF16)
-            g_v = mm(p_low, g_out)
-            g_k = mm(g_s, stack_heads(q))
-            g_st = jnp.concatenate([g_s[:, :SEGLEN].T, g_s[:, SEGLEN:].T], axis=1)
-            g_q = mm(g_st, stack_heads(k)) * HDIM**-0.5
-            gqkv_ref[at, lanes[0]] = g_q.astype(BF16)
-            gqkv_ref[at, lanes[1]] = g_k.astype(BF16)
-            gqkv_ref[at, lanes[2]] = g_v.astype(BF16)
-    g_qkv = gqkv_ref[...]
-    sums_ref[6] += fold_rows(g_qkv[:, :width].astype(F32))
-    sums_ref[7] += fold_rows(g_qkv[:, 2 * width :].astype(F32))
-    gx_ref[...] = g_one + mm_nt(g_qkv, wqkv[...])
-
-
-def backward_block(gcls, ccls, cot, y, n2, r2, slope, n1, r1, qkv, probs, w_qkv, w_out, w_up, w_down, gain, tile=256, ff_chunk=768):
+
+def early_backward(gcls, ccls, cot, y, n2, r2, slope, n1, r1, w_up, w_down, gains, tile=256, ff_chunk=768):
     total, width = cot.shape
     inners = w_up.shape[-1]
-    segs = tile // SEGLEN
-    pairs = width // LANES
     any_spec = pl.BlockSpec(memory_space=pl.ANY)
 
     def rows_of(cols):
@@ -301,31 +268,22 @@
         ((total, width), BF16, rows_of(width)),
         ((total, inners), BF16, rows_of(inners)),
         ((total, width), BF16, rows_of(width)),
-        ((total, 3 * width), BF16, rows_of(3 * width)),
-        ((total, width), F32, rows_of(width)),
-        ((8, 8, width), F32, pl.BlockSpec((8, 8, width), lambda i: (0, 0, 0))),
+        ((6, 8, width), F32, pl.BlockSpec((6, 8, width), lambda i: (0, 0, 0))),
         ((8, inners), F32, pl.BlockSpec((8, inners), lambda i: (0, 0))),
     ]
     return pl.pallas_call(
-        functools.partial(backward_kernel, ff_chunk=ff_chunk),
+        functools.partial(early_kernel, ff_chunk=ff_chunk),
         grid=(total // tile,),
         in_specs=[whole(gcls), whole(ccls), rows_of(width), rows_of(width), rows_of(width), rows_of(LANES), rows_of(inners),
-                  rows_of(width), rows_of(LANES), rows_of(3 * width),
-                  pl.BlockSpec((segs, pairs, SEGLEN, 2 * SEGLEN), lambda i: (i, 0, 0, 0)),
-                  any_spec, any_spec, any_spec, any_spec, whole(gain)],
+                  rows_of(width), rows_of(LANES), any_spec, any_spec, whole(gains)],
         out_specs=[o[2] for o in outs],
         out_shape=[jax.ShapeDtypeStruct(o[0], o[1]) for o in outs],
-        scratch_shapes=[
-            pltpu.VMEM(w_qkv.shape[1:], BF16),
-            pltpu.VMEM(w_out.shape[1:], BF16),
-            pltpu.VMEM(w_up.shape[1:], BF16),
-            pltpu.VMEM(w_down.shape[1:], BF16),
-            pltpu.SemaphoreType.DMA((4,)),
-        ],
+        scratch_shapes=[pltpu.VMEM(w_up.shape[1:], BF16), pltpu.VMEM(w_down.shape[1:], BF16), pltpu.SemaphoreType.DMA((2,))],
         compiler_params=pltpu.CompilerParams(vmem_limit_bytes=60 * 2**20),
-        name="segment_backward",
-    )(gcls, ccls, cot, y, n2, r2, slope, n1, r1, qkv, probs, w_qkv, w_out, w_up, w_down, gain)
-
+        name="early_backward",
+    )(gcls, ccls, cot, y, n2, r2, slope, n1, r1, w_up, w_down, gains)
+
+OUTS = 13
 NEGATIVE = -1000000000.0
 MESH = pl.DeviceIdType.MESH
 
@@ -335,19 +293,30 @@
 
 
 def cross_kernel(
-    cls_ref, cot_ref, place_ref, keycol_ref, keyrow_ref, table_ref, wqkv_hbm, wout_hbm, wup_hbm, wdown_hbm, bias_ref, gain_ref, bup_ref,
-    ccls_ref, gcls_ref, sums_ref, bsums_ref, gpos_ref, xt_ref, mixedt_ref, firstt_ref, hiddent_ref, gqkv_ref, gbranch_ref, ginner_ref, gsecond_ref,
-    wqkv, wout, wup, wdown, packed, gathered, qkv_ref, probs_ref, mixed_ref, slope_ref, whole_ref, sems, send_sems, recv_sems, *, ff_chunk, devices,
+    cls_ref, cot_hbm, place_ref, keycol_ref, keyrow_ref, table_ref, wqkv_hbm, wout_hbm, wup_hbm, wdown_hbm, bias_ref, gain_ref, bup_ref,
+    *refs, ff_chunk, devices,
 ):
+    (
+        ccls_ref, gcls_ref, sums_ref, bsums_ref, gpos_ref, xt_ref, mixedt_ref, firstt_ref, hiddent_ref,
+        gqkv_ref, gbranch_ref, ginner_ref, gsecond_ref,
+    ) = outs = refs[OUTS : 2 * OUTS]
+    homes = refs[:OUTS]
+    (
+        wqkv, wout, wup, wdown, cot_rows, cot_low, packed, gathered, qkv_ref, probs_ref, mixed_ref, slope_ref, whole_ref, sems, out_sems, cot_sems, send_sems, recv_sems,
+    ) = refs[2 * OUTS :]
+    writes = [pltpu.make_async_copy(src, dst, out_sems.at[i]) for i, (src, dst) in enumerate(zip(outs, homes))]
     copies = [
         pltpu.make_async_copy(src.at[1], dst, sems.at[i])
         for i, (src, dst) in enumerate(
             ((wqkv_hbm, wqkv), (wout_hbm, wout), (wup_hbm, wup), (wdown_hbm, wdown))
         )
     ]
-    for copy in copies:
+    own, width = cls_ref.shape
+    cot_copies = [
+        pltpu.make_async_copy(cot_hbm.at[pl.ds(i * SEGLEN, 16)], cot_rows.at[i], cot_sems.at[i]) for i in range(own)
+    ]
+    for copy in cot_copies + copies:
         copy.start()
-    own, width = cls_ref.shape
     rows = own * devices
     inners = wup.shape[1]
     me = lax.axis_index("seg")
@@ -356,7 +325,10 @@
     for hop in range(1, devices):
         pl.semaphore_signal(barrier, inc=1, device_id=(line, lax.rem(me + hop, devices)), device_id_type=MESH)
     packed[0:own, :] = cls_ref[...].astype(BF16)
-    packed[own:, :] = cot_ref[...]
+    for i, copy in enumerate(cot_copies):
+        copy.wait()
+        cot_low[i : i + 1, :] = cot_rows[i, 0:8, :].astype(F32)[0:1]
+    packed[own:, :] = cot_low[...].astype(BF16)
     pl.semaphore_wait(barrier, devices - 1)
     sends = []
     for hop in range(1, devices):
@@ -366,8 +338,9 @@
         )
         send.start()
         sends.append(send)
-    bias = bias_ref[...].astype(F32)
-    gain = gain_ref[...].astype(F32)
+    bias = bias_ref[1].astype(F32)
+    gain = gain_ref[1].astype(F32)
+    up_bias = bup_ref[1:2, :].astype(F32)
     onehot = (place_ref[...] == lax.broadcasted_iota(jnp.int32, (rows, table_ref.shape[0]), 1)).astype(F32)
     embed = mm(onehot.astype(BF16), table_ref[...])
     allowed = keycol_ref[...] == keyrow_ref[...]
@@ -412,7 +385,7 @@
     total = first.astype(F32) + bias[4:5]
     for c in range(inners // ff_chunk):
         cols = slice(c * ff_chunk, (c + 1) * ff_chunk)
-        hidden, slope = gelu_both(mm(first, wup[:, cols]) + bup_ref[:, cols].astype(F32))
+        hidden, slope = gelu_both(mm(first, wup[:, cols]) + up_bias[:, cols])
         hidden = hidden.astype(BF16)
         hiddent_ref[cols, :] = turned(hidden)
         slope_ref[:, cols] = slope
@@ -421,6 +394,8 @@
     mine = pl.ds(pl.multiple_of(me * own, own), own)
     whole_ref[0] = (n2 * gain[1:2] + bias[5:6]).astype(BF16).astype(F32)
     ccls_ref[...] = whole_ref[0, mine, :]
+    for i in (0, 5, 6, 7, 8):
+        writes[i].start()
 
     def row_sum(values):
         return jnp.sum(values.astype(F32), axis=0, keepdims=True)
@@ -444,6 +419,8 @@
     g_branch = g_one.astype(BF16)
     gbranch_ref[...] = g_branch
     sums_ref[5:6, :] = row_sum(g_branch)
+    for i in (10, 11, 12):
+        writes[i].start()
     g_mixed = mm_nt(g_branch, wout[...]).astype(BF16)
     for pair in range(width // LANES):
         lanes = [slice(part * width + pair * LANES, part * width + (pair + 1) * LANES) for part in range(3)]
@@ -466,9 +443,13 @@
     whole_ref[1] = g_x
     gcls_ref[...] = whole_ref[1, mine, :]
     gpos_ref[...] = lax.dot_general(onehot, g_x, (((0,), (0,)), ((), ())), preferred_element_type=F32, precision=lax.Precision.HIGHEST)
-
-
-def cross_block(cls, cot, place, keys, table, w_qkv, w_out, w_up, w_down, bias, gain, bup, devices, ff_chunk=768):
+    for i in (1, 2, 3, 4, 9):
+        writes[i].start()
+    for write in writes:
+        write.wait()
+
+
+def cross_block(cls, cot, place, keys, table, w_qkv, w_out, w_up, w_down, biases, gains, b_up, devices, ff_chunk=768):
     own, width = cls.shape
     rows = own * devices
     inners = w_up.shape[-1]
@@ -481,14 +462,17 @@
     ]
     return pl.pallas_call(
         functools.partial(cross_kernel, ff_chunk=ff_chunk, devices=devices),
-        in_specs=[vmem] * 6 + [any_spec] * 4 + [vmem] * 3,
-        out_specs=[vmem] * len(outs),
+        in_specs=[vmem, any_spec] + [vmem] * 4 + [any_spec] * 4 + [vmem] * 3,
+        out_specs=[any_spec] * len(outs),
         out_shape=[jax.ShapeDtypeStruct(*o) for o in outs],
-        scratch_shapes=[
+        scratch_shapes=[pltpu.VMEM(*o) for o in outs]
+        + [
             pltpu.VMEM(w_qkv.shape[1:], BF16),
             pltpu.VMEM(w_out.shape[1:], BF16),
             pltpu.VMEM(w_up.shape[1:], BF16),
             pltpu.VMEM(w_down.shape[1:], BF16),
+            pltpu.VMEM((own, 16, width), BF16),
+            pltpu.VMEM((own, width), F32),
             pltpu.VMEM((2 * own, width), BF16),
             pltpu.VMEM((devices, 2 * own, width), BF16),
             pltpu.VMEM((rows, 3 * width), BF16),
@@ -497,33 +481,71 @@
             pltpu.VMEM((rows, inners), F32),
             pltpu.VMEM((2, rows, width), F32),
             pltpu.SemaphoreType.DMA((4,)),
+            pltpu.SemaphoreType.DMA((OUTS,)),
+            pltpu.SemaphoreType.DMA((own,)),
             pltpu.SemaphoreType.DMA((devices,)),
             pltpu.SemaphoreType.DMA((devices,)),
         ],
         compiler_params=pltpu.CompilerParams(vmem_limit_bytes=50 * 2**20, collective_id=0, has_side_effects=True),
         name="cross_block",
-    )(cls, cot, place, keys, jnp.tile(keys.reshape(1, rows), (1, 2)), table, w_qkv, w_out, w_up, w_down, bias, gain, bup)
+    )(cls, cot, place, keys, jnp.tile(keys.reshape(1, rows), (1, 2)), table, w_qkv, w_out, w_up, w_down, biases, gains, b_up)
 
 RING = 4
 CROSS_UNITS = 3
 SEG_UNITS = 12
 UNITS = CROSS_UNITS + SEG_UNITS
-PAIRS = (UNITS + 1) // 2
-AHEAD = 4
+CHAINS = UNITS + 1
 PART = 48
+GROUPS = 3
+EARLY = 9
+TILES = 4
+GROUP_STEPS = TILES + 1
+LAST_AT = EARLY + GROUPS * GROUP_STEPS
+STEPS = LAST_AT + TILES
+
+
+PAIR_MOMENTS = [(4, 6, 8, 13), (6, 8, 11, 16), (8, 11, 14, 19), (11, 14, 17, 21), (14, 17, 20, 24), (17, 20, 23, 26)]
+LATE_MOMENTS = [(14, 18, 21, 23, 26), (19, 23, 25, 27, STEPS), (24, STEPS, STEPS, STEPS, STEPS), (STEPS,) * 5]
+SMALL_MOMENTS = (1, 4, 6, 8, 10, 12)
+SMALL_LATE = (24, 25, 26, STEPS, STEPS, STEPS)
+
+
+def comm_schedule():
+    table = {s: [] for s in range(STEPS + 1)}
+    for pair, moments in enumerate(PAIR_MOMENTS):
+        for n in (2 * pair, 2 * pair + 1):
+            for action, at in zip(("two", "three", "final", "out"), moments):
+                table[at].append((action, n))
+            if n + 4 < CROSS_UNITS + EARLY:
+                table[moments[0]].append(("send", n + 4))
+    first = CROSS_UNITS + EARLY
+    table[EARLY + 1].append(("one", first - 1))
+    for n, moments in enumerate(LATE_MOMENTS, first):
+        for action, at in zip(("one", "two", "three", "final", "out"), moments):
+            if action != "one" or n < UNITS:
+                table[at].append((action, n))
+    for d in range(6):
+        table[SMALL_MOMENTS[d]].append(("small", d))
+        table[SMALL_LATE[d]].append(("late", d))
+    order = ("small", "late", "one", "out", "final", "three", "two", "send")
+    for at in range(STEPS):
+        table[at].sort(key=lambda item: (order.index(item[0]), item[1]))
+    rank = {"late": 0, "two": 1, "three": 2, "final": 3, "out": 4}
+    table[STEPS].sort(key=lambda item: (rank[item[0]] if item[0] != "late" else item[1] - 2.5, item[1]))
+    return table
 
 
 def add_low(a, b):
     return (a.astype(F32) + b.astype(F32)).astype(BF16)
 
 
-def total_kernel(
-    firstt, ginner, hiddent, gsecond, mixedt, gbranch, xt, gqkv,
+def late_kernel(
+    firstt, ginner, hiddent, gsecond, mixedt, gbranch, xt, qkv, probs, wqkv_hbm, wout_hbm,
     cfirstt, cginner, chiddent, cgsecond, cmixedt, cgbranch, cxt, cgqkv,
     sums, bsums, csums, cbsums, gpos,
-    dqkv_ref, dout_ref, dup_ref, ddown_ref, small_ref,
-    aslot, bslot, csend, crecv, keep, r1, r2, r3, rf, acc, racc,
-    load_sems, csend_sems, crecv_sems, s1_sems, q1_sems, s2_sems, q2_sems, s3_sems, q3_sems, sf_sems, qf_sems, sa_sems, qa_sems,
+    dqkv_ref, dout_ref, dup_ref, ddown_ref, small_ref, gx_ref,
+    aslot, bslot, qkv_slot, probs_slot, gbranch_slot, gx_slot, wqkv, wout, fold, csend, crecv, keep, r1, r2, r3, rf, acc, racc, late_acc, late_racc,
+    load_sems, tile_sems, store_sems, weight_sems, csend_sems, crecv_sems, s1_sems, q1_sems, s2_sems, q2_sems, s3_sems, q3_sems, sf_sems, qf_sems, sa_sems, qa_sems,
     *, share,
 ):
     width = bslot.shape[-1]
@@ -540,33 +562,97 @@
     for peer in (flip_c, flip_x, flip_y, flip_zl, flip_zh, flip_yzh):
         pl.semaphore_signal(barrier, inc=1, device_id=peer, device_id_type=MESH)
 
-    def load(u, do):
-        slot = u % 2
-        a_sem, b_sem = load_sems.at[slot, 0], load_sems.at[slot, 1]
-
-        def pair(a, b):
-            for copy in (pltpu.make_async_copy(a, aslot.at[slot], a_sem), pltpu.make_async_copy(b, bslot.at[slot], b_sem)):
-                getattr(copy, do)()
+    tile = gbranch_slot.shape[1]
+    segs = tile // SEGLEN
+
+    def a_slot(u):
+        return jnp.where((u < 4) | (u >= EARLY), 0, (u + 1) % 2)
+
+    def b_slot(u):
+        return jnp.where(u < 4, u % 2, jnp.where(u < EARLY, u // 8, u - EARLY))
+
+    def load_unit(u, do):
+        def act(src, dst, side):
+            getattr(pltpu.make_async_copy(src, dst, load_sems.at[side]), do)()
 
         def columns(ref, j):
             return ref.at[:, pl.ds(pl.multiple_of(j * width, width), width)]
 
+        @pl.when(u == 0)
+        def _():
+            act(firstt, aslot.at[0], 0)
+
         @pl.when(u < 4)
         def _():
-            pair(firstt, columns(ginner, u))
+            act(columns(ginner, u), bslot.at[u % 2], 1)
 
         @pl.when((u >= 4) & (u < 8))
         def _():
-            pair(hiddent.at[:, :, :, u - 4], gsecond)
+            act(hiddent.at[:, :, :, u - 4], aslot.at[(u + 1) % 2], 0)
+
+        @pl.when(u == 4)
+        def _():
+            act(gsecond, bslot.at[0], 1)
 
         @pl.when(u == 8)
         def _():
-            pair(mixedt, gbranch)
-
-        @pl.when(u >= 9)
-        def _():
-            pair(xt, columns(gqkv, u - 9))
-
+            act(mixedt, aslot.at[1], 0)
+            act(gbranch, bslot.at[1], 1)
+
+        @pl.when(u == EARLY)
+        def _():
+            act(xt, aslot.at[0], 0)
+
+    def tile_rows(i):
+        return pl.ds(pl.multiple_of(i * tile, tile), tile)
+
+    def load_tile(j, i, slot, late, do):
+        copies = [pltpu.make_async_copy(gbranch.at[tile_rows(i)], gbranch_slot.at[slot], tile_sems.at[slot, 0])]
+        if not late:
+            copies.append(pltpu.make_async_copy(qkv.at[j, tile_rows(i)], qkv_slot.at[slot], tile_sems.at[slot, 1]))
+            copies.append(
+                pltpu.make_async_copy(probs.at[pl.ds(i * segs, segs), pl.ds(2 * j, 2)], probs_slot.at[slot], tile_sems.at[slot, 2])
+            )
+        for copy in copies:
+            getattr(copy, do)()
+
+    def place(s):
+        group = (s - EARLY) // GROUP_STEPS
+        return group, (s - EARLY) % GROUP_STEPS
+
+    def load(s, do):
+        group, part = place(s)
+        inside = (s >= EARLY) & (s < LAST_AT)
+
+        @pl.when(s < EARLY)
+        def _():
+            load_unit(s, do)
+
+        @pl.when(inside & (part < TILES))
+        def _():
+            load_tile(group, part, part % 2, False, do)
+
+        @pl.when(inside & (part == TILES))
+        def _():
+            load_unit(EARLY + group, do)
+
+        @pl.when(s >= LAST_AT)
+        def _():
+            load_tile(0, s - LAST_AT, (s - LAST_AT) % 2, True, do)
+
+    def store_gx(i):
+        return pltpu.make_async_copy(gx_slot.at[i % 2], gx_ref.at[tile_rows(i)], store_sems.at[i % 2])
+
+    weight_copies = [pltpu.make_async_copy(wout_hbm.at[0], wout, weight_sems.at[0])]
+    for j in range(GROUPS):
+        for part in range(3):
+            weight_copies.append(
+                pltpu.make_async_copy(
+                    wqkv_hbm.at[0, :, pl.ds(part * width + j * GROUP, GROUP)],
+                    wqkv.at[j, :, pl.ds(part * GROUP, GROUP)],
+                    weight_sems.at[1 + 3 * j + part],
+                )
+            )
     load(0, "start")
 
     def remote(src, dst, send_sem, recv_sem, peer):
@@ -589,46 +675,62 @@
         slot = n % RING
         return remote(csend.at[slot], crecv.at[slot], csend_sems.at[slot], crecv_sems.at[slot], flip_c)
 
+    def part_of(n):
+        if isinstance(n, int) and n >= UNITS - 1:
+            half = width // 2
+            return UNITS - 1, slice((n - UNITS + 1) * half, (n - UNITS + 2) * half)
+        return n, slice(0, width)
+
     def copy_one(n, t):
         (b1, _, _), (peer, _, _) = way(t)
-        return remote(keep.at[n, pl.ds(4 * (1 - b1), 4)], r1.at[n], s1_sems.at[n], q1_sems.at[n], peer)
+        m, cols = part_of(n)
+        return remote(keep.at[m, pl.ds(4 * (1 - b1), 4), :, cols], r1.at[m, :, :, cols], s1_sems.at[n], q1_sems.at[n], peer)
 
     def copy_two(n, t):
         (b1, b2, _), (_, peer, _) = way(t)
-        return remote(keep.at[n, pl.ds(4 * b1 + 2 * (1 - b2), 2)], r2.at[n], s2_sems.at[n], q2_sems.at[n], peer)
+        m, cols = part_of(n)
+        return remote(keep.at[m, pl.ds(4 * b1 + 2 * (1 - b2), 2), :, cols], r2.at[m, :, :, cols], s2_sems.at[n], q2_sems.at[n], peer)
 
     def copy_three(n, t):
         (b1, b2, b3), (_, _, peer) = way(t)
-        return remote(keep.at[n, 4 * b1 + 2 * b2 + 1 - b3], r3.at[n], s3_sems.at[n], q3_sems.at[n], peer)
+        m, cols = part_of(n)
+        return remote(keep.at[m, 4 * b1 + 2 * b2 + 1 - b3, :, cols], r3.at[m, :, cols], s3_sems.at[n], q3_sems.at[n], peer)
 
     def own_block(n, t):
         (b1, b2, b3), _ = way(t)
-        return keep.at[n, 4 * b1 + 2 * b2 + b3]
+        m, cols = part_of(n)
+        return keep.at[m, 4 * b1 + 2 * b2 + b3, :, cols]
 
     def step_one(n, t):
         core_copy(n).wait_recv()
         keep[n] = add_low(keep[n], crecv[n % RING])
 
-        @pl.when(jnp.asarray(n) < AHEAD)
+        @pl.when((n < 4) | (n >= CROSS_UNITS + EARLY))
         def _():
             copy_one(n, t).start()
+
+        if isinstance(n, int) and n == UNITS - 1:
+            copy_one(n + 1, 1).start()
 
     def step_two(n, t):
         (b1, _, _), _ = way(t)
         copy_one(n, t).wait()
+        m, cols = part_of(n)
         at = pl.ds(4 * b1, 4)
-        keep[n, at] = add_low(keep[n, at], r1[n])
+        keep[m, at, :, cols] = add_low(keep[m, at, :, cols], r1[m, :, :, cols])
         copy_two(n, t).start()
 
     def step_three(n, t):
         (b1, b2, _), _ = way(t)
         copy_two(n, t).wait()
+        m, cols = part_of(n)
         at = pl.ds(4 * b1 + 2 * b2, 2)
-        keep[n, at] = add_low(keep[n, at], r2[n])
+        keep[m, at, :, cols] = add_low(keep[m, at, :, cols], r2[m, :, :, cols])
         copy_three(n, t).start()
 
     def final_to(n, t, slot, peer):
-        return remote(own_block(n, t), rf.at[n, slot], sf_sems.at[n], qf_sems.at[n, slot], peer)
+        m, cols = part_of(n)
+        return remote(own_block(n, t), rf.at[m, slot, :, cols], sf_sems.at[n], qf_sems.at[n, slot], peer)
 
     def sends_final(n, t, act):
         straight = (y == 1) & ((t == 1) | (zh == 1))
@@ -648,11 +750,12 @@
     def step_final(n, t):
         copy_three(n, t).wait()
         (b1, b2, b3), _ = way(t)
+        m, cols = part_of(n)
         at = 4 * b1 + 2 * b2 + b3
-        keep[n, at] = add_low(keep[n, at], r3[n])
+        keep[m, at, :, cols] = add_low(keep[m, at, :, cols], r3[m, :, cols])
         sends_final(n, t, lambda copy: copy.start())
 
-    def put(u, value):
+    def put(u, value, cols=slice(0, 16 * PART)):
         def columns(j):
             return pl.ds(pl.multiple_of(j * width, width), width)
 
@@ -668,11 +771,17 @@
         def _():
             dout_ref[...] = value
 
-        @pl.when(u >= 9)
-        def _():
-            dqkv_ref[:, columns(u - 9)] = value
+        for j in range(GROUPS):
+            @pl.when(u == EARLY + j)
+            def _(j=j):
+                for part in range(3):
+                    first, last = max(part * GROUP, cols.start), min((part + 1) * GROUP, cols.stop)
+                    if first < last:
+                        to = part * (width - GROUP) + j * GROUP
+                        dqkv_ref[:, to + first : to + last] = value[:, first - cols.start : last - cols.start]
 
     def step_out(n, t, u):
+        m, cols = part_of(n)
         sends_final(n, t, lambda copy: copy.wait_send())
 
         @pl.when(y == 0)
@@ -681,12 +790,12 @@
 
             @pl.when((t == 1) | (zh == 0))
             def _():
-                put(u, own_block(n, t)[...].astype(F32) + rf[n, 0].astype(F32))
+                put(u, own_block(n, t)[...].astype(F32) + rf[m, 0, :, cols].astype(F32), cols)
 
             @pl.when((t == 0) & (zh == 1))
             def _():
                 final_to(n, t, 1, flip_y).wait_recv()
-                put(u, rf[n, 0].astype(F32) + rf[n, 1].astype(F32))
+                put(u, rf[m, 0, :, cols].astype(F32) + rf[m, 1, :, cols].astype(F32), cols)
 
     def cross_final(n):
         return remote(keep.at[n, pl.ds(2 * x, 2)], rf.at[n], sf_sems.at[n], qf_sems.at[n, 0], flip_y)
@@ -714,22 +823,28 @@
 
     small_peers = (flip_c, flip_x, flip_y, flip_zl, flip_zh)
 
-    def small_copy(d):
-        return remote(acc.at[d], racc.at[d], sa_sems.at[d], qa_sems.at[d], small_peers[d])
-
-    def small_step(d):
-        small_copy(d).wait()
-        acc[d + 1] = acc[d] + racc[d]
+    rounds = ((acc, racc), (late_acc, late_racc))
+
+    def small_copy(late, d):
+        own, other = rounds[late]
+        return remote(own.at[d], other.at[d], sa_sems.at[late, d], qa_sems.at[late, d], small_peers[d])
+
+    def small_step(late, d):
+        own, other = rounds[late]
+        small_copy(late, d).wait()
+        own[d + 1] = own[d] + other[d]
         if d + 1 < len(small_peers):
-            small_copy(d + 1).start()
-        else:
-            small_ref[...] = acc[d + 1]
-
-    seg_rows = [jnp.sum(sums[i], axis=0, keepdims=True) for i in range(8)]
+            small_copy(late, d + 1).start()
+        elif late:
+            small_ref[0:8, :] = acc[d + 1, 0:8, :] + own[d + 1]
+            small_ref[8:32, :] = acc[d + 1, 8:32, :]
+
+    seg_rows = [jnp.sum(sums[i], axis=0, keepdims=True) for i in range(6)]
     seg_up = jnp.sum(bsums[...], axis=0, keepdims=True)
     order = (6, 7, 5, 4, 2, 1)
     for i, row in enumerate(order):
-        acc[0, i : i + 1, :] = seg_rows[row]
+        if row < 6:
+            acc[0, i : i + 1, :] = seg_rows[row]
         acc[0, 6 + i : 7 + i, :] = csums[row : row + 1, :] * share
     for i, row in enumerate((3, 0)):
         acc[0, 12 + i : 13 + i, :] = seg_rows[row]
@@ -737,7 +852,9 @@
     for i in range(4):
         acc[0, 16 + i : 17 + i, :] = seg_up[:, i * width : (i + 1) * width]
         acc[0, 20 + i : 21 + i, :] = cbsums[:, i * width : (i + 1) * width] * share
+    acc[0, 0:2, :] = jnp.zeros_like(acc[0, 0:2, :])
     acc[0, 24:32, :] = gpos[...] * share
+    late_acc[0] = jnp.zeros_like(late_acc[0])
 
     def cross_unit(n, parts):
         if n >= RING:
@@ -755,7 +872,6 @@
             if rel == 1:
                 if n == 0:
                     pl.semaphore_wait(barrier, 6)
-                    small_copy(0).start()
                 core_copy(n).start()
 
     def plain(ref):
@@ -766,133 +882,211 @@
 
     def cut(ref, j):
         return ref[:, j * width : (j + 1) * width]
+
+    def cut_group(ref, j):
+        return jnp.concatenate([ref[:, part * width + j * GROUP : part * width + (j + 1) * GROUP] for part in range(3)], axis=1)
 
     cross_parts = (
         lambda: [(plain(cfirstt), cut(cginner, j)) for j in range(4)],
         lambda: [(nested(chiddent, j), cgsecond[...]) for j in range(4)],
-        lambda: [(plain(cmixedt), cgbranch[...])] + [(plain(cxt), cut(cgqkv, j)) for j in range(3)],
+        lambda: [(plain(cmixedt), cgbranch[...])] + [(plain(cxt), cut_group(cgqkv, j)) for j in range(GROUPS)],
     )
 
     def compute(u):
         n = u + CROSS_UNITS - jnp.maximum(CROSS_UNITS - 1 - u, 0)
         t = n % 2
-        for i in range(CROSS_UNITS):
-            @pl.when(u == i)
-            def _(i=i):
-                cross_unit(2 * i, cross_parts[i]())
-                if i > 0:
-                    step_one(2 * i - 1, 1)
-
-        load(u, "wait")
-
-        @pl.when(u + 1 < SEG_UNITS)
-        def _():
-            load(u + 1, "start")
-
         @pl.when(n >= RING)
         def _():
             core_copy(n).wait_send()
 
-        right = bslot[u % 2]
+        right = bslot[b_slot(u)]
         for rel in (1, 0):
             core = c if rel == 0 else 1 - c
-            left = aslot[u % 2, :, core].reshape(8 * PART, -1)
+            left = aslot[a_slot(u), :, core].reshape(8 * PART, -1)
             value = mm(left, right).astype(BF16)
             for far in range(2):
                 for part in range(4):
                     block = value[(far * 4 + part) * PART : (far * 4 + part + 1) * PART]
-                    at = choose(t, far * 4 + (part % 2) * 2 + part // 2, (part // 2) * 4 + far * 2 + part % 2)
-                    if rel == 1:
-                        csend[n % RING, at] = block
-                    else:
-                        keep[n, at] = block
+                    ways = far * 4 + (part % 2) * 2 + part // 2, (part // 2) * 4 + far * 2 + part % 2
+                    for side, way_of in ((0, t), (1, t + (1 - t) * (n // (UNITS - 1)))):
+                        at = choose(way_of, *ways)
+                        cols = slice(side * width // 2, (side + 1) * width // 2)
+                        if rel == 1:
+                            csend[n % RING, at, :, cols] = block[:, cols]
+                        else:
+                            keep[n, at, :, cols] = block[:, cols]
             if rel == 1:
                 core_copy(n).start()
-        step_one(n - 1, (n - 1) % 2)
-
-    def step(u, carry):
-        @pl.when(u < SEG_UNITS)
-        def _():
-            compute(u)
-
-        @pl.when(u == SEG_UNITS)
-        def _():
-            step_one(UNITS - 1, (UNITS - 1) % 2)
-
-        for d in range(len(small_peers)):
-            @pl.when(u == 2 * d + 1)
-            def _(d=d):
-                small_step(d)
-
-        def on_pair(p, even, odd, cross):
-            @pl.when((p >= 0) & (p < CROSS_UNITS))
-            def _():
-                cross(2 * p)
-
-            @pl.when((p >= CROSS_UNITS) & (p < PAIRS))
-            def _():
-                even(2 * p)
-
-            @pl.when((p >= 0) & (p < PAIRS - 1))
-            def _():
-                odd(2 * p + 1)
-
-        @pl.when(u % 2 == 1)
-        def _():
-            p = u // 2 - 1
-            on_pair(
-                p - 3,
-                lambda n: step_out(n, 0, 2 * (p - 3) - CROSS_UNITS),
-                lambda n: step_out(n, 1, p - 3 + jnp.maximum(p - 3 - CROSS_UNITS + 1, 0)),
-                lambda n: None,
-            )
-            on_pair(p - 2, lambda n: step_final(n, 0), lambda n: step_final(n, 1), lambda n: cross_step_out(n, p - 2))
-            on_pair(p - 1, lambda n: step_three(n, 0), lambda n: step_three(n, 1), lambda n: cross_step_final(n))
-            on_pair(p, lambda n: step_two(n, 0), lambda n: step_two(n, 1), lambda n: step_two(n, 0))
-            q = p + AHEAD // 2
-
-            @pl.when((q >= AHEAD // 2) & (q < PAIRS))
-            def _():
-                copy_one(2 * q, 0).start()
-
-            @pl.when((q >= AHEAD // 2) & (q < PAIRS - 1))
-            def _():
-                copy_one(2 * q + 1, 1).start()
+
+        @pl.when(n < CROSS_UNITS + EARLY)
+        def _():
+            step_one(n - 1, (n - 1) % 2)
+
+    def attention_tile(j, i):
+        slot = i % 2
+        out_rows = pl.ds(pl.multiple_of(j * GROUP, GROUP), GROUP)
+        g_mixed = mm_nt(gbranch_slot[slot], wout[out_rows, :]).astype(BF16)
+        for seg in range(segs):
+            at = slice(seg * SEGLEN, (seg + 1) * SEGLEN)
+            to = pl.ds(pl.multiple_of(i * tile + seg * SEGLEN, SEGLEN), SEGLEN)
+            for half in range(2):
+                lanes = pair_lanes(half)
+                q = qkv_slot[slot, at, lanes[0]] * HDIM**-0.5
+                k = qkv_slot[slot, at, lanes[1]]
+                v = qkv_slot[slot, at, lanes[2]]
+                p_low = probs_slot[slot, seg, half]
+                p = p_low.astype(F32)
+                g_out = stack_heads(g_mixed[at, lanes[0]])
+                g_p = mm_nt(v, g_out)
+                g_s = (p * (g_p - jnp.sum(g_p * p, axis=0, keepdims=True))).astype(BF16)
+                g_v = mm(p_low, g_out).astype(BF16)
+                g_k = mm(g_s, stack_heads(q)).astype(BF16)
+                g_st = jnp.concatenate([g_s[:, :SEGLEN].T, g_s[:, SEGLEN:].T], axis=1)
+                g_q = (mm(g_st, stack_heads(k)) * HDIM**-0.5).astype(BF16)
+                bslot[j, to, lanes[0]] = g_q
+                bslot[j, to, lanes[1]] = g_k
+                bslot[j, to, lanes[2]] = g_v
+                fold[0, j, :, lanes[0]] += fold_rows(g_q.astype(F32))
+                fold[1, j, :, lanes[0]] += fold_rows(g_v.astype(F32))
+
+    def last_tile(i):
+        slot = i % 2
+
+        @pl.when(i >= 2)
+        def _():
+            store_gx(i - 2).wait()
+
+        total = gbranch_slot[slot].astype(F32)
+        for j in range(GROUPS):
+            total = total + mm_nt(bslot[j, tile_rows(i), :], wqkv[j])
+        gx_slot[slot] = total.astype(BF16)
+        store_gx(i).start()
+
+    def run(action, n):
+        if action in ("small", "late"):
+            late = int(action == "late")
+            if late and n == 0:
+                for row in range(2):
+                    for j in range(GROUPS):
+                        late_acc[0, row : row + 1, j * GROUP : (j + 1) * GROUP] = jnp.sum(fold[row, j], axis=0, keepdims=True)
+            if n == 0:
+                small_copy(late, 0).start()
+            else:
+                small_step(late, n - 1)
+            return
+        t = n % 2
+        cross = t == 0 and n < 2 * CROSS_UNITS
+        if action == "one":
+            step_one(n, t)
+        elif action == "send":
+            copy_one(n, t).start()
+        elif action == "two":
+            step_two(n, t)
+        elif action == "three":
+            cross_step_final(n) if cross else step_three(n, t)
+        elif action == "final":
+            cross_step_out(n, n // 2) if cross else step_final(n, t)
+        elif not cross:
+            step_out(n, t, n // 2 if n < 2 * CROSS_UNITS else min(n, UNITS - 1) - CROSS_UNITS)
+
+    schedule = comm_schedule()
+
+    def step(s, carry):
+        for at in range(STEPS):
+            if schedule[at]:
+                @pl.when(s == at)
+                def _(at=at):
+                    for action, n in schedule[at]:
+                        run(action, n)
+
+        @pl.when(s == EARLY)
+        def _():
+            for copy in weight_copies:
+                copy.wait()
+
+        for i in range(1, CROSS_UNITS):
+            @pl.when(s == i)
+            def _(i=i):
+                cross_unit(2 * i, cross_parts[i]())
+                step_one(2 * i - 1, 1)
+
+        load(s, "wait")
+
+        @pl.when(s == 1)
+        def _():
+            for copy in weight_copies:
+                copy.start()
+
+        @pl.when(s + 1 < STEPS)
+        def _():
+            load(s + 1, "start")
+
+        group, part = place(s)
+        inside = (s >= EARLY) & (s < LAST_AT)
+        multiply = (s < EARLY) | (inside & (part == TILES))
+
+        @pl.when(multiply)
+        def _():
+            compute(jnp.where(s < EARLY, s, EARLY + group))
+
+        @pl.when(inside & (part < TILES))
+        def _():
+            attention_tile(group, part)
+
+        @pl.when(s >= LAST_AT)
+        def _():
+            last_tile(s - LAST_AT)
 
         return carry
 
-    lax.fori_loop(0, 2 * PAIRS + 8, step, 0)
+    fold[...] = jnp.zeros_like(fold)
+    cross_unit(0, cross_parts[0]())
+    lax.fori_loop(0, STEPS, step, 0)
+    for action, n in schedule[STEPS]:
+        run(action, n)
+    for i in range(TILES - 2, TILES):
+        store_gx(i).wait()
     for n in range(UNITS - RING, UNITS):
         core_copy(n).wait_send()
 
 
-def total_grads(big, cross, small, share):
-    firstt, ginner, hiddent, gsecond, mixedt, gbranch, xt, gqkv = big
+def late_backward(big, cross, small, attn, share):
+    firstt, ginner, hiddent, gsecond, mixedt, gbranch, xt = big
+    qkv, probs, w_qkv, w_out = attn
     cfirstt, cginner, chiddent, cgsecond, cmixedt, cgbranch, cxt, cgqkv = cross
     width, depth = firstt.shape
     inners = ginner.shape[1]
     rows = cfirstt.shape[1]
+    tile = depth // TILES
     assert width == 16 * PART and inners == 4 * width
 
     def blocks(a, n):
         return a.reshape((2, 2, 4) + ((n,) if n > 1 else ()) + (PART, a.shape[1]))
 
     operands = [
-        blocks(firstt, 1), ginner, blocks(hiddent, 4), gsecond, blocks(mixedt, 1), gbranch, blocks(xt, 1), gqkv,
+        blocks(firstt, 1), ginner, blocks(hiddent, 4), gsecond, blocks(mixedt, 1), gbranch, blocks(xt, 1), qkv, probs, w_qkv, w_out,
         blocks(cfirstt, 1), cginner, blocks(chiddent, 4), cgsecond, blocks(cmixedt, 1), cgbranch, blocks(cxt, 1), cgqkv, *small,
     ]
     vmem = pl.BlockSpec(memory_space=pltpu.VMEM)
     any_spec = pl.BlockSpec(memory_space=pl.ANY)
-    outs = [(PART, 3 * width), (PART, width), (PART, inners), (4 * PART, width), (32, width)]
+    outs = [((PART, 3 * width), F32), ((PART, width), F32), ((PART, inners), F32), ((4 * PART, width), F32), ((32, width), F32), ((depth, width), BF16)]
+    segs = tile // SEGLEN
     dma = pltpu.SemaphoreType.DMA
     return pl.pallas_call(
-        functools.partial(total_kernel, share=share),
-        in_specs=[any_spec] * 8 + [vmem] * (len(operands) - 8),
-        out_specs=[vmem] * len(outs),
-        out_shape=[jax.ShapeDtypeStruct(o, F32) for o in outs],
+        functools.partial(late_kernel, share=share),
+        in_specs=[any_spec] * 11 + [vmem] * (len(operands) - 11),
+        out_specs=[vmem] * 5 + [any_spec],
+        out_shape=[jax.ShapeDtypeStruct(*o) for o in outs],
         scratch_shapes=[
             pltpu.VMEM((2, 2, 2, 4, PART, depth), BF16),
-            pltpu.VMEM((2, depth, width), BF16),
+            pltpu.VMEM((GROUPS, depth, width), BF16),
+            pltpu.VMEM((2, tile, width), BF16),
+            pltpu.VMEM((2, segs, 2, SEGLEN, 2 * SEGLEN), BF16),
+            pltpu.VMEM((2, tile, width), BF16),
+            pltpu.VMEM((2, tile, width), BF16),
+            pltpu.VMEM((GROUPS, width, 3 * GROUP), BF16),
+            pltpu.VMEM(w_out.shape[1:], BF16),
+            pltpu.VMEM((2, GROUPS, 8, GROUP), F32),
             pltpu.VMEM((RING, 8, PART, width), BF16),
             pltpu.VMEM((RING, 8, PART, width), BF16),
             pltpu.VMEM((UNITS, 8, PART, width), BF16),
@@ -902,22 +1096,91 @@
             pltpu.VMEM((UNITS, 2, PART, width), BF16),
             pltpu.VMEM((6, 32, width), F32),
             pltpu.VMEM((5, 32, width), F32),
-            dma((2, 2)), dma((RING,)), dma((RING,)), dma((UNITS,)), dma((UNITS,)), dma((UNITS,)), dma((UNITS,)),
-            dma((UNITS,)), dma((UNITS,)), dma((UNITS,)), dma((UNITS, 2)), dma((5,)), dma((5,)),
+            pltpu.VMEM((6, 8, width), F32),
+            pltpu.VMEM((5, 8, width), F32),
+            dma((2,)), dma((2, 3)), dma((2,)), dma((1 + 3 * GROUPS,)), dma((RING,)), dma((RING,)), dma((CHAINS,)), dma((CHAINS,)), dma((CHAINS,)), dma((CHAINS,)),
+            dma((CHAINS,)), dma((CHAINS,)), dma((CHAINS,)), dma((CHAINS, 2)), dma((2, 5)), dma((2, 5)),
         ],
-        compiler_params=pltpu.CompilerParams(vmem_limit_bytes=60 * 2**20, collective_id=1, has_side_effects=True),
-        name="total_grads",
+        compiler_params=pltpu.CompilerParams(vmem_limit_bytes=63 * 2**20, collective_id=1, has_side_effects=True),
+        name="late_backward",
     )(*operands)
 
-def small_grads(sums, bsums, csums, cbsums, gpos, cross_share):
-    seg_rows = jnp.sum(sums, axis=1)
+def finish_kernel(gx_ref, a_ref, b_ref, c_ref, d_ref, gx_out, a_out, b_out, c_out, d_out):
+    gx_out[...] = gx_ref[...].astype(F32)
+
+    @pl.when(pl.program_id(0) == 0)
+    def _():
+        for src, dst in ((a_ref, a_out), (b_ref, b_out), (c_ref, c_out), (d_ref, d_out)):
+            dst[...] = src[...]
+
+
+def finish(gx, grads, tile=512):
+    total, width = gx.shape
+    rows = pl.BlockSpec((tile, width), lambda i: (i, 0))
+    held = [pl.BlockSpec(g.shape, lambda i: (0, 0)) for g in grads]
+    return pl.pallas_call(
+        finish_kernel,
+        grid=(total // tile,),
+        in_specs=[rows] + held,
+        out_specs=[rows] + held,
+        out_shape=[jax.ShapeDtypeStruct(gx.shape, F32)] + [jax.ShapeDtypeStruct(g.shape, F32) for g in grads],
+        name="finish",
+    )(gx, *grads)
+
+
+def small_grads(sums, bsums, csums, cbsums, gpos, bias_sums, cross_share):
+    seg_rows = jnp.concatenate([jnp.sum(sums, axis=1), bias_sums])
     cross_rows = csums * cross_share
-    seg_up = jnp.sum(bsums, axis=0)
     order = jnp.array([6, 7, 5, 4, 2, 1])
     biases = jnp.stack([seg_rows[order], cross_rows[order]])
     gains = jnp.stack([seg_rows[jnp.array([3, 0])], cross_rows[jnp.array([3, 0])]])
-    ups = jnp.stack([seg_up, cbsums[0] * cross_share])
+    ups = jnp.stack([jnp.sum(bsums, axis=0), cbsums[0] * cross_share])
     return biases.reshape(-1), gains.reshape(-1), ups.reshape(-1), (gpos * cross_share).reshape(-1)
+
+
+def attention_back(qkv, probs, gbranch, w_qkv, w_out):
+    total, width = gbranch.shape
+    heads = width // HDIM
+    segs = total // SEGLEN
+    scale = HDIM**-0.5
+
+    def split(a):
+        return a.reshape(segs, SEGLEN, heads, HDIM)
+
+    def merge(a):
+        return a.reshape(total, width)
+
+    q, k, v = (
+        split(qkv[:, :, part * GROUP : (part + 1) * GROUP].transpose(1, 0, 2).reshape(total, width)) for part in range(3)
+    )
+    p_low = probs.reshape(segs, heads // 2, SEGLEN, 2, SEGLEN).transpose(0, 1, 3, 2, 4).reshape(segs, heads, SEGLEN, SEGLEN)
+    g_out = split(mm_nt(gbranch, w_out).astype(BF16))
+    p = p_low.astype(F32)
+    g_p = jnp.einsum("sqhd,skhd->shkq", g_out, v, preferred_element_type=F32)
+    g_s = (p * (g_p - jnp.sum(g_p * p, axis=2, keepdims=True))).astype(BF16)
+    g_v = jnp.einsum("shkq,sqhd->skhd", p_low, g_out, preferred_element_type=F32)
+    g_k = jnp.einsum("shkq,sqhd->skhd", g_s, q, preferred_element_type=F32) * scale
+    g_q = jnp.einsum("shkq,skhd->sqhd", g_s, k, preferred_element_type=F32) * scale
+    g_qkv = jnp.concatenate([merge(g_q), merge(g_k), merge(g_v)], axis=1).astype(BF16)
+    return g_qkv, gbranch.astype(F32) + mm_nt(g_qkv, w_qkv)
+
+
+def generic_total(seg_pairs, cross_pairs, small, planes, own):
+    axes = ("row", "seg")
+    me = lax.axis_index("seg")
+    shards = [
+        lax.psum_scatter(part, axes, scatter_dimension=0, tiled=True) for part in small_grads(*small, 1.0 / planes)
+    ]
+
+    def mine(values, dim):
+        return lax.dynamic_slice_in_dim(values, me * own, own, dim)
+
+    big = []
+    for at in (6, 4, 0, 2):
+        cross = mm(mine(cross_pairs[at], 1), mine(cross_pairs[at + 1], 0))
+        both = jnp.concatenate([mm(seg_pairs[at], seg_pairs[at + 1]), cross], axis=0)
+        big.append(lax.psum_scatter(both, axes, scatter_dimension=0, tiled=True))
+    return big, shards
 
 
 def per_device(
@@ -929,7 +1192,6 @@
     segments = doc_ids.shape[1]
     total = row_count * local_length
     own = row_count * seg_here
-    me = lax.axis_index("seg")
 
     seg_place = jnp.arange(segments)
     same_doc = doc_ids[:, :, None] == doc_ids[:, None, :]
@@ -942,48 +1204,36 @@
     keys = by_device(doc_ids + segments * jnp.arange(row_count)[:, None])
 
     cot = cotangent.reshape(total, width)
-    cot_cls = cotangent.reshape(own, SEGLEN, width)[:, 0]
     qkv, probs, n1, r1, slope, n2, r2, y, cls, xt, mixedt, firstt, hiddent = forward_block(
-        tokens.reshape(total, width), w_qkv, w_out, w_up, w_down, biases[0], gains[0], b_up[0:1]
+        tokens.reshape(total, width), w_qkv, w_out, w_up, w_down, biases, gains, b_up
     )
     (ccls, gcls, csums, cbsums, gpos, cxt, cmixedt, cfirstt, chiddent, cgqkv, cgbranch, cginner, cgsecond) = cross_block(
-        cls, cot_cls, place, keys, pos_table, w_qkv, w_out, w_up, w_down, biases[1], gains[1], b_up[1:2], planes
+        cls, cot, place, keys, pos_table, w_qkv, w_out, w_up, w_down, biases, gains, b_up, planes
     )
-    output, gsecond, ginner, gbranch, gqkv, gx, sums, bsums = backward_block(
-        gcls, ccls, cot, y, n2, r2, slope, n1, r1, qkv, probs, w_qkv, w_out, w_up, w_down, gains[0]
+    output, gsecond, ginner, gbranch, sums, bsums = early_backward(
+        gcls, ccls, cot, y, n2, r2, slope, n1, r1, w_up, w_down, gains
     )
-    seg_pairs = (firstt, ginner, hiddent, gsecond, mixedt, gbranch, xt, gqkv)
     cross_pairs = (cfirstt, cginner, chiddent, cgsecond, cmixedt, cgbranch, cxt, cgqkv)
-    if (lines, planes) == (8, 4) and width == 16 * PART:
-        *big, small = total_grads(seg_pairs, cross_pairs, (sums, bsums, csums, cbsums, gpos), 1.0 / planes)
+    share = 1.0 / planes
+    if (lines, planes) == (8, 4) and total == 2048 and width == 16 * PART:
+        *grads, small, gx = late_backward(
+            (firstt, ginner, hiddent, gsecond, mixedt, gbranch, xt), cross_pairs, (sums, bsums, csums, cbsums, gpos), (qkv, probs, w_qkv, w_out), share
+        )
+        gx, *grads = finish(gx, grads)
         small = small.reshape(-1)
-        index = lax.axis_index("row") * planes + me
+        index = lax.axis_index("row") * planes + lax.axis_index("seg")
         shards, start = [], 0
         for size in (12 * width, 4 * width, 8 * width, segments * width):
             count = size // (lines * planes)
             shards.append(lax.dynamic_slice_in_dim(small, start + index * count, count, 0))
             start += size
     else:
-        big, shards = generic_total(seg_pairs, cross_pairs, (sums, bsums, csums, cbsums, gpos), planes, own)
-    return (output.reshape(tokens.shape), gx.reshape(tokens.shape), *big, *shards)
-
-
-def generic_total(seg_pairs, cross_pairs, small, planes, own):
-    axes = ("row", "seg")
-    me = lax.axis_index("seg")
-    shards = [
-        lax.psum_scatter(part, axes, scatter_dimension=0, tiled=True) for part in small_grads(*small, 1.0 / planes)
-    ]
-
-    def mine(values, dim):
-        return lax.dynamic_slice_in_dim(values, me * own, own, dim)
-
-    big = []
-    for at in (6, 4, 0, 2):
-        cross = mm(mine(cross_pairs[at], 1), mine(cross_pairs[at + 1], 0))
-        both = jnp.concatenate([mm(seg_pairs[at], seg_pairs[at + 1]), cross], axis=0)
-        big.append(lax.psum_scatter(both, axes, scatter_dimension=0, tiled=True))
-    return big, shards
+        gqkv, gx = attention_back(qkv, probs, gbranch, w_qkv[0], w_out[0])
+        bias_sums = jnp.stack([jnp.sum(gqkv[:, at : at + width].astype(F32), axis=0) for at in (0, 2 * width)])
+        grads, shards = generic_total(
+            (firstt, ginner, hiddent, gsecond, mixedt, gbranch, xt, gqkv), cross_pairs, (sums, bsums, csums, cbsums, gpos, bias_sums), planes, own
+        )
+    return (output.reshape(tokens.shape), gx.reshape(tokens.shape), *grads, *shards)
 
 
 def solution(mesh):

time: 286 us -> 264 us (0.923)
  local copies, waits for them, and re-layouts: 25.3 us -> 13.4 us
  Pallas kernels: 259 us -> 249 us
    pallas_call x2 -> x3, Pallas kernels: 174 us -> 158 us  [the longest x1 116 us: late_backward(): pl.pallas_call(functools.partial(late_kernel, share=share), in_specs=[any...]
    unnamed x38 -> x42, local copies, waits for them, and re-layouts: 16.8 us -> 10.9 us
    pallas_call x1, Pallas kernels: 21.3 us -> 26.4 us  [cross_block(): pl.pallas_call(functools.partial(cross_kernel, ff_chunk=ff_chunk, devices...]
    slice x3 -> x0, local copies, waits for them, and re-layouts: 3.19 us -> none  [the longest x1 1.4 us: per_device(): b_up[1:2]]
where the time goes in v3:
time: 264 us
  Pallas kernels  249 us (94%)
  local copies, waits for them, and re-layouts  13.4 us (5%)
    pallas_call x1, Pallas kernels, late_backward(): pl.pallas_call(functools.partial(late_kernel, share=share), in_specs=[any...  116 us
    pallas_call x1, Pallas kernels, forward_block(): pl.pallas_call(functools.partial(forward_kernel, ff_chunk=ff_chunk), grid...  65.5 us
    pallas_call x1, Pallas kernels, early_backward(): pl.pallas_call(functools.partial(early_kernel, ff_chunk=ff_chunk), grid=(...  35.3 us
    pallas_call x1, Pallas kernels, cross_block(): pl.pallas_call(functools.partial(cross_kernel, ff_chunk=ff_chunk, devices...  26.4 us
    unnamed x42, local copies, waits for them, and re-layouts  10.9 us
    pallas_call x1, Pallas kernels, finish(): pl.pallas_call(finish_kernel, grid=(total // tile,), in_specs=[rows] + he...  6.31 us

profile of v3, /device:TPU:0, one launch (start us, length us, event | category | flops | bytes accessed | tf_op | source)
XLA Modules:
  0.0 264.0 jit_solution(3891782690072911121)
XLA Ops:
  0.6 1.3 copy.37.bias_ref
  2.0 0.0 copy-start.19
  2.0 0.0 copy-start.3
  2.0 0.0 copy-start.9
  2.0 0.0 copy-start.10
  2.0 0.0 copy-start.16
  2.0 65.5 %segment_forward.1 = (bf16[3,2048,768]{2,1,0:T(8,128)(2,1)}, bf16[16,6,128,256]{3,2,1,0:T(8,128)(2,1)}, bf16[2048,768]{1,0:T(8,128)(2,1)}, f32[2048,128]{1,0:T(8...) custom-call(bf16[2048,768]{1,0:T(8,128)(2,1)} %bitcast.25, ...), custom_call_target="tpu_custom_call" | custom-call | tf_op jit(solution)/shard_map/segment_forward/pallas_call | solution.py:172
  67.5 0.0 copy-done.19
  67.5 0.1 copy.40
  67.6 0.1 copy.41
  67.7 0.1 reshape.109.keycol_ref
  67.8 0.1 tile.10
  67.9 0.1 tile.12.keyrow_ref
  68.0 0.3 select_reduce_fusion
  68.2 0.1 copy.38
  68.3 0.1 subtract_bitcast_fusion
  68.4 0.1 copy.39
  68.5 0.1 reshape.108.place_ref
  68.6 0.0 copy-done.3
  68.6 0.0 copy-done.9
  68.6 0.0 copy-done.10
  68.6 0.0 copy-done.16
  68.6 0.0 copy-start.11
  68.6 0.8 copy-done.11
  69.4 26.4 %cross_block.1 = (f32[16,768]{1,0:T(8,128)S(1)}, f32[16,768]{1,0:T(8,128)S(1)}, f32[8,768]{1,0:T(8,128)S(1)}, f32[1,3072]{1,0:T(1,128)S(1)}, f32[8,768]{1,0:T(8,...) custom-call(f32[16,768]{1,0:T(8,128)S(1)} %copy-done.11, ...), custom_call_target="tpu_custom_call" | custom-call | tf_op jit(solution)/shard_map/cross_block/pallas_call | solution.py:463
  95.8 0.0 copy-start
  95.8 0.9 copy-done
  96.7 0.0 copy-start.1
  96.7 0.7 copy-done.1
  97.4 0.0 copy-start.2
  97.4 0.7 copy-done.2
  98.1 0.0 copy-start.4
  98.1 0.7 copy-done.4
  98.8 0.0 copy-start.5
  98.8 0.7 copy-done.5
  99.5 0.0 copy-start.6
  99.5 0.7 copy-done.6
  100.2 0.0 copy-start.7
  100.2 0.6 copy-done.7
  100.8 0.0 copy-start.8
  100.8 0.6 copy-done.8
  101.4 0.0 copy-start.12
  101.4 0.6 copy-done.12
  102.1 0.0 copy-start.13
  102.1 0.6 copy-done.13
  102.7 0.0 copy-start.14
  102.7 0.6 copy-done.14
  103.3 0.0 copy-start.15
  103.3 0.6 copy-done.15
  103.9 0.0 copy-start.17
  103.9 0.6 copy-done.17
  104.5 35.3 %early_backward.1 = (bf16[2048,768]{1,0:T(8,128)(2,1)}, bf16[2048,768]{1,0:T(8,128)(2,1)}, bf16[2048,3072]{1,0:T(8,128)(2,1)}, bf16[2048,768]{1,0:T(8,128)(2,1)}...) custom-call(f32[16,768]{1,0:T(8,128)} %copy-done.13, f32[16,768]{1,0:T(8,128)} %copy-done.12, bf16[2048,768]{1,0:T(8,128)(2,1)} %bitcast.24, ...), custom_call_target="tpu_custom_call" | custom-call | tf_op jit(solution)/shard_map/early_backward/pallas_call | solution.py:274
  139.8 115.9 %late_backward.1 = (f32[48,2304]{1,0:T(8,128)}, f32[48,768]{1,0:T(8,128)}, f32[48,3072]{1,0:T(8,128)}, f32[192,768]{1,0:T(8,128)}, f32[32,768]{1,0:T(8,128)}, /*index=5*/bf16[2048,768]{1,0:T(8,128)(2,1)}) custom-call(bf16[2,2,4,48,2048]{4,3,2,1,0:T(8,128)(2,1)} %bitcast.28, bf16[2048,3072]{1,0:T(8,128)(2,1)} %get-tuple-element.64.ginner, ...), custom_call_target="tpu_custom_call" | custom-call | tf_op jit(solution)/shard_map/late_backward/pallas_call | solution.py:1075
  255.8 0.0 copy-start.18
  255.8 6.3 %finish.1 = (f32[2048,768]{1,0:T(8,128)}, f32[48,2304]{1,0:T(8,128)}, f32[48,768]{1,0:T(8,128)}, f32[48,3072]{1,0:T(8,128)}, f32[192,768]{1,0:T(8,128)}) custom-call(bf16[2048,768]{1,0:T(8,128)(2,1)} %get-tuple-element.85.gx_ref, f32[48,2304]{1,0:T(8,128)} %get-tuple-element.86.a_ref, f32[48,768]{1,0:T(8,128)} %get-tuple-element.87.b_ref, ...), custom_call_target="tpu_custom_call" | custom-call | tf_op jit(solution)/shard_map/finish/pallas_call | solution.py:1121
  262.1 0.0 copy-done.18
  262.1 0.6 fusion
  262.8 0.7 dynamic_slice.12
  263.4 0.6 dynamic_slice.13
  (5 shorter events, 0.0 us)
Async XLA Ops:
  2.0 65.5 %copy-start.19 = (s32[8,8]{1,0:T(8,128)S(1)}, s32[8,8]{1,0:T(8,128)}, u32[]{:S(2)}) copy-start(s32[8,8]{1,0:T(8,128)} %param.12) | copy-start | bytes 772
  2.0 66.6 %copy-start.3 = (bf16[2,6,768]{2,1,0:T(8,128)(2,1)S(1)}, bf16[2,6,768]{2,1,0:T(8,128)(2,1)}, u32[]{:S(2)}) copy-start(bf16[2,6,768]{2,1,0:T(8,128)(2,1)} %copy.37.bias_ref) | copy-start | bytes 55300
  2.0 66.6 %copy-start.9 = (bf16[2,2,768]{2,1,0:T(2,128)(2,1)S(1)}, bf16[2,2,768]{2,1,0:T(2,128)(2,1)}, u32[]{:S(2)}) copy-start(bf16[2,2,768]{2,1,0:T(2,128)(2,1)} %gain_ref.5) | copy-start | bytes 18436
  2.0 66.6 %copy-start.10 = (bf16[2,3072]{1,0:T(2,128)(2,1)S(1)}, bf16[2,3072]{1,0:T(2,128)(2,1)}, u32[]{:S(2)}) copy-start(bf16[2,3072]{1,0:T(2,128)(2,1)} %bup_ref.3) | copy-start | bytes 36868
  2.0 66.6 %copy-start.16 = (bf16[8,768]{1,0:T(8,128)(2,1)S(1)}, bf16[8,768]{1,0:T(8,128)(2,1)}, u32[]{:S(2)}) copy-start(bf16[8,768]{1,0:T(8,128)(2,1)} %table_ref.1) | copy-start | bytes 36868
  68.6 0.8 copy-start.11
  95.8 0.9 copy-start
  96.7 0.7 copy-start.1
  97.4 0.7 copy-start.2
  98.1 0.7 copy-start.4
  98.8 0.7 copy-start.5
  99.5 0.7 copy-start.6
  100.2 0.6 copy-start.7
  100.8 0.6 copy-start.8
  101.4 0.6 copy-start.12
  102.1 0.6 copy-start.13
  102.7 0.6 copy-start.14
  103.3 0.6 copy-start.15
  103.9 0.6 copy-start.17
  255.8 6.3 %copy-start.18 = (f32[32,768]{1,0:T(8,128)S(1)}, f32[32,768]{1,0:T(8,128)}, u32[]{:S(2)}) copy-start(f32[32,768]{1,0:T(8,128)} %get-tuple-element.95) | copy-start | bytes 294916

commit v4 on v3

--- a/solution.py
+++ b/solution.py
@@ -52,144 +52,14 @@
 
 
 def gelu_both(u):
+    u = u.astype(BF16)
     square = u * u
-    t = jnp.tanh(u * (GELU_A + GELU_B * square))
-    half = 0.5 * u
-    hidden = half + half * t
-    slope = 0.5 + 0.5 * t + half * (1.0 - t * t) * (GELU_A + (3.0 * GELU_B) * square)
+    bend = GELU_B * square
+    half = 0.5 * jnp.tanh(u * (GELU_A + bend))
+    gate = half + 0.5
+    hidden = u * gate
+    slope = gate + hidden * (0.5 - half) * (2.0 * GELU_A + 6.0 * bend)
     return hidden, slope
-
-
-def forward_kernel(
-    x_ref, wqkv_hbm, wout_hbm, wup_hbm, wdown_hbm, bias_ref, gain_ref, bup_ref,
-    qkv_ref, probs_ref, n1_ref, r1_ref, slope_ref, n2_ref, r2_ref, y_ref, cls_ref, xt_ref, mixedt_ref, firstt_ref, hiddent_ref,
-    wqkv, wout, wup, wdown, mixed_ref, sems, *, ff_chunk,
-):
-    step = pl.program_id(0)
-    copies = [
-        pltpu.make_async_copy(src.at[0], dst, sems.at[i])
-        for i, (src, dst) in enumerate(
-            ((wqkv_hbm, wqkv), (wout_hbm, wout), (wup_hbm, wup), (wdown_hbm, wdown))
-        )
-    ]
-
-    @pl.when(step == 0)
-    def _():
-        for copy in copies:
-            copy.start()
-        copies[0].wait()
-
-    rows, width = x_ref.shape
-    bias = bias_ref[0].astype(F32)
-    gain = gain_ref[0].astype(F32)
-    up_bias = bup_ref[0:1, :].astype(F32)
-    x = x_ref[...]
-    xt_ref[...] = x.T
-    for part in range(3):
-        cols = slice(part * width, (part + 1) * width)
-        out = mm(x, wqkv[:, cols])
-        if part == 0:
-            out = out + bias[0:1]
-        if part == 2:
-            out = out + bias[1:2]
-        out = out.astype(BF16)
-        for group in range(width // GROUP):
-            qkv_ref[group, :, part * GROUP : (part + 1) * GROUP] = out[:, group * GROUP : (group + 1) * GROUP]
-    for seg in range(rows // SEGLEN):
-        at = slice(seg * SEGLEN, (seg + 1) * SEGLEN)
-        for pair in range(width // LANES):
-            q, k, v = (qkv_ref[pair // 2, at, lanes] for lanes in pair_lanes(pair % 2))
-            scores = mm_nt(k, stack_heads(q * HDIM**-0.5))
-            e = jnp.exp(scores - jnp.max(scores, axis=0, keepdims=True))
-            p = (e * (1.0 / jnp.sum(e, axis=0, keepdims=True))).astype(BF16)
-            probs_ref[seg, pair] = p
-            pt = jnp.concatenate([p[:, :SEGLEN].T, p[:, SEGLEN:].T], axis=1)
-            mixed_ref[at, pair * LANES : (pair + 1) * LANES] = mm(pt, stack_heads(v)).astype(BF16)
-
-    @pl.when(step == 0)
-    def _():
-        for copy in copies[1:]:
-            copy.wait()
-
-    mixed = mixed_ref[...]
-    mixedt_ref[...] = mixed.T
-    resid = x.astype(F32) + mm(mixed, wout[...]) + bias[2:3]
-    n1, r1 = norm_stats(resid)
-    n1_ref[...] = n1.astype(BF16)
-    r1_ref[...] = jnp.broadcast_to(r1, r1_ref.shape)
-    first = (n1 * gain[0:1] + bias[3:4]).astype(BF16)
-    firstt_ref[...] = first.T
-    total = first.astype(F32) + bias[4:5]
-    inners = wup.shape[1]
-    for c in range(inners // ff_chunk):
-        cols = slice(c * ff_chunk, (c + 1) * ff_chunk)
-        inner = mm(first, wup[:, cols]) + up_bias[:, cols]
-        hidden, slope = gelu_both(inner)
-        hidden = hidden.astype(BF16)
-        hiddent_ref[cols, :] = hidden.T
-        slope_ref[:, cols] = slope.astype(BF16)
-        total = total + mm(hidden, wdown[cols, :])
-    n2, r2 = norm_stats(total)
-    n2_ref[...] = n2.astype(BF16)
-    r2_ref[...] = jnp.broadcast_to(r2, r2_ref.shape)
-    y = (n2 * gain[1:2] + bias[5:6]).astype(BF16)
-    y_ref[...] = y
-    for seg in range(rows // SEGLEN):
-        cls_ref[pl.ds(step * (rows // SEGLEN) + seg, 1), :] = y[seg * SEGLEN : seg * SEGLEN + 8].astype(F32)[0:1]
-
-
-def forward_block(x, w_qkv, w_out, w_up, w_down, bias, gain, bup, tile=256, ff_chunk=768):
-    total, width = x.shape
-    inners = w_up.shape[-1]
-    segs = tile // SEGLEN
-    pairs = width // LANES
-    any_spec = pl.BlockSpec(memory_space=pl.ANY)
-
-    def rows_of(cols):
-        return pl.BlockSpec((tile, cols), lambda i: (i, 0))
-
-    def whole(a):
-        return pl.BlockSpec(a.shape, lambda i: (0,) * a.ndim)
-
-    def cols_of(rows):
-        return pl.BlockSpec((rows, tile), lambda i: (0, i))
-
-    outs = [
-        ((width // GROUP, total, 3 * GROUP), BF16, pl.BlockSpec((width // GROUP, tile, 3 * GROUP), lambda i: (0, i, 0))),
-        ((total // SEGLEN, pairs, SEGLEN, 2 * SEGLEN), BF16, pl.BlockSpec((segs, pairs, SEGLEN, 2 * SEGLEN), lambda i: (i, 0, 0, 0))),
-        ((total, width), BF16, rows_of(width)),
-        ((total, LANES), F32, rows_of(LANES)),
-        ((total, inners), BF16, rows_of(inners)),
-        ((total, width), BF16, rows_of(width)),
-        ((total, LANES), F32, rows_of(LANES)),
-        ((total, width), BF16, rows_of(width)),
-        ((total // SEGLEN, width), F32, pl.BlockSpec((total // SEGLEN, width), lambda i: (0, 0))),
-        ((width, total), BF16, cols_of(width)),
-        ((width, total), BF16, cols_of(width)),
-        ((width, total), BF16, cols_of(width)),
-        ((inners, total), BF16, cols_of(inners)),
-    ]
-    return pl.pallas_call(
-        functools.partial(forward_kernel, ff_chunk=ff_chunk),
-        grid=(total // tile,),
-        in_specs=[rows_of(width), any_spec, any_spec, any_spec, any_spec, whole(bias), whole(gain), whole(bup)],
-        out_specs=[o[2] for o in outs],
-        out_shape=[jax.ShapeDtypeStruct(o[0], o[1]) for o in outs],
-        scratch_shapes=[
-            pltpu.VMEM(w_qkv.shape[1:], BF16),
-            pltpu.VMEM(w_out.shape[1:], BF16),
-            pltpu.VMEM(w_up.shape[1:], BF16),
-            pltpu.VMEM(w_down.shape[1:], BF16),
-            pltpu.VMEM((tile, width), BF16),
-            pltpu.SemaphoreType.DMA((4,)),
-        ],
-        compiler_params=pltpu.CompilerParams(vmem_limit_bytes=60 * 2**20),
-        name="segment_forward",
-    )(x, w_qkv, w_out, w_up, w_down, bias, gain, bup)
-
-def fold_rows(values):
-    rows, cols = values.shape
-    return jnp.sum(values.reshape(rows // 8, 8, cols), axis=0)
 
 
 def norm_back(grad, gain, normal, rstd):
@@ -199,90 +69,6 @@
     return (scaled - a - normal * b) * rstd
 
 
-def early_kernel(
-    gcls_ref, ccls_ref, cot_ref, y_ref, n2_ref, r2_ref, slope_ref, n1_ref, r1_ref, wup_hbm, wdown_hbm, gain_ref,
-    out_ref, gsecond_ref, ginner_ref, gbranch_ref, sums_ref, bsums_ref, wup, wdown, sems, *, ff_chunk,
-):
-    step = pl.program_id(0)
-    copies = [
-        pltpu.make_async_copy(src.at[0], dst, sems.at[i]) for i, (src, dst) in enumerate(((wdown_hbm, wdown), (wup_hbm, wup)))
-    ]
-
-    @pl.when(step == 0)
-    def _():
-        for copy in copies:
-            copy.start()
-        sums_ref[...] = jnp.zeros_like(sums_ref)
-        bsums_ref[...] = jnp.zeros_like(bsums_ref)
-        for copy in copies:
-            copy.wait()
-
-    rows, width = cot_ref.shape
-    segs = rows // SEGLEN
-    inners = wup.shape[1]
-    gain = gain_ref[0].astype(F32)
-    place = lax.broadcasted_iota(jnp.int32, (rows, width), 0)
-    gy = cot_ref[...].astype(F32)
-    y = y_ref[...].astype(F32)
-    for seg in range(segs):
-        at = pl.ds(step * segs + seg, 1)
-        gy = jnp.where(place == seg * SEGLEN, gcls_ref[at, :], gy)
-        y = jnp.where(place == seg * SEGLEN, ccls_ref[at, :], y)
-    out_ref[...] = y.astype(BF16)
-    n2 = n2_ref[...].astype(F32)
-    sums_ref[0] += fold_rows(gy * n2)
-    sums_ref[1] += fold_rows(gy)
-    g_two = norm_back(gy, gain[1:2], n2, r2_ref[:, 0:1])
-    g_second = g_two.astype(BF16)
-    gsecond_ref[...] = g_second
-    sums_ref[2] += fold_rows(g_second.astype(F32))
-    g_first = g_two
-    for c in range(inners // ff_chunk):
-        cols = slice(c * ff_chunk, (c + 1) * ff_chunk)
-        g_inner = mm_nt(g_second, wdown[cols, :]) * slope_ref[:, cols].astype(F32)
-        g_low = g_inner.astype(BF16)
-        ginner_ref[:, cols] = g_low
-        bsums_ref[:, cols] += fold_rows(g_low.astype(F32))
-        g_first = g_first + mm_nt(g_low, wup[:, cols])
-    n1 = n1_ref[...].astype(F32)
-    sums_ref[3] += fold_rows(g_first * n1)
-    sums_ref[4] += fold_rows(g_first)
-    g_branch = norm_back(g_first, gain[0:1], n1, r1_ref[:, 0:1]).astype(BF16)
-    gbranch_ref[...] = g_branch
-    sums_ref[5] += fold_rows(g_branch.astype(F32))
-
-
-def early_backward(gcls, ccls, cot, y, n2, r2, slope, n1, r1, w_up, w_down, gains, tile=256, ff_chunk=768):
-    total, width = cot.shape
-    inners = w_up.shape[-1]
-    any_spec = pl.BlockSpec(memory_space=pl.ANY)
-
-    def rows_of(cols):
-        return pl.BlockSpec((tile, cols), lambda i: (i, 0))
-
-    def whole(a):
-        return pl.BlockSpec(a.shape, lambda i: (0,) * len(a.shape))
-
-    outs = [
-        ((total, width), BF16, rows_of(width)),
-        ((total, width), BF16, rows_of(width)),
-        ((total, inners), BF16, rows_of(inners)),
-        ((total, width), BF16, rows_of(width)),
-        ((6, 8, width), F32, pl.BlockSpec((6, 8, width), lambda i: (0, 0, 0))),
-        ((8, inners), F32, pl.BlockSpec((8, inners), lambda i: (0, 0))),
-    ]
-    return pl.pallas_call(
-        functools.partial(early_kernel, ff_chunk=ff_chunk),
-        grid=(total // tile,),
-        in_specs=[whole(gcls), whole(ccls), rows_of(width), rows_of(width), rows_of(width), rows_of(LANES), rows_of(inners),
-                  rows_of(width), rows_of(LANES), any_spec, any_spec, whole(gains)],
-        out_specs=[o[2] for o in outs],
-        out_shape=[jax.ShapeDtypeStruct(o[0], o[1]) for o in outs],
-        scratch_shapes=[pltpu.VMEM(w_up.shape[1:], BF16), pltpu.VMEM(w_down.shape[1:], BF16), pltpu.SemaphoreType.DMA((2,))],
-        compiler_params=pltpu.CompilerParams(vmem_limit_bytes=60 * 2**20),
-        name="early_backward",
-    )(gcls, ccls, cot, y, n2, r2, slope, n1, r1, w_up, w_down, gains)
-
 OUTS = 13
 NEGATIVE = -1000000000.0
 MESH = pl.DeviceIdType.MESH
@@ -292,66 +78,22 @@
     return values.astype(F32).T.astype(BF16)
 
 
-def cross_kernel(
-    cls_ref, cot_hbm, place_ref, keycol_ref, keyrow_ref, table_ref, wqkv_hbm, wout_hbm, wup_hbm, wdown_hbm, bias_ref, gain_ref, bup_ref,
-    *refs, ff_chunk, devices,
-):
+def cross_part(me, place_ref, keycol_ref, keyrow_ref, table_ref, bias_ref, gain_ref, bup_ref, outs, writes, weights, copies, scratch, ff_chunk):
     (
         ccls_ref, gcls_ref, sums_ref, bsums_ref, gpos_ref, xt_ref, mixedt_ref, firstt_ref, hiddent_ref,
         gqkv_ref, gbranch_ref, ginner_ref, gsecond_ref,
-    ) = outs = refs[OUTS : 2 * OUTS]
-    homes = refs[:OUTS]
-    (
-        wqkv, wout, wup, wdown, cot_rows, cot_low, packed, gathered, qkv_ref, probs_ref, mixed_ref, slope_ref, whole_ref, sems, out_sems, cot_sems, send_sems, recv_sems,
-    ) = refs[2 * OUTS :]
-    writes = [pltpu.make_async_copy(src, dst, out_sems.at[i]) for i, (src, dst) in enumerate(zip(outs, homes))]
-    copies = [
-        pltpu.make_async_copy(src.at[1], dst, sems.at[i])
-        for i, (src, dst) in enumerate(
-            ((wqkv_hbm, wqkv), (wout_hbm, wout), (wup_hbm, wup), (wdown_hbm, wdown))
-        )
-    ]
-    own, width = cls_ref.shape
-    cot_copies = [
-        pltpu.make_async_copy(cot_hbm.at[pl.ds(i * SEGLEN, 16)], cot_rows.at[i], cot_sems.at[i]) for i in range(own)
-    ]
-    for copy in cot_copies + copies:
-        copy.start()
-    rows = own * devices
+    ) = outs
+    wqkv, wout, wup, wdown = weights
+    qkv_ref, probs_ref, mixed_ref, slope_ref, whole_ref = scratch
+    own, width = ccls_ref.shape
+    rows = whole_ref.shape[1]
     inners = wup.shape[1]
-    me = lax.axis_index("seg")
-    line = lax.axis_index("row")
-    barrier = pltpu.get_barrier_semaphore()
-    for hop in range(1, devices):
-        pl.semaphore_signal(barrier, inc=1, device_id=(line, lax.rem(me + hop, devices)), device_id_type=MESH)
-    packed[0:own, :] = cls_ref[...].astype(BF16)
-    for i, copy in enumerate(cot_copies):
-        copy.wait()
-        cot_low[i : i + 1, :] = cot_rows[i, 0:8, :].astype(F32)[0:1]
-    packed[own:, :] = cot_low[...].astype(BF16)
-    pl.semaphore_wait(barrier, devices - 1)
-    sends = []
-    for hop in range(1, devices):
-        send = pltpu.make_async_remote_copy(
-            src_ref=packed, dst_ref=gathered.at[hop], send_sem=send_sems.at[hop], recv_sem=recv_sems.at[hop],
-            device_id=(line, lax.rem(me + hop, devices)), device_id_type=MESH,
-        )
-        send.start()
-        sends.append(send)
     bias = bias_ref[1].astype(F32)
     gain = gain_ref[1].astype(F32)
     up_bias = bup_ref[1:2, :].astype(F32)
     onehot = (place_ref[...] == lax.broadcasted_iota(jnp.int32, (rows, table_ref.shape[0]), 1)).astype(F32)
     embed = mm(onehot.astype(BF16), table_ref[...])
     allowed = keycol_ref[...] == keyrow_ref[...]
-    gathered[0] = packed[...]
-    for send in sends:
-        send.wait()
-    for hop in range(devices):
-        at = pl.ds(pl.multiple_of(lax.rem(me - hop + devices, devices) * own, own), own)
-        block = gathered[hop].astype(F32)
-        whole_ref[0, at, :] = block[:own]
-        whole_ref[1, at, :] = block[own:]
     x = (whole_ref[0] + embed).astype(BF16)
     gy = whole_ref[1]
     xt_ref[...] = turned(x)
@@ -364,16 +106,21 @@
         if part == 2:
             out = out + bias[1:2]
         qkv_ref[:, cols] = out.astype(BF16)
-    for pair in range(width // LANES):
-        q, k, v = (qkv_ref[:, part * width + pair * LANES : part * width + (pair + 1) * LANES] for part in range(3))
-        scores = jnp.where(allowed, mm_nt(k, stack_heads(q * HDIM**-0.5)), NEGATIVE)
-        e = jnp.exp(scores - jnp.max(scores, axis=0, keepdims=True))
+    low = low_lanes((rows, LANES))
+    pairs = range(width // LANES)
+    lanes = [[slice(part * width + pair * LANES, part * width + (pair + 1) * LANES) for part in range(3)] for pair in pairs]
+    scores = [
+        jnp.where(allowed, mm_nt(qkv_ref[:, at[1]], stack_heads(qkv_ref[:, at[0]] * HDIM**-0.5)), NEGATIVE) for at in lanes
+    ]
+    pt = []
+    for pair in pairs:
+        e = jnp.exp(scores[pair] - jnp.max(scores[pair], axis=0, keepdims=True))
         p = e * (1.0 / jnp.sum(e, axis=0, keepdims=True))
         probs_ref[pair] = p
-        pt = p.T.astype(BF16)
-        low = low_lanes((rows, LANES))
-        mixed = jnp.where(low, mm(pt[:rows], v), mm(pt[rows:], v))
-        mixed_ref[:, pair * LANES : (pair + 1) * LANES] = mixed.astype(BF16)
+        pt.append(p.T.astype(BF16))
+    for pair, at in enumerate(lanes):
+        v = qkv_ref[:, at[2]]
+        mixed_ref[:, at[0]] = jnp.where(low, mm(pt[pair][:rows], v), mm(pt[pair][rows:], v)).astype(BF16)
     copies[1].wait()
     mixed = mixed_ref[...]
     mixedt_ref[...] = turned(mixed)
@@ -383,12 +130,13 @@
     copies[2].wait()
     copies[3].wait()
     total = first.astype(F32) + bias[4:5]
-    for c in range(inners // ff_chunk):
-        cols = slice(c * ff_chunk, (c + 1) * ff_chunk)
-        hidden, slope = gelu_both(mm(first, wup[:, cols]) + up_bias[:, cols])
+    chunks = [slice(c * ff_chunk, (c + 1) * ff_chunk) for c in range(inners // ff_chunk)]
+    inner = [mm(first, wup[:, cols]) for cols in chunks]
+    for c, cols in enumerate(chunks):
+        hidden, slope = gelu_both(inner[c] + up_bias[:, cols])
         hidden = hidden.astype(BF16)
         hiddent_ref[cols, :] = turned(hidden)
-        slope_ref[:, cols] = slope
+        slope_ref[:, cols] = slope.astype(F32)
         total = total + mm(hidden, wdown[cols, :])
     n2, r2 = norm_stats(total)
     mine = pl.ds(pl.multiple_of(me * own, own), own)
@@ -407,9 +155,9 @@
     gsecond_ref[...] = g_second
     sums_ref[2:3, :] = row_sum(g_second)
     g_first = g_two
-    for c in range(inners // ff_chunk):
-        cols = slice(c * ff_chunk, (c + 1) * ff_chunk)
-        g_inner = (mm_nt(g_second, wdown[cols, :]) * slope_ref[:, cols]).astype(BF16)
+    g_hidden = [mm_nt(g_second, wdown[cols, :]) for cols in chunks]
+    for c, cols in enumerate(chunks):
+        g_inner = (g_hidden[c] * slope_ref[:, cols]).astype(BF16)
         ginner_ref[:, cols] = g_inner
         bsums_ref[:, cols] = row_sum(g_inner)
         g_first = g_first + mm_nt(g_inner, wup[:, cols])
@@ -422,20 +170,20 @@
     for i in (10, 11, 12):
         writes[i].start()
     g_mixed = mm_nt(g_branch, wout[...]).astype(BF16)
-    for pair in range(width // LANES):
-        lanes = [slice(part * width + pair * LANES, part * width + (pair + 1) * LANES) for part in range(3)]
-        q, k, v = (qkv_ref[:, at] for at in lanes)
+    g_out = [stack_heads(g_mixed[:, at[0]]) for at in lanes]
+    g_p = [mm_nt(qkv_ref[:, at[2]], g_out[pair]) for pair, at in enumerate(lanes)]
+    g_s, g_st = [], []
+    for pair in pairs:
         p = probs_ref[pair]
-        g_out = stack_heads(g_mixed[:, lanes[0]])
-        g_p = mm_nt(v, g_out)
-        g_s = p * (g_p - jnp.sum(g_p * p, axis=0, keepdims=True))
-        g_st = g_s.T.astype(BF16)
-        g_s = g_s.astype(BF16)
-        low = low_lanes((rows, LANES))
-        g_q = jnp.where(low, mm(g_st[:rows], k), mm(g_st[rows:], k)) * HDIM**-0.5
-        gqkv_ref[:, lanes[0]] = g_q.astype(BF16)
-        gqkv_ref[:, lanes[1]] = mm(g_s, stack_heads(q * HDIM**-0.5)).astype(BF16)
-        gqkv_ref[:, lanes[2]] = mm(p.astype(BF16), g_out).astype(BF16)
+        g = p * (g_p[pair] - jnp.sum(g_p[pair] * p, axis=0, keepdims=True))
+        g_s.append(g.astype(BF16))
+        g_st.append(g.T.astype(BF16))
+    for pair, at in enumerate(lanes):
+        q, k, _ = (qkv_ref[:, part] for part in at)
+        g_q = jnp.where(low, mm(g_st[pair][:rows], k), mm(g_st[pair][rows:], k)) * HDIM**-0.5
+        gqkv_ref[:, at[0]] = g_q.astype(BF16)
+        gqkv_ref[:, at[1]] = mm(g_s[pair], stack_heads(q * HDIM**-0.5)).astype(BF16)
+        gqkv_ref[:, at[2]] = mm(probs_ref[pair].astype(BF16), g_out[pair]).astype(BF16)
     g_qkv = gqkv_ref[...]
     sums_ref[6:7, :] = row_sum(g_qkv[:, :width])
     sums_ref[7:8, :] = row_sum(g_qkv[:, 2 * width :])
@@ -449,46 +197,427 @@
         write.wait()
 
 
-def cross_block(cls, cot, place, keys, table, w_qkv, w_out, w_up, w_down, biases, gains, b_up, devices, ff_chunk=768):
-    own, width = cls.shape
+def forward_kernel(
+    x_ref, wqkv_hbm, wout_hbm, wup_hbm, wdown_hbm, cot_hbm, bias_ref, gain_ref, bup_ref, place_ref, keycol_ref, keyrow_ref, table_ref,
+    qkv_ref, probs_ref, n1_ref, r1_ref, slope_ref, n2_ref, r2_ref, y_ref, xt_ref, mixedt_ref, firstt_ref, hiddent_ref,
+    *refs, ff_chunk, devices,
+):
+    homes, outs, refs = refs[:OUTS], refs[OUTS : 2 * OUTS], refs[2 * OUTS :]
+    wqkv, wout, wup, wdown, mixed_ref, first_ref, sems, cls_ref, cot_rows, cot_low, packed, gathered = refs[:12]
+    cross_weights, cross_scratch = refs[12:16], refs[16:21]
+    cross_sems, out_sems, cot_sems, send_sems, recv_sems = refs[21:]
+    step = pl.program_id(0)
+    last = pl.num_programs(0) - 1
+    copies = [
+        pltpu.make_async_copy(src.at[0], dst, sems.at[i])
+        for i, (src, dst) in enumerate(
+            ((wqkv_hbm, wqkv), (wout_hbm, wout), (wup_hbm, wup), (wdown_hbm, wdown))
+        )
+    ]
+
+    own = cls_ref.shape[0]
+    line, me = lax.axis_index("row"), lax.axis_index("seg")
+    peers = [(line, lax.rem(me + hop, devices)) for hop in range(1, devices)]
+    cot_copies = [
+        pltpu.make_async_copy(cot_hbm.at[pl.ds(i * SEGLEN, 16)], cot_rows.at[i], cot_sems.at[i]) for i in range(own)
+    ]
+    cross_copies = [
+        pltpu.make_async_copy(src.at[1], dst, cross_sems.at[i])
+        for i, (src, dst) in enumerate(zip((wqkv_hbm, wout_hbm, wup_hbm, wdown_hbm), cross_weights))
+    ]
+    writes = [pltpu.make_async_copy(src, dst, out_sems.at[i]) for i, (src, dst) in enumerate(zip(outs, homes))]
+    barrier = pltpu.get_barrier_semaphore()
+
+    def sends(kind):
+        return [
+            pltpu.make_async_remote_copy(
+                src_ref=packed.at[kind], dst_ref=gathered.at[kind, hop + 1], send_sem=send_sems.at[kind, hop],
+                recv_sem=recv_sems.at[kind, hop], device_id=peer, device_id_type=MESH,
+            )
+            for hop, peer in enumerate(peers)
+        ]
+
+    def arrived(kind, whole_ref):
+        for send in sends(kind):
+            send.wait()
+        gathered[kind, 0] = packed[kind]
+        for hop in range(devices):
+            rows_at = pl.ds(pl.multiple_of(lax.rem(me - hop + devices, devices) * own, own), own)
+            whole_ref[1 - kind, rows_at, :] = gathered[kind, hop].astype(F32)
+
+    @pl.when(step == 0)
+    def _():
+        for peer in peers:
+            pl.semaphore_signal(barrier, inc=1, device_id=peer, device_id_type=MESH)
+        for copy in copies:
+            copy.start()
+        copies[0].wait()
+        copies[1].wait()
+
+    @pl.when(step == 1)
+    def _():
+        copies[2].wait()
+        copies[3].wait()
+        for copy in cot_copies + cross_copies:
+            copy.start()
+
+    @pl.when(step == 2)
+    def _():
+        for i, copy in enumerate(cot_copies):
+            copy.wait()
+            cot_low[i : i + 1, :] = cot_rows[i, 0:8, :].astype(F32)[0:1]
+        packed[0] = cot_low[...].astype(BF16)
+        pl.semaphore_wait(barrier, devices - 1)
+        for send in sends(0):
+            send.start()
+
+    rows, width = x_ref.shape
+    bias = bias_ref[0].astype(F32)
+    gain = gain_ref[0].astype(F32)
+    up_bias = bup_ref[0:1, :].astype(F32)
+    inners = wup.shape[1]
+    chunks = [slice(c * ff_chunk, (c + 1) * ff_chunk) for c in range(inners // ff_chunk)]
+    items = [(seg, pair) for seg in range(rows // SEGLEN) for pair in range(width // LANES)]
+    every = range(len(items))
+    at = [slice(seg * SEGLEN, (seg + 1) * SEGLEN) for seg, _ in items]
+
+    def front(state):
+        def project_part(part):
+            x = x_ref[...]
+            out = mm(x, wqkv[:, part * width : (part + 1) * width])
+            if part == 0:
+                out = out + bias[0:1]
+            if part == 2:
+                out = out + bias[1:2]
+            out = out.astype(BF16)
+            for group in range(width // GROUP):
+                qkv_ref[group, :, part * GROUP : (part + 1) * GROUP] = out[:, group * GROUP : (group + 1) * GROUP]
+
+        def piece(e, part):
+            pair = items[e][1]
+            return qkv_ref[pair // 2, at[e], pair_lanes(pair % 2)[part]]
+
+        def scores():
+            xt_ref[...] = x_ref[...].T
+            state["scores"] = [mm_nt(piece(e, 1), stack_heads(piece(e, 0) * HDIM**-0.5)) for e in every]
+
+        def softmax(part):
+            for e in every[part :: 2]:
+                score = state["scores"][e]
+                ex = jnp.exp(score - jnp.max(score, axis=0, keepdims=True))
+                p = (ex * (1.0 / jnp.sum(ex, axis=0, keepdims=True))).astype(BF16)
+                probs_ref[items[e][0], items[e][1]] = p
+                state[e] = jnp.concatenate([p[:, :SEGLEN].T, p[:, SEGLEN:].T], axis=1)
+
+        def mix():
+            for e, (_, pair) in enumerate(items):
+                mixed_ref[at[e], pair * LANES : (pair + 1) * LANES] = mm(state[e], stack_heads(piece(e, 2))).astype(BF16)
+
+        def project_out():
+            mixed = mixed_ref[...]
+            mixedt_ref[...] = mixed.T
+            state["resid"] = x_ref[...].astype(F32) + mm(mixed, wout[...]) + bias[2:3]
+
+        def norm():
+            n1, r1 = norm_stats(state["resid"])
+            n1_ref[...] = n1.astype(BF16)
+            r1_ref[...] = jnp.broadcast_to(r1, r1_ref.shape)
+            first = (n1 * gain[0:1] + bias[3:4]).astype(BF16)
+            firstt_ref[...] = first.T
+            state["first"] = first
+
+        return [lambda part=part: project_part(part) for part in range(3)] + [scores, lambda: softmax(0), lambda: softmax(1), mix, project_out, norm]
+
+    def back(state):
+        first = first_ref[...]
+        state["total"] = first.astype(F32) + bias[4:5]
+
+        def up(c):
+            state["inner", c] = mm(first, wup[:, chunks[c]])
+
+        def gelu(c):
+            cols = chunks[c]
+            hidden, slope = gelu_both(state["inner", c] + up_bias[:, cols])
+            hidden = hidden.astype(BF16)
+            hiddent_ref[cols, :] = hidden.T
+            slope_ref[:, cols] = slope.astype(BF16)
+            state["hidden", c] = hidden
+
+        def down(c):
+            state["total"] = state["total"] + mm(state["hidden", c], wdown[chunks[c], :])
+
+        def norm():
+            n2, r2 = norm_stats(state["total"])
+            n2_ref[...] = n2.astype(BF16)
+            r2_ref[...] = jnp.broadcast_to(r2, r2_ref.shape)
+            y = (n2 * gain[1:2] + bias[5:6]).astype(BF16)
+            y_ref[...] = y
+            segs = rows // SEGLEN
+            for seg in range(segs):
+                cls_ref[pl.ds((step - 1) * segs + seg, 1), :] = y[seg * SEGLEN : seg * SEGLEN + 8].astype(F32)[0:1]
+
+        pieces = [lambda: up(0)]
+        for c in range(len(chunks)):
+            if c + 1 < len(chunks):
+                pieces.append(lambda c=c: up(c + 1))
+            pieces += [lambda c=c: gelu(c), lambda c=c: down(c)]
+        return pieces + [norm]
+
+    def run(with_front, with_back):
+        state = {}
+        lists = ([back(state)] if with_back else []) + ([front(state)] if with_front else [])
+        turns = sorted((((i + 0.5) / len(pieces), k, i) for k, pieces in enumerate(lists) for i in range(len(pieces))))
+        for _, k, i in turns:
+            lists[k][i]()
+        if with_front:
+            first_ref[...] = state["first"]
+
+    @pl.when(step == 0)
+    def _():
+        run(True, False)
+
+    @pl.when((step > 0) & (step < last))
+    def _():
+        run(True, True)
+
+    @pl.when(step == last)
+    def _():
+        run(False, True)
+        packed[1] = cls_ref[...].astype(BF16)
+        for send in sends(1):
+            send.start()
+        arrived(0, cross_scratch[-1])
+        arrived(1, cross_scratch[-1])
+        cross_part(
+            me, place_ref, keycol_ref, keyrow_ref, table_ref, bias_ref, gain_ref, bup_ref, outs, writes,
+            cross_weights, cross_copies, cross_scratch, ff_chunk,
+        )
+
+
+def forward_blocks(x, cot, w_qkv, w_out, w_up, w_down, bias, gain, bup, place, keys, table, devices, tile=256, ff_chunk=768):
+    total, width = x.shape
+    inners = w_up.shape[-1]
+    segs = tile // SEGLEN
+    pairs = width // LANES
+    any_spec = pl.BlockSpec(memory_space=pl.ANY)
+
+    steps = total // tile
+
+    def rows_of(cols, late):
+        return pl.BlockSpec((tile, cols), lambda i: (jnp.maximum(i - 1, 0) if late else jnp.minimum(i, steps - 1), 0))
+
+    def whole(a):
+        return pl.BlockSpec(a.shape, lambda i: (0,) * a.ndim)
+
+    def cols_of(rows, late):
+        return pl.BlockSpec((rows, tile), lambda i: (0, jnp.maximum(i - 1, 0) if late else jnp.minimum(i, steps - 1)))
+
+    outs = [
+        ((width // GROUP, total, 3 * GROUP), BF16, pl.BlockSpec((width // GROUP, tile, 3 * GROUP), lambda i: (0, jnp.minimum(i, steps - 1), 0))),
+        ((total // SEGLEN, pairs, SEGLEN, 2 * SEGLEN), BF16, pl.BlockSpec((segs, pairs, SEGLEN, 2 * SEGLEN), lambda i: (jnp.minimum(i, steps - 1), 0, 0, 0))),
+        ((total, width), BF16, rows_of(width, False)),
+        ((total, LANES), F32, rows_of(LANES, False)),
+        ((total, inners), BF16, rows_of(inners, True)),
+        ((total, width), BF16, rows_of(width, True)),
+        ((total, LANES), F32, rows_of(LANES, True)),
+        ((total, width), BF16, rows_of(width, True)),
+        ((width, total), BF16, cols_of(width, False)),
+        ((width, total), BF16, cols_of(width, False)),
+        ((width, total), BF16, cols_of(width, False)),
+        ((inners, total), BF16, cols_of(inners, True)),
+    ]
+    own = total // SEGLEN
     rows = own * devices
-    inners = w_up.shape[-1]
-    vmem = pl.BlockSpec(memory_space=pltpu.VMEM)
-    any_spec = pl.BlockSpec(memory_space=pl.ANY)
-    outs = [
+    cross_outs = [
         ((own, width), F32), ((own, width), F32), ((8, width), F32), ((1, inners), F32), (table.shape, F32),
         ((width, rows), BF16), ((width, rows), BF16), ((width, rows), BF16), ((inners, rows), BF16),
         ((rows, 3 * width), BF16), ((rows, width), BF16), ((rows, inners), BF16), ((rows, width), BF16),
     ]
+    keyrow = jnp.tile(keys.reshape(1, rows), (1, 2))
+    dma = pltpu.SemaphoreType.DMA
     return pl.pallas_call(
-        functools.partial(cross_kernel, ff_chunk=ff_chunk, devices=devices),
-        in_specs=[vmem, any_spec] + [vmem] * 4 + [any_spec] * 4 + [vmem] * 3,
-        out_specs=[any_spec] * len(outs),
-        out_shape=[jax.ShapeDtypeStruct(*o) for o in outs],
-        scratch_shapes=[pltpu.VMEM(*o) for o in outs]
+        functools.partial(forward_kernel, ff_chunk=ff_chunk, devices=devices),
+        grid=(steps + 1,),
+        in_specs=[rows_of(width, False), any_spec, any_spec, any_spec, any_spec, any_spec]
+        + [whole(a) for a in (bias, gain, bup, place, keys, keyrow, table)],
+        out_specs=[o[2] for o in outs] + [pl.BlockSpec(memory_space=pltpu.HBM)] * OUTS,
+        out_shape=[jax.ShapeDtypeStruct(o[0], o[1]) for o in outs + cross_outs],
+        scratch_shapes=[pltpu.VMEM(*o) for o in cross_outs]
         + [
             pltpu.VMEM(w_qkv.shape[1:], BF16),
             pltpu.VMEM(w_out.shape[1:], BF16),
             pltpu.VMEM(w_up.shape[1:], BF16),
             pltpu.VMEM(w_down.shape[1:], BF16),
+            pltpu.VMEM((tile, width), BF16),
+            pltpu.VMEM((tile, width), BF16),
+            dma((4,)),
+            pltpu.VMEM((own, width), F32),
             pltpu.VMEM((own, 16, width), BF16),
             pltpu.VMEM((own, width), F32),
-            pltpu.VMEM((2 * own, width), BF16),
-            pltpu.VMEM((devices, 2 * own, width), BF16),
+            pltpu.VMEM((2, own, width), BF16),
+            pltpu.VMEM((2, devices, own, width), BF16),
+            pltpu.VMEM(w_qkv.shape[1:], BF16),
+            pltpu.VMEM(w_out.shape[1:], BF16),
+            pltpu.VMEM(w_up.shape[1:], BF16),
+            pltpu.VMEM(w_down.shape[1:], BF16),
             pltpu.VMEM((rows, 3 * width), BF16),
-            pltpu.VMEM((width // LANES, rows, 2 * rows), F32),
+            pltpu.VMEM((pairs, rows, 2 * rows), F32),
             pltpu.VMEM((rows, width), BF16),
             pltpu.VMEM((rows, inners), F32),
             pltpu.VMEM((2, rows, width), F32),
-            pltpu.SemaphoreType.DMA((4,)),
-            pltpu.SemaphoreType.DMA((OUTS,)),
-            pltpu.SemaphoreType.DMA((own,)),
-            pltpu.SemaphoreType.DMA((devices,)),
-            pltpu.SemaphoreType.DMA((devices,)),
+            dma((4,)), dma((OUTS,)), dma((own,)), dma((2, devices - 1)), dma((2, devices - 1)),
         ],
-        compiler_params=pltpu.CompilerParams(vmem_limit_bytes=50 * 2**20, collective_id=0, has_side_effects=True),
-        name="cross_block",
-    )(cls, cot, place, keys, jnp.tile(keys.reshape(1, rows), (1, 2)), table, w_qkv, w_out, w_up, w_down, biases, gains, b_up)
+        compiler_params=pltpu.CompilerParams(vmem_limit_bytes=63 * 2**20, collective_id=0, has_side_effects=True),
+        name="forward_blocks",
+    )(x, w_qkv, w_out, w_up, w_down, cot, bias, gain, bup, place, keys, keyrow, table)
+
+def fold_rows(values):
+    rows, cols = values.shape
+    return jnp.sum(values.reshape(rows // 8, 8, cols), axis=0)
+
+
+def early_kernel(
+    gcls_ref, ccls_ref, cot_ref, y_ref, n2_ref, r2_ref, slope_ref, n1_ref, r1_ref, wup_hbm, wdown_hbm, gain_ref,
+    out_ref, gsecond_ref, ginner_ref, gbranch_ref, sums_ref, bsums_ref, wup, wdown, two_ref, sems, *, ff_chunk,
+):
+    step = pl.program_id(0)
+    last = pl.num_programs(0) - 1
+    copies = [
+        pltpu.make_async_copy(src.at[0], dst, sems.at[i]) for i, (src, dst) in enumerate(((wdown_hbm, wdown), (wup_hbm, wup)))
+    ]
+
+    @pl.when(step == 0)
+    def _():
+        for copy in copies:
+            copy.start()
+        sums_ref[...] = jnp.zeros_like(sums_ref)
+        bsums_ref[...] = jnp.zeros_like(bsums_ref)
+
+    @pl.when(step == 1)
+    def _():
+        for copy in copies:
+            copy.wait()
+
+    rows, width = cot_ref.shape
+    segs = rows // SEGLEN
+    inners = wup.shape[1]
+    gain = gain_ref[0].astype(F32)
+    chunks = [slice(c * ff_chunk, (c + 1) * ff_chunk) for c in range(inners // ff_chunk)]
+
+    def front(state):
+        def gradient():
+            place = lax.broadcasted_iota(jnp.int32, (rows, width), 0)
+            gy = cot_ref[...].astype(F32)
+            y = y_ref[...].astype(F32)
+            for seg in range(segs):
+                at = pl.ds(step * segs + seg, 1)
+                gy = jnp.where(place == seg * SEGLEN, gcls_ref[at, :], gy)
+                y = jnp.where(place == seg * SEGLEN, ccls_ref[at, :], y)
+            out_ref[...] = y.astype(BF16)
+            state["gy"] = gy
+
+        def norm():
+            gy = state["gy"]
+            n2 = n2_ref[...].astype(F32)
+            sums_ref[0] += fold_rows(gy * n2)
+            sums_ref[1] += fold_rows(gy)
+            state["two"] = norm_back(gy, gain[1:2], n2, r2_ref[:, 0:1])
+
+        def store():
+            low = state["two"].astype(BF16)
+            gsecond_ref[...] = low
+            sums_ref[2] += fold_rows(low.astype(F32))
+
+        return [gradient, norm, store]
+
+    def back(state):
+        g_two = two_ref[...]
+        g_second = g_two.astype(BF16)
+        state["first"] = g_two
+
+        def down(c):
+            state["hidden", c] = mm_nt(g_second, wdown[chunks[c], :])
+
+        def slope(c):
+            cols = chunks[c]
+            g_low = state["hidden", c].astype(BF16) * slope_ref[:, cols]
+            ginner_ref[:, cols] = g_low
+            bsums_ref[:, cols] += fold_rows(g_low.astype(F32))
+            state["inner", c] = g_low
+
+        def up(c):
+            state["first"] = state["first"] + mm_nt(state["inner", c], wup[:, chunks[c]])
+
+        def norm():
+            g_first = state["first"]
+            n1 = n1_ref[...].astype(F32)
+            sums_ref[3] += fold_rows(g_first * n1)
+            sums_ref[4] += fold_rows(g_first)
+            g_branch = norm_back(g_first, gain[0:1], n1, r1_ref[:, 0:1]).astype(BF16)
+            gbranch_ref[...] = g_branch
+            sums_ref[5] += fold_rows(g_branch.astype(F32))
+
+        pieces = [lambda: down(0)]
+        for c in range(len(chunks)):
+            if c + 1 < len(chunks):
+                pieces.append(lambda c=c: down(c + 1))
+            pieces += [lambda c=c: slope(c), lambda c=c: up(c)]
+        return pieces + [norm]
+
+    def run(with_front, with_back):
+        state = {}
+        lists = ([back(state)] if with_back else []) + ([front(state)] if with_front else [])
+        turns = sorted((((i + 0.5) / len(pieces), k, i) for k, pieces in enumerate(lists) for i in range(len(pieces))))
+        for _, k, i in turns:
+            lists[k][i]()
+        if with_front:
+            two_ref[...] = state["two"]
+
+    @pl.when(step == 0)
+    def _():
+        run(True, False)
+
+    @pl.when((step > 0) & (step < last))
+    def _():
+        run(True, True)
+
+    @pl.when(step == last)
+    def _():
+        run(False, True)
+
+
+def early_backward(gcls, ccls, cot, y, n2, r2, slope, n1, r1, w_up, w_down, gains, tile=256, ff_chunk=768):
+    total, width = cot.shape
+    inners = w_up.shape[-1]
+    any_spec = pl.BlockSpec(memory_space=pl.ANY)
+
+    steps = total // tile
+
+    def rows_of(cols, late=False):
+        return pl.BlockSpec((tile, cols), lambda i: (jnp.maximum(i - 1, 0) if late else jnp.minimum(i, steps - 1), 0))
+
+    def whole(a):
+        return pl.BlockSpec(a.shape, lambda i: (0,) * len(a.shape))
+
+    outs = [
+        ((total, width), BF16, rows_of(width)),
+        ((total, width), BF16, rows_of(width)),
+        ((total, inners), BF16, rows_of(inners, True)),
+        ((total, width), BF16, rows_of(width, True)),
+        ((6, 8, width), F32, pl.BlockSpec((6, 8, width), lambda i: (0, 0, 0))),
+        ((8, inners), F32, pl.BlockSpec((8, inners), lambda i: (0, 0))),
+    ]
+    return pl.pallas_call(
+        functools.partial(early_kernel, ff_chunk=ff_chunk),
+        grid=(steps + 1,),
+        in_specs=[whole(gcls), whole(ccls), rows_of(width), rows_of(width), rows_of(width), rows_of(LANES), rows_of(inners, True),
+                  rows_of(width, True), rows_of(LANES, True), any_spec, any_spec, whole(gains)],
+        out_specs=[o[2] for o in outs],
+        out_shape=[jax.ShapeDtypeStruct(o[0], o[1]) for o in outs],
+        scratch_shapes=[pltpu.VMEM(w_up.shape[1:], BF16), pltpu.VMEM(w_down.shape[1:], BF16), pltpu.VMEM((tile, width), F32), pltpu.SemaphoreType.DMA((2,))],
+        compiler_params=pltpu.CompilerParams(vmem_limit_bytes=60 * 2**20),
+        name="early_backward",
+    )(gcls, ccls, cot, y, n2, r2, slope, n1, r1, w_up, w_down, gains)
 
 RING = 4
 CROSS_UNITS = 3
@@ -926,28 +1055,27 @@
         slot = i % 2
         out_rows = pl.ds(pl.multiple_of(j * GROUP, GROUP), GROUP)
         g_mixed = mm_nt(gbranch_slot[slot], wout[out_rows, :]).astype(BF16)
-        for seg in range(segs):
-            at = slice(seg * SEGLEN, (seg + 1) * SEGLEN)
-            to = pl.ds(pl.multiple_of(i * tile + seg * SEGLEN, SEGLEN), SEGLEN)
-            for half in range(2):
-                lanes = pair_lanes(half)
-                q = qkv_slot[slot, at, lanes[0]] * HDIM**-0.5
-                k = qkv_slot[slot, at, lanes[1]]
-                v = qkv_slot[slot, at, lanes[2]]
-                p_low = probs_slot[slot, seg, half]
-                p = p_low.astype(F32)
-                g_out = stack_heads(g_mixed[at, lanes[0]])
-                g_p = mm_nt(v, g_out)
-                g_s = (p * (g_p - jnp.sum(g_p * p, axis=0, keepdims=True))).astype(BF16)
-                g_v = mm(p_low, g_out).astype(BF16)
-                g_k = mm(g_s, stack_heads(q)).astype(BF16)
-                g_st = jnp.concatenate([g_s[:, :SEGLEN].T, g_s[:, SEGLEN:].T], axis=1)
-                g_q = (mm(g_st, stack_heads(k)) * HDIM**-0.5).astype(BF16)
-                bslot[j, to, lanes[0]] = g_q
-                bslot[j, to, lanes[1]] = g_k
-                bslot[j, to, lanes[2]] = g_v
-                fold[0, j, :, lanes[0]] += fold_rows(g_q.astype(F32))
-                fold[1, j, :, lanes[0]] += fold_rows(g_v.astype(F32))
+        items = [(seg, half) for seg in range(segs) for half in range(2)]
+        at = [slice(seg * SEGLEN, (seg + 1) * SEGLEN) for seg, _ in items]
+        lanes = [pair_lanes(half) for _, half in items]
+        to = [pl.ds(pl.multiple_of(i * tile + seg * SEGLEN, SEGLEN), SEGLEN) for seg, _ in items]
+        every = range(len(items))
+        g_out = [stack_heads(g_mixed[at[e], lanes[e][0]]) for e in every]
+        g_p = [mm_nt(qkv_slot[slot, at[e], lanes[e][2]], g_out[e]) for e in every]
+        g_v = [mm(probs_slot[slot, seg, half], g_out[e]) for e, (seg, half) in enumerate(items)]
+        g_s = []
+        for e, (seg, half) in enumerate(items):
+            p = probs_slot[slot, seg, half].astype(F32)
+            g_s.append((p * (g_p[e] - jnp.sum(g_p[e] * p, axis=0, keepdims=True))).astype(BF16))
+        g_k = [mm(g_s[e], stack_heads(qkv_slot[slot, at[e], lanes[e][0]] * HDIM**-0.5)) for e in every]
+        g_st = [jnp.concatenate([g_s[e][:, :SEGLEN].T, g_s[e][:, SEGLEN:].T], axis=1) for e in every]
+        g_q = [mm(g_st[e], stack_heads(qkv_slot[slot, at[e], lanes[e][1]])) * HDIM**-0.5 for e in every]
+        for e in every:
+            for part, value in enumerate((g_q[e], g_k[e], g_v[e])):
+                value = value.astype(BF16)
+                bslot[j, to[e], lanes[e][part]] = value
+                if part != 1:
+                    fold[part // 2, j, :, lanes[e][0]] += fold_rows(value.astype(F32))
 
     def last_tile(i):
         slot = i % 2
@@ -1204,11 +1332,12 @@
     keys = by_device(doc_ids + segments * jnp.arange(row_count)[:, None])
 
     cot = cotangent.reshape(total, width)
-    qkv, probs, n1, r1, slope, n2, r2, y, cls, xt, mixedt, firstt, hiddent = forward_block(
-        tokens.reshape(total, width), w_qkv, w_out, w_up, w_down, biases, gains, b_up
-    )
-    (ccls, gcls, csums, cbsums, gpos, cxt, cmixedt, cfirstt, chiddent, cgqkv, cgbranch, cginner, cgsecond) = cross_block(
-        cls, cot, place, keys, pos_table, w_qkv, w_out, w_up, w_down, biases, gains, b_up, planes
+    (
+        qkv, probs, n1, r1, slope, n2, r2, y, xt, mixedt, firstt, hiddent,
+        ccls, gcls, csums, cbsums, gpos, cxt, cmixedt, cfirstt, chiddent, cgqkv, cgbranch, cginner, cgsecond,
+    ) = forward_blocks(
+        tokens.reshape(total, width), cot, w_qkv, w_out, w_up, w_down, biases, gains, b_up, place, keys, pos_table, planes,
+        tile=256 if planes <= 4 else 128,
     )
     output, gsecond, ginner, gbranch, sums, bsums = early_backward(
         gcls, ccls, cot, y, n2, r2, slope, n1, r1, w_up, w_down, gains

time: 264 us -> 231 us (0.88)
  Pallas kernels: 249 us -> 223 us
  local copies, waits for them, and re-layouts: 13.4 us -> 6.33 us
    pallas_call x2 -> x1, Pallas kernels: 91.8 us -> 69.3 us  [forward_blocks(): pl.pallas_call(functools.partial(forward_kernel, ff_chunk=ff_chunk, devic...]
    unnamed x42 -> x4, local copies, waits for them, and re-layouts: 10.9 us -> 2.1 us
    pallas_call x1, Pallas kernels: 116 us -> 112 us  [late_backward(): pl.pallas_call(functools.partial(late_kernel, share=share), in_specs=[any...]
where the time goes in v4:
time: 231 us
  Pallas kernels  223 us (97%)
  local copies, waits for them, and re-layouts  6.33 us (3%)
    pallas_call x1, Pallas kernels, late_backward(): pl.pallas_call(functools.partial(late_kernel, share=share), in_specs=[any...  112 us
    pallas_call x1, Pallas kernels, forward_blocks(): pl.pallas_call(functools.partial(forward_kernel, ff_chunk=ff_chunk, devic...  69.3 us
    pallas_call x1, Pallas kernels, early_backward(): pl.pallas_call(functools.partial(early_kernel, ff_chunk=ff_chunk), grid=(...  34.9 us
    pallas_call x1, Pallas kernels, finish(): pl.pallas_call(finish_kernel, grid=(total // tile,), in_specs=[rows] + he...  6.31 us

profile of v4, /device:TPU:0, one launch (start us, length us, event | category | flops | bytes accessed | tf_op | source)
XLA Modules:
  0.0 230.9 jit_solution(11836157955497374804)
XLA Ops:
  0.6 0.8 copy.37
  1.4 0.1 copy.38
  1.5 0.7 reshape.109.keycol_ref
  2.2 0.1 tile.10
  2.3 0.6 tile.12.keyrow_ref
  2.9 1.0 select_reduce_fusion
  4.0 0.1 copy.35
  4.0 0.1 subtract_bitcast_fusion
  4.1 0.1 copy.36
  4.2 0.7 reshape.108.place_ref
  4.9 1.3 copy.40.bias_ref
  6.2 69.3 %forward_blocks.1 = (bf16[3,2048,768]{2,1,0:T(8,128)(2,1)}, bf16[16,6,128,256]{3,2,1,0:T(8,128)(2,1)}, bf16[2048,768]{1,0:T(8,128)(2,1)}, f32[2048,128]{1,0:T(8,...) custom-call(bf16[2048,768]{1,0:T(8,128)(2,1)} %bitcast.21, ...), custom_call_target="tpu_custom_call" | custom-call | tf_op jit(solution)/shard_map/forward_blocks/pallas_call | solution.py:438
  75.5 34.9 %early_backward.1 = (bf16[2048,768]{1,0:T(8,128)(2,1)}, bf16[2048,768]{1,0:T(8,128)(2,1)}, bf16[2048,3072]{1,0:T(8,128)(2,1)}, bf16[2048,768]{1,0:T(8,128)(2,1)}...) custom-call(f32[16,768]{1,0:T(8,128)} %get-tuple-element.52.gcls_ref, f32[16,768]{1,0:T(8,128)} %get-tuple-element.53.ccls_ref, ...), custom_call_target="tpu_custom_call" | custom-call | tf_op jit(solution)/shard_map/early_backward/pallas_call | solution.py:610
  110.4 112.2 %late_backward.1 = (f32[48,2304]{1,0:T(8,128)}, f32[48,768]{1,0:T(8,128)}, f32[48,3072]{1,0:T(8,128)}, f32[192,768]{1,0:T(8,128)}, f32[32,768]{1,0:T(8,128)}, /*index=5*/bf16[2048,768]{1,0:T(8,128)(2,1)}) custom-call(bf16[2,2,4,48,2048]{4,3,2,1,0:T(8,128)(2,1)} %bitcast.24, bf16[2048,3072]{1,0:T(8,128)(2,1)} %get-tuple-element.62.ginner, ...), custom_call_target="tpu_custom_call" | custom-call | tf_op jit(solution)/shard_map/late_backward/pallas_call | solution.py:1203
  222.7 0.0 copy-start
  222.7 6.3 %finish.1 = (f32[2048,768]{1,0:T(8,128)}, f32[48,2304]{1,0:T(8,128)}, f32[48,768]{1,0:T(8,128)}, f32[48,3072]{1,0:T(8,128)}, f32[192,768]{1,0:T(8,128)}) custom-call(bf16[2048,768]{1,0:T(8,128)(2,1)} %get-tuple-element.83.gx_ref, f32[48,2304]{1,0:T(8,128)} %get-tuple-element.84.a_ref, f32[48,768]{1,0:T(8,128)} %get-tuple-element.85.b_ref, ...), custom_call_target="tpu_custom_call" | custom-call | tf_op jit(solution)/shard_map/finish/pallas_call | solution.py:1249
  229.0 0.0 copy-done
  229.0 0.6 fusion
  229.7 0.7 dynamic_slice.12
  230.3 0.6 dynamic_slice.13
  (5 shorter events, 0.0 us)
Async XLA Ops:
  222.7 6.3 %copy-start = (f32[32,768]{1,0:T(8,128)S(1)}, f32[32,768]{1,0:T(8,128)}, u32[]{:S(2)}) copy-start(f32[32,768]{1,0:T(8,128)} %get-tuple-element.93) | copy-start | bytes 294916
